TPU v7x, 32 devices: a whole 2x2x4 slice. The times are simulated.
32 devices in a mesh: group: 2 (over y), expert: 4 (over z), context: 2 (over x), tensor: 2 (over core).
Axes of the slice: x: 2, y: 2, z: 4, core: 2. Of those that a mesh axis runs over, the one named last changes fastest.
Arguments:
- tokens: bfloat16 [2048, 4096], P(('group', 'expert', 'context', 'tensor')), parts along dimension 0, may hold values from -6 to 6
- expert_ids: int32 [2048, 1], P(('group', 'expert', 'context', 'tensor')), parts along dimension 0, may hold values from 0 to 15; in each aligned block of 64 rows (0 to 63, 64 to 127, ...) at most 5 rows name the same one
- route_weights: float32 [2048, 1], P(('group', 'expert', 'context', 'tensor')), parts along dimension 0, may hold values from 0.05 to 1
- gate_weight: bfloat16 [16, 4096, 1536], P('expert', None, ('context', 'tensor')), may hold values from -0.09375 to 0.09375
- up_weight: bfloat16 [16, 4096, 1536], P('expert', None, ('context', 'tensor')), may hold values from -0.09375 to 0.09375
- down_weight: bfloat16 [16, 1536, 4096], P('expert', None, ('context', 'tensor')), may hold values from -0.15625 to 0.15625
Outputs:
- combined: bfloat16 [2048, 4096], P(('group', 'expert', 'context', 'tensor')), parts along dimension 0
There are 2 independent parts, one for each index of `group`. A program takes and returns all parts, laid end to end along the dimension named above; an argument that names none is the same for every part. Nothing has to cross between parts.
Inputs may be any that keep to these rules, and one draw needn't show every extreme that they name: `expert_ids`: each row names 1 different experts. Within the rows of one device (aligned blocks of 64 rows) no expert is named by more than 5 rows, and in every draw some expert is named by exactly 5 rows of some block.
All inputs are finite; a program needn't handle non-finite values.
Results may differ from a plain program's by a relative error of at most 0.0057.
Values may be sent and summed in bfloat16 or wider, within the bound.
No kernel may reach another device: no remote copies, remote signals or barrier semaphores. Data moves between devices by JAX's collectives and lax.ppermute only.
A program may use at most 128 MiB of HBM per device.

v0:
```python
import jax
import jax.numpy as jnp
from jax import lax
from jax.sharding import PartitionSpec as P


def on_device(tokens, expert_ids, route_weights, gate_weight, up_weight, down_weight):
    token_count = tokens.shape[0]
    width = tokens.shape[1]
    chosen_count = expert_ids.shape[1]
    local_experts = gate_weight.shape[0]
    groups = lax.axis_size("expert")
    expert_count = local_experts * groups
    capacity = max(2, token_count * chosen_count * 5 // (4 * expert_count))
    expert_table = jnp.arange(expert_count, dtype=jnp.int32)
    chosen = expert_ids[:, :, None] == expert_table[None, None, :]
    member = jnp.sum(chosen.astype(jnp.int32), axis=1)
    slot_rank = jnp.cumsum(member, axis=0) - 1
    slot_table = jnp.arange(capacity, dtype=jnp.int32)
    placed = (member[:, :, None] > 0) & (slot_rank[:, :, None] == slot_table[None, None, :])
    placed_grid = placed.reshape(token_count, groups, local_experts, capacity).transpose(0, 2, 1, 3)
    placed_flat = placed_grid.reshape(token_count, local_experts * groups * capacity)
    selector = placed_flat.astype(jnp.bfloat16)
    outgoing = jnp.dot(selector.T, tokens, preferred_element_type=jnp.float32).astype(jnp.bfloat16)
    outgoing = outgoing.reshape(local_experts, groups, capacity, width)
    incoming = lax.all_to_all(outgoing, "expert", split_axis=1, concat_axis=1, tiled=True)
    incoming = incoming.reshape(local_experts, groups * capacity, width)
    row_block = lax.all_gather(incoming, ("context", "tensor"), axis=1, tiled=True)
    gate_act = jnp.einsum(
        "end,edf->enf", row_block, gate_weight, preferred_element_type=jnp.float32
    )
    up_act = jnp.einsum("end,edf->enf", row_block, up_weight, preferred_element_type=jnp.float32)
    hidden_local = (jax.nn.silu(gate_act) * up_act).astype(jnp.bfloat16)
    expert_out = jnp.einsum(
        "erf,efd->erd",
        lax.all_gather(hidden_local, ("context", "tensor"), axis=2, tiled=True),
        down_weight,
        preferred_element_type=jnp.float32,
    ).astype(jnp.bfloat16)
    gathered_back = lax.all_to_all(
        expert_out, ("context", "tensor"), split_axis=1, concat_axis=2, tiled=True
    )
    gathered_back = gathered_back.reshape(local_experts, groups, capacity, width)
    returned = lax.all_to_all(gathered_back, "expert", split_axis=1, concat_axis=1, tiled=True)
    returned = returned.reshape(local_experts * groups * capacity, width)
    ranks = jnp.take_along_axis(slot_rank, expert_ids, axis=1)
    owner_group = expert_ids // local_experts
    local_slot = expert_ids % local_experts
    flat_index = (local_slot * groups + owner_group) * capacity + ranks
    picked = jnp.take(returned, flat_index.reshape(-1), axis=0).reshape(
        token_count, chosen_count, width
    )
    combined = jnp.sum(route_weights[:, :, None] * picked.astype(jnp.float32), axis=1)
    return combined.astype(jnp.bfloat16)


def solution(mesh):
    return jax.shard_map(
        on_device,
        mesh=mesh,
        in_specs=(
            P(("group", "expert", "context", "tensor"), None),
            P(("group", "expert", "context", "tensor"), None),
            P(("group", "expert", "context", "tensor"), None),
            P("expert", None, ("context", "tensor")),
            P("expert", None, ("context", "tensor")),
            P("expert", None, ("context", "tensor")),
        ),
        out_specs=P(("group", "expert", "context", "tensor"), None),
        check_vma=False,
    )
```

profile of v0, /device:TPU:0, one launch (start us, length us, event | category | flops | bytes accessed | tf_op | source)
XLA Modules:
  0.0 132.8 jit_solution(10595658112060865692)
XLA Ops:
  6.5 0.8 fusion.12
  7.3 0.7 convert_compare_fusion
  8.1 0.1 eq.82
  8.2 0.1 reduce_window_sum.11
  8.4 0.4 convolution_convert_fusion
  8.8 0.3 reshape.113
  9.1 0.6 copy.17
  9.7 23.5 %all_to_all.25 = bf16[4,4,5,4096]{3,0,2,1:T(4,128)(2,1)} all-to-all(bf16[4,4,5,4096]{3,0,2,1:T(4,128)(2,1)S(1)} %copy.17), channel_id=1, replica_groups=mesh['group'=2,'expert'=4,'context'=2,'tensor'=2] {'expert'}, dimensions={1} | all-to-all | bytes 1310720 | tf_op jit(solution)/shard_map/all_to_all | solution.py:26
  33.2 24.8 %all-gather.2.cloned.1.call-done = bf16[4,80,4096]{2,0,1:T(4,128)(2,1)} async-done(((bf16[4,20,4096]{2,0,1:T(4,128)(2,1)}), bf16[4,80,4096]{2,0,1:T(4,128)(2,1)}) %all-gather.2.cloned.1.call-update) | async-done | bytes 2621456 | tf_op jit(solution)/shard_map/all_gather | solution.py:28
  58.0 9.7 %fusion.2 = f32[4,80,384]{2,1,0:T(8,128)S(1)} fusion(bf16[4,4096,384]{2,1,0:T(8,128)(2,1)} %param.9, bf16[4,80,4096]{2,0,1:T(4,128)(2,1)} %all-gather.2.cloned.1.call-done), kind=kOutput, calls=%fused_computation.5 | convolution fusion | flops 1006632960 | bytes 15695872 | tf_op jit(solution)/shard_map/end,edf->enf/dot_general | solution.py:29
  67.7 6.9 %fusion.7 = bf16[4,80,384]{2,1,0:T(8,128)(2,1)S(1)} fusion(bf16[4,4096,384]{2,1,0:T(8,128)(2,1)S(1)} %copy-done.1, bf16[4,80,4096]{2,0,1:T(4,128)(2,1)} %all-gather.2.cloned.1.call-done, f32[4,80,384]{2,1,0:T(8,128)S(1)} %fusion.2), kind=kOutput, calls=%fused_computation.9 | convolution fusion | flops 1007370240 | bytes 15941632 | tf_op jit(solution)/shard_map/end,edf->enf/dot_general | solution.py:32
  74.7 9.9 %all_gather.7 = bf16[4,80,1536]{2,1,0:T(8,128)(2,1)S(1)} all-gather(bf16[4,80,384]{2,1,0:T(8,128)(2,1)S(1)} %fusion.7), channel_id=1, replica_groups=mesh['group'=2,'expert'=4,'context'=2,'tensor'=2] {'context','tensor'}, dimensions={2}, use_global_device_ids=true | all-gather | bytes 1228800 | tf_op jit(solution)/shard_map/all_gather | solution.py:36
  84.5 2.4 %convolution_convert_fusion.1 = bf16[4,80,1024]{2,1,0:T(8,128)(2,1)S(1)} fusion(bf16[4,80,1536]{2,1,0:T(8,128)(2,1)S(1)} %all_gather.7, bf16[4,1536,1024]{2,1,0:T(8,128)(2,1)S(1)} %copy-done.2), kind=kOutput, calls=%fused_computation.7 | convolution fusion | flops 1006960640 | bytes 14221312 | tf_op jit(solution)/shard_map/erf,efd->erd/dot_general | solution.py:34
  86.9 0.5 copy.20
  87.4 12.7 %all_to_all.26 = bf16[4,80,1024]{2,0,1:T(4,128)(2,1)S(1)} all-to-all(bf16[4,80,1024]{2,0,1:T(4,128)(2,1)S(1)} %copy.20), channel_id=1, replica_groups=mesh['group'=2,'expert'=4,'context'=2,'tensor'=2] {'context','tensor'}, dimensions={1} | all-to-all | bytes 1310720 | tf_op jit(solution)/shard_map/all_to_all | solution.py:40
  100.1 0.5 copy.21
  100.6 1.3 %reshape.115 = bf16[4,4,5,4096]{3,0,2,1:T(4,128)(2,1)} reshape(bf16[4,20,4,1024]{3,2,0,1:T(4,128)(2,1)S(1)} %copy.21) | data formatting | bytes 1310720 | tf_op jit(solution)/shard_map/reshape | solution.py:43
  101.9 4.6 %all-to-all-start.2 = ((bf16[4,4,5,4096]{3,0,2,1:T(4,128)(2,1)}), bf16[4,4,5,4096]{3,0,2,1:T(4,128)(2,1)S(1)}, u32[]{:S(2)}, u32[]{:S(2)}) async-start(bf16[4,4,5,4096]{3,0,2,1:T(4,128)(2,1)} %reshape.115), calls=%async_computation.2 | async-start | bytes 1310720 | tf_op jit(solution)/shard_map/all_to_all | solution.py:44
  106.6 0.8 gather_fusion.1
  107.4 16.0 %all-to-all-done.2 = bf16[4,4,5,4096]{3,0,2,1:T(4,128)(2,1)S(1)} async-done(((bf16[4,4,5,4096]{3,0,2,1:T(4,128)(2,1)}), bf16[4,4,5,4096]{3,0,2,1:T(4,128)(2,1)S(1)}, u32[]{:S(2)}, u32[]{:S(2)}) %all-to-all-start.2) | async-done | bytes 655392 | tf_op jit(solution)/shard_map/all_to_all | solution.py:44
  123.5 0.4 copy.22
  123.9 0.3 reshape.116
  124.1 0.9 gather_fusion
  125.0 1.0 multiply_convert_fusion
  (27 shorter events, 0.2 us)
Async XLA Ops:
  6.5 1.9 %copy-start = (bf16[64,4096]{1,0:T(8,128)(2,1)S(1)}, bf16[64,4096]{1,0:T(8,128)(2,1)}, u32[]{:S(2)}) copy-start(bf16[64,4096]{1,0:T(8,128)(2,1)} %param.6) | copy-start | bytes 1572868
  6.5 51.5 %all-gather.2.cloned.1.call-start = ((), (), s32[]{:S(2)}) async-start(), calls=%async_computation.3 | async-start | bytes 3276800 | tf_op jit(solution)/shard_map/all_gather | solution.py:28
  58.0 9.7 %copy-start.1 = (bf16[4,4096,384]{2,1,0:T(8,128)(2,1)S(1)}, bf16[4,4096,384]{2,1,0:T(8,128)(2,1)}, u32[]{:S(2)}) copy-start(bf16[4,4096,384]{2,1,0:T(8,128)(2,1)} %param.10) | copy-start | bytes 37748740
  58.0 26.5 %copy-start.2 = (bf16[4,1536,1024]{2,1,0:T(8,128)(2,1)S(1)}, bf16[4,1536,1024]{2,1,0:T(8,128)(2,1)}, u32[]{:S(2)}) copy-start(bf16[4,1536,1024]{2,1,0:T(8,128)(2,1)} %param.11) | copy-start | bytes 37748740
  74.6 31.9 %copy-start.3 = (s32[64,1]{0,1:T(1,128)S(1)}, s32[64,1]{0,1:T(1,128)}, u32[]{:S(2)}) copy-start(s32[64,1]{0,1:T(1,128)} %param.7) | copy-start | bytes 772
  84.5 40.5 %copy-start.4 = (f32[64,1]{0,1:T(1,128)S(1)}, f32[64,1]{0,1:T(1,128)}, u32[]{:S(2)}) copy-start(f32[64,1]{0,1:T(1,128)} %param.8) | copy-start | bytes 772
  101.9 21.5 %all-to-all-start.2 = ((bf16[4,4,5,4096]{3,0,2,1:T(4,128)(2,1)}), bf16[4,4,5,4096]{3,0,2,1:T(4,128)(2,1)S(1)}, u32[]{:S(2)}, u32[]{:S(2)}) async-start(bf16[4,4,5,4096]{3,0,2,1:T(4,128)(2,1)} %reshape.115), calls=%async_computation.2 | async-start | bytes 1310720 | tf_op jit(solution)/shard_map/all_to_all | solution.py:44
Sparse Core Ops, SparseCore 0:
  33.3 24.6 all-gather.1
where the time goes:
time: 133 us
  blocking collectives  46 us (35%)
  waiting for transfers between devices  40.9 us (31%)
  matrix products  19.4 us (15%)
  between operations  13.5 us (10%)
  local copies, waits for them, and re-layouts  5.76 us (4%)
  starting transfers between devices  4.59 us (3%)
  other arithmetic  2.65 us (2%)
    all_gather x1, waiting for transfers between devices, on_device(): lax.all_gather(incoming, ('context', 'tensor'), axis=1, tiled=True)  24.8 us
    all_to_all x1, blocking collectives, on_device(): lax.all_to_all(outgoing, 'expert', split_axis=1, concat_axis=1, tiled=True)  23.5 us
    all_to_all x1, waiting for transfers between devices, on_device(): lax.all_to_all(gathered_back, 'expert', split_axis=1, concat_axis=1, tile...  16 us
    all_to_all x1, blocking collectives, on_device(): lax.all_to_all(expert_out, ('context', 'tensor'), split_axis=1, concat_ax...  12.7 us
    all_gather x1, blocking collectives, on_device(): lax.all_gather(hidden_local, ('context', 'tensor'), axis=2, tiled=True)  9.86 us
    dot_general x1, matrix products, on_device(): jnp.einsum('end,edf->enf', row_block, gate_weight, preferred_element_type...  9.68 us
    dot_general x1, matrix products, on_device(): jnp.einsum('end,edf->enf', row_block, up_weight, preferred_element_type=j...  6.92 us
    all_to_all x1, starting transfers between devices, on_device(): lax.all_to_all(gathered_back, 'expert', split_axis=1, concat_axis=1, tile...  4.59 us
  transfers between devices with their start and end apart: 2, of which 2 were waited for; matrix products, arithmetic and copies ran while one was open for 1% of the time, Pallas kernels for 0%

commit v1 on v0

v1 whole, which is shorter than its diff:
```python
import functools
import jax
import jax.numpy as jnp
from jax import lax
from jax.experimental import pallas as pl
from jax.experimental.pallas import tpu as pltpu
from jax.sharding import PartitionSpec as P

BIG = 4096
PARTS = 2
VMEM_LIMIT = 48 * 1024 * 1024
F32, BF16, I32 = jnp.float32, jnp.bfloat16, jnp.int32


def div(x, by):
    return ((x.astype(F32) + 0.5) * (1.0 / by)).astype(I32)


def onehot(cond):
    return jnp.where(cond, 1.0, 0.0).astype(BF16)


def dot(a, b):
    return jnp.dot(a, b, preferred_element_type=F32)


def iota(shape, dim):
    return lax.broadcasted_iota(I32, shape, dim)


def as_column(row):
    n = row.shape[1]
    square = jnp.broadcast_to(row, (n, n))
    return jnp.sum(jnp.where(iota((n, n), 0) == iota((n, n), 1), square, jnp.zeros((), row.dtype)), axis=1, keepdims=True)


def slot_keys(ids_row, cap):
    n = ids_row.shape[1]
    ids_col = as_column(ids_row)
    earlier = (ids_col == ids_row) & (iota((n, n), 0) < iota((n, n), 1))
    rank = jnp.sum(jnp.where(earlier, 1, 0), axis=0, keepdims=True)
    return ids_row * cap + rank


def dispatch_kernel(cfg, pos_ref, ids_ref, tok_ref, *outs):
    z = pos_ref[0]
    n = tok_ref.shape[0]
    keys = slot_keys(ids_ref[...], cfg.cap)
    keys = jnp.concatenate([keys + j * BIG for j in range(cfg.nd)], axis=1)
    stacked = jnp.concatenate([tok_ref[:, j * cfg.w:(j + 1) * cfg.w] for j in range(cfg.nd)], axis=0)
    i = iota((cfg.rp, 1), 0)
    j = div(i, cfg.rows)
    target = i - j * cfg.rows + j * BIG
    for h in range(PARTS):
        for r in range(cfg.groups):
            base = (jnp.bitwise_xor(z, r) * cfg.local + h * cfg.ne) * cfg.cap
            outs[h * cfg.groups + r][...] = dot(onehot(keys - base == target), stacked).astype(BF16)


def hidden_kernel(cfg, h, pos_ref, *refs):
    srcs = refs[: cfg.sources]
    gate_hbm, up_hbm, out_ref, gate, up, rows, sems = refs[cfg.sources:]
    kb = cfg.kb
    depth = gate.shape[1] // kb
    copies = []
    for e in range(cfg.ne):
        for k in range(kb):
            part = pl.ds(k * depth, depth)
            pair = []
            for m, (src, dst) in enumerate(((gate_hbm, gate), (up_hbm, up))):
                cp = pltpu.make_async_copy(src.at[h * cfg.ne + e, part], dst.at[e, part], sems.at[(e * kb + k) * 2 + m])
                cp.start()
                pair.append(cp)
            copies.append(pair)
    je = cfg.nd * cfg.ne
    i, c = iota((je * 16, 1), 0), iota((1, 2 * cfg.rp), 1)
    slot = i & 7
    want = ((i >> 3) & 1) * cfg.rp + (i >> 4) * cfg.cap + slot
    spread = onehot((want == c) & (slot < cfg.cap))
    for k in range(cfg.sources // 2):
        pair = jnp.concatenate([srcs[2 * k][...], srcs[2 * k + 1][...]], axis=0)
        spaced = dot(spread, pair).astype(BF16)
        for j in range(cfg.nd):
            for e in range(cfg.ne):
                at = (j * cfg.ne + e) * 16
                rows[e, k * 16:(k + 1) * 16, j * cfg.w:(j + 1) * cfg.w] = spaced[at:at + 16]
    per = cfg.sources * cfg.cap
    i = iota((per, 1), 0)
    s = div(i, cfg.cap)
    slot = i - s * cfg.cap
    rel = jnp.bitwise_xor(s, pos_ref[1] * 2 + pos_ref[2])
    compact = onehot(iota((1, cfg.sources * 8), 1) == rel * 8 + slot)
    for e in range(cfg.ne):
        g = u = 0.0
        for k in range(kb):
            for cp in copies[e * kb + k]:
                cp.wait()
            x = rows[e, :, k * depth:(k + 1) * depth]
            g = g + dot(x, gate[e, k * depth:(k + 1) * depth])
            u = u + dot(x, up[e, k * depth:(k + 1) * depth])
        hid = (g / (1.0 + jnp.exp(-g)) * u).astype(BF16)
        out_ref[e * per:(e + 1) * per] = dot(compact, hid).astype(BF16)


def down_kernel(cfg, h, pos_ref, own, x, core, xcore, down_hbm, *refs):
    outs = refs[: cfg.groups * 2]
    down, full, sems = refs[cfg.groups * 2:]
    c, t = pos_ref[1], pos_ref[2]
    copies = []
    for e in range(cfg.ne):
        cp = pltpu.make_async_copy(down_hbm.at[h * cfg.ne + e], down.at[e], sems.at[e])
        cp.start()
        copies.append(cp)
    f = own.shape[1]
    for ref, dc, dt in ((own, 0, 0), (x, 1, 0), (core, 0, 1), (xcore, 1, 1)):
        at = (jnp.bitwise_xor(c, dc) * 2 + jnp.bitwise_xor(t, dt)) * f
        full[:, pl.ds(pl.multiple_of(at, 128), f)] = ref[...]
    per = cfg.sources * cfg.cap
    results = []
    for e in range(cfg.ne):
        copies[e].wait()
        results.append(dot(full[e * per:(e + 1) * per], down[e]).astype(BF16))
    width = down.shape[2] // 2
    stacked = jnp.concatenate([v[:, q * width:(q + 1) * width] for q in range(2) for v in results], axis=0)
    m = iota((4 * cfg.rows, 1), 0)
    qt = div(m, cfg.rows)
    p = m - qt * cfg.rows
    e = div(p, cfg.cap)
    slot = p - e * cfg.cap
    want = (qt >> 1) * (cfg.ne * per) + e * per + (qt & 1) * cfg.cap + slot
    lane = iota((1, 2 * cfg.ne * per), 1)
    for r in range(cfg.groups):
        for dc in range(2):
            place = (r * 2 + jnp.bitwise_xor(c, dc)) * 2 * cfg.cap
            outs[r * 2 + dc][...] = dot(onehot(lane - place == want), stacked).astype(BF16)


def combine_kernel(cfg, pos_ref, ids_own, ids_peer, route_own, route_peer, *refs):
    count = PARTS * cfg.groups * 2
    msgs = refs[:count]
    mine, other = refs[count:]
    z, c, t = pos_ref[0], pos_ref[1], pos_ref[2]
    block = 4 * cfg.rows
    lanes = iota((1, PARTS * cfg.groups * block), 1)
    hr = div(lanes, block)
    m = lanes - hr * block
    hh = div(hr, cfg.groups)
    r = hr - hh * cfg.groups
    qt = div(m, cfg.rows)
    p = m - qt * cfg.rows
    code = (jnp.bitwise_xor(r, z) * cfg.local + hh * cfg.ne) * cfg.cap + p + qt * BIG
    picks = []
    for rel, ids in enumerate((ids_own, ids_peer)):
        key = as_column(slot_keys(ids[...], cfg.cap))
        for q in range(2):
            picks.append(onehot(key + (q * 2 + jnp.bitwise_xor(t, rel)) * BIG == code))
    picks = jnp.concatenate(picks, axis=0)
    n = ids_own.shape[1]
    weights = [as_column(route_own[...]), as_column(route_peer[...])]
    for dc in range(2):
        stacked = jnp.concatenate([msgs[k * 2 + dc][...] for k in range(PARTS * cfg.groups)], axis=0)
        got = dot(picks, stacked)
        width = got.shape[1]
        at = jnp.bitwise_xor(c, dc) * (2 * width)
        for rel, out in enumerate((mine, other)):
            for q in range(2):
                k = rel * 2 + q
                out[:, pl.ds(pl.multiple_of(at + q * width, 128), width)] = (weights[rel] * got[k * n:(k + 1) * n]).astype(BF16)


def join_kernel(pos_ref, mine, other, out):
    t = pos_ref[2]
    width = mine.shape[1] // 2
    for cc in range(2):
        for ref, dt in ((mine, 0), (other, 1)):
            at = cc * 2 * width + jnp.bitwise_xor(t, dt) * width
            out[:, pl.ds(pl.multiple_of(at, 128), width)] = ref[:, cc * width:(cc + 1) * width]


class Sizes:
    pass


def swap(x, axis):
    return lax.ppermute(x, axis, [(0, 1), (1, 0)])


def on_device(tokens, expert_ids, route_weights, gate_weight, up_weight, down_weight):
    cfg = Sizes()
    n, width = tokens.shape
    cfg.groups = lax.axis_size("expert")
    cfg.local = gate_weight.shape[0]
    experts = cfg.groups * cfg.local
    cfg.cap = max(2, n * 5 // (4 * experts))
    cfg.ne = cfg.local // PARTS
    cfg.rows = cfg.ne * cfg.cap
    cfg.nd = 16 // cfg.ne
    cfg.w = width // cfg.nd
    cfg.rp = cfg.rows * cfg.nd
    cfg.sources = cfg.groups * 4
    cfg.kb = 4
    f = gate_weight.shape[2]
    ff, wide = down_weight.shape[1:]
    per = cfg.sources * cfg.cap

    z, c, t = (lax.axis_index(a) for a in ("expert", "context", "tensor"))
    pos = jnp.stack([z, c, t]).astype(I32)
    ids = expert_ids.reshape(1, n)
    route = route_weights.reshape(1, n)
    smem = pl.BlockSpec(memory_space=pltpu.SMEM)
    vmem = pl.BlockSpec(memory_space=pltpu.VMEM)
    hbm = pl.BlockSpec(memory_space=pl.ANY)
    params = pltpu.CompilerParams(vmem_limit_bytes=VMEM_LIMIT)

    def call(kernel, ins, outs, scratch=(), name=None):
        return pl.pallas_call(kernel, in_specs=ins, out_specs=[vmem] * len(outs), out_shape=outs,
                              scratch_shapes=scratch, compiler_params=params, name=name)

    shape = jax.ShapeDtypeStruct
    blocks = call(functools.partial(dispatch_kernel, cfg), [smem, vmem, vmem],
                  [shape((cfg.rp, cfg.w), BF16)] * (PARTS * cfg.groups), name="dispatch")(pos, ids, tokens)
    ids_peer, route_peer = swap(ids, "tensor"), swap(route, "tensor")

    arrived = [[blocks[h * cfg.groups]] + [
        lax.ppermute(blocks[h * cfg.groups + r], "expert", [(i, i ^ r) for i in range(cfg.groups)])
        for r in range(1, cfg.groups)] for h in range(PARTS)]
    returned = []
    for h in range(PARTS):
        sources = []
        for a in arrived[h]:
            ax = swap(a, "context")
            sources += [a, swap(a, "tensor"), ax, swap(ax, "tensor")]
        hid = call(
            functools.partial(hidden_kernel, cfg, h), [smem] + [vmem] * cfg.sources + [hbm, hbm],
            [shape((cfg.ne * per, f), BF16)],
            [pltpu.VMEM((cfg.ne, width, f), BF16), pltpu.VMEM((cfg.ne, width, f), BF16),
             pltpu.VMEM((cfg.ne, cfg.sources * 8, width), BF16),
             pltpu.SemaphoreType.DMA((cfg.ne * cfg.kb * 2,))], name="hidden",
        )(pos, *sources, gate_weight, up_weight)[0]
        hx = swap(hid, "context")
        outs = call(
            functools.partial(down_kernel, cfg, h), [smem] + [vmem] * 4 + [hbm],
            [shape((4 * cfg.rows, wide // 2), BF16)] * (cfg.groups * 2),
            [pltpu.VMEM((cfg.ne, ff, wide), BF16), pltpu.VMEM((cfg.ne * per, ff), BF16),
             pltpu.SemaphoreType.DMA((cfg.ne,))], name="down",
        )(pos, hid, hx, swap(hid, "tensor"), swap(hx, "tensor"), down_weight)
        for r in range(cfg.groups):
            for dc in range(2):
                o = outs[r * 2 + dc]
                if r or dc:
                    o = lax.ppermute(o, ("expert", "context"), [
                        (i * 2 + k, (i ^ r) * 2 + (k ^ dc)) for i in range(cfg.groups) for k in range(2)])
                returned.append(o)
    mine, other = call(
        functools.partial(combine_kernel, cfg), [smem] + [vmem] * (4 + len(returned)),
        [shape((n, 2 * wide), BF16)] * 2, name="combine")(pos, ids, ids_peer, route, route_peer, *returned)
    return call(join_kernel, [smem, vmem, vmem], [shape((n, width), BF16)], name="join")(
        pos, mine, swap(other, "tensor"))[0]


def by_gathers(tokens, expert_ids, route_weights, gate_weight, up_weight, down_weight):
    n, width = tokens.shape
    local = gate_weight.shape[0]
    groups = lax.axis_size("expert")
    experts = local * groups
    cap = max(2, n * 5 // (4 * experts))
    ids = expert_ids[:, 0]
    member = (ids[:, None] == jnp.arange(experts, dtype=I32)[None, :]).astype(I32)
    rank = jnp.sum((jnp.cumsum(member, axis=0) - 1) * member, axis=1)
    key = ids * cap + rank
    pick = onehot(key[:, None] == jnp.arange(experts * cap, dtype=I32)[None, :])
    out = jnp.dot(pick.T, tokens, preferred_element_type=F32).astype(BF16)
    out = out.reshape(groups, local, cap, width).transpose(1, 0, 2, 3)
    inc = lax.all_to_all(out, "expert", split_axis=1, concat_axis=1, tiled=True)
    inc = inc.reshape(local, groups * cap, width)
    rows = lax.all_gather(inc, ("context", "tensor"), axis=1, tiled=True)
    g = jnp.einsum("end,edf->enf", rows, gate_weight, preferred_element_type=F32)
    u = jnp.einsum("end,edf->enf", rows, up_weight, preferred_element_type=F32)
    hid = (jax.nn.silu(g) * u).astype(BF16)
    hid = lax.all_gather(hid, ("context", "tensor"), axis=2, tiled=True)
    res = jnp.einsum("erf,efd->erd", hid, down_weight, preferred_element_type=F32).astype(BF16)
    back = lax.all_to_all(res, ("context", "tensor"), split_axis=1, concat_axis=2, tiled=True)
    back = back.reshape(local, groups, cap, width)
    back = lax.all_to_all(back, "expert", split_axis=1, concat_axis=1, tiled=True)
    back = back.transpose(1, 0, 2, 3).reshape(experts * cap, width)
    picked = jnp.dot(pick, back, preferred_element_type=F32)
    return (route_weights * picked).astype(BF16)


def solution(mesh):
    size = dict(mesh.shape)
    paired = size["context"] == 2 and size["tensor"] == 2 and size["expert"] == 4
    rows = P(("group", "expert", "context", "tensor"), None)
    weights = P("expert", None, ("context", "tensor"))
    return jax.shard_map(
        on_device if paired else by_gathers,
        mesh=mesh,
        in_specs=(rows, rows, rows, weights, weights, weights),
        out_specs=rows,
        check_vma=False,
    )
```

time: 133 us -> 101 us (0.76)
  blocking collectives: 46 us -> 0 us
  starting transfers between devices: 4.59 us -> 47.1 us
  Pallas kernels: 0 us -> 26.5 us
  matrix products: 19.4 us -> 0 us
  waiting for transfers between devices: 40.9 us -> 25.3 us
  between operations: 13.5 us -> 0.15 us
  local copies, waits for them, and re-layouts: 5.76 us -> 1.7 us
  other arithmetic: 2.65 us -> 0.08 us
    ppermute x0 -> x53, starting transfers between devices: none -> 47.1 us  [the longest x14 21.9 us: on_device(): lax.ppermute(o, ('expert', 'context'), [(i * 2 + k, (i ^ r) * 2 + (k ^ dc...]
    all_to_all x2 -> x0, blocking collectives: 36.2 us -> none  [the longest x1 23.5 us: on_device(): lax.all_to_all(outgoing, 'expert', split_axis=1, concat_axis=1, tiled=True)]
    pallas_call x0 -> x7, Pallas kernels: none -> 26.5 us  [the longest x2 13.2 us: on_device(): call(functools.partial(hidden_kernel, cfg, h), [smem] + [vmem] * cfg.sour...]
    ppermute x0 -> x53, waiting for transfers between devices: none -> 25.3 us  [the longest x33 12.8 us: swap(): return lax.ppermute(x, axis, [(0, 1), (1, 0)])]
    all_gather x1 -> x0, waiting for transfers between devices: 24.8 us -> none  [on_device(): lax.all_gather(incoming, ('context', 'tensor'), axis=1, tiled=True)]
    dot_general x4 -> x0, matrix products: 19.4 us -> none  [the longest x1 9.68 us: on_device(): jnp.einsum('end,edf->enf', row_block, gate_weight, preferred_element_type...]
    all_to_all x1 -> x0, waiting for transfers between devices: 16 us -> none  [on_device(): lax.all_to_all(gathered_back, 'expert', split_axis=1, concat_axis=1, tile...]
    all_gather x1 -> x0, blocking collectives: 9.86 us -> none  [on_device(): lax.all_gather(hidden_local, ('context', 'tensor'), axis=2, tiled=True)]
  transfers between devices with their start and end apart: 2 -> 53, of which waited for: 2 -> 15; matrix products, arithmetic and copies ran while one was open for 1% -> 0% of each run, Pallas kernels for 0% -> 22%
where the time goes in v1:
time: 101 us
  starting transfers between devices  47.1 us (47%)
  Pallas kernels  26.5 us (26%)
  waiting for transfers between devices  25.3 us (25%)
  local copies, waits for them, and re-layouts  1.7 us (2%)
    ppermute x14, starting transfers between devices, on_device(): lax.ppermute(o, ('expert', 'context'), [(i * 2 + k, (i ^ r) * 2 + (k ^ dc...  21.9 us
    ppermute x33, starting transfers between devices, swap(): return lax.ppermute(x, axis, [(0, 1), (1, 0)])  15.2 us
    pallas_call x2, Pallas kernels, on_device(): call(functools.partial(hidden_kernel, cfg, h), [smem] + [vmem] * cfg.sour...  13.2 us
    ppermute x33, waiting for transfers between devices, swap(): return lax.ppermute(x, axis, [(0, 1), (1, 0)])  12.8 us
    ppermute x6, starting transfers between devices, on_device(): lax.ppermute(blocks[h * cfg.groups + r], 'expert', [(i, i ^ r) for i in r...  10 us
    pallas_call x2, Pallas kernels, on_device(): call(functools.partial(down_kernel, cfg, h), [smem] + [vmem] * 4 + [hbm],...  9.25 us
    ppermute x6, waiting for transfers between devices, on_device(): lax.ppermute(blocks[h * cfg.groups + r], 'expert', [(i, i ^ r) for i in r...  7.4 us
    ppermute x14, waiting for transfers between devices, on_device(): lax.ppermute(o, ('expert', 'context'), [(i * 2 + k, (i ^ r) * 2 + (k ^ dc...  5.08 us
  transfers between devices with their start and end apart: 53, of which 15 were waited for; matrix products, arithmetic and copies ran while one was open for 0% of the time, Pallas kernels for 22%

profile of v1, /device:TPU:0, one launch (start us, length us, event | category | flops | bytes accessed | tf_op | source)
XLA Modules:
  0.0 100.9 jit_solution(16661521181719319442)
XLA Ops:
  1.8 1.5 %dispatch.1 = (bf16[80,512]{1,0:T(8,128)(2,1)S(1)}, bf16[80,512]{1,0:T(8,128)(2,1)S(1)}, bf16[80,512]{1,0:T(8,128)(2,1)S(1)}, bf16[80,512]{1,0:T(8,128)(2,1)S(1)...) custom-call(s32[3]{0:T(128)S(1)} %pad_add_fusion.pos_ref, ...), custom_call_target="tpu_custom_call" | custom-call | tf_op jit(solution)/shard_map/dispatch/pallas_call | solution.py:220
  3.3 3.1 %collective-permute-start.30 = (bf16[80,512]{1,0:T(8,128)(2,1)S(1)}, bf16[80,512]{1,0:T(8,128)(2,1)S(1)}, u32[]{:S(2)}, u32[]{:S(2)}) collective-permute-start(bf16[80,512]{1,0:T(8,128)(2,1)S(1)} %get-tuple-element.44), channel_id=1, source_target_pairs={{0,4},{4,0},{8,12},{12,8},{1,5},{5,1},{9,13},{13,9},{2,6},{6,2},{1... | collective-permute-start | bytes 245768 | tf_op jit(solution)/shard_map/ppermute | solution.py:225
  6.4 2.6 %collective-permute-start.34 = (bf16[80,512]{1,0:T(8,128)(2,1)S(1)}, bf16[80,512]{1,0:T(8,128)(2,1)S(1)}, u32[]{:S(2)}, u32[]{:S(2)}) collective-permute-start(bf16[80,512]{1,0:T(8,128)(2,1)S(1)} %get-tuple-element.45), channel_id=1, source_target_pairs={{0,8},{4,12},{8,0},{12,4},{1,9},{5,13},{9,1},{13,5},{2,10},{6,14},... | collective-permute-start | bytes 245768 | tf_op jit(solution)/shard_map/ppermute | solution.py:225
  9.0 1.7 %collective-permute-start.28 = (bf16[80,512]{1,0:T(8,128)(2,1)S(1)}, bf16[80,512]{1,0:T(8,128)(2,1)S(1)}, u32[]{:S(2)}, u32[]{:S(2)}) collective-permute-start(bf16[80,512]{1,0:T(8,128)(2,1)S(1)} %get-tuple-element.43.refs_0_), channel_id=1, source_target_pairs={{0,2},{2,0},{1,3},{3,1},{4,6},{6,4},{5,7},{7,5},{8,10},{10,8},{9,1... | collective-permute-start | bytes 245768 | tf_op jit(solution)/shard_map/ppermute | solution.py:185
  10.7 1.8 %collective-permute-start.9 = (bf16[80,512]{1,0:T(8,128)(2,1)S(1)}, bf16[80,512]{1,0:T(8,128)(2,1)S(1)}, u32[]{:S(2)}, u32[]{:S(2)}) collective-permute-start(bf16[80,512]{1,0:T(8,128)(2,1)S(1)} %get-tuple-element.33), channel_id=1, source_target_pairs={{0,8},{4,12},{8,0},{12,4},{1,9},{5,13},{9,1},{13,5},{2,10},{6,14},... | collective-permute-start | bytes 245768 | tf_op jit(solution)/shard_map/ppermute | solution.py:225
  12.5 6.0 %collective-permute-done.34.refs_8_ = bf16[80,512]{1,0:T(8,128)(2,1)S(1)} collective-permute-done((bf16[80,512]{1,0:T(8,128)(2,1)S(1)}, bf16[80,512]{1,0:T(8,128)(2,1)S(1)}, u32[]{:S(2)}, u32[]{:S(2)}) %collective-permute-start.34) | collective-permute-done | bytes 81952 | tf_op jit(solution)/shard_map/ppermute | solution.py:225
  18.4 2.6 %collective-permute-start.13 = (bf16[80,512]{1,0:T(8,128)(2,1)S(1)}, bf16[80,512]{1,0:T(8,128)(2,1)S(1)}, u32[]{:S(2)}, u32[]{:S(2)}) collective-permute-start(bf16[80,512]{1,0:T(8,128)(2,1)S(1)} %get-tuple-element.34), channel_id=1, source_target_pairs={{0,12},{4,8},{8,4},{12,0},{1,13},{5,9},{9,5},{13,1},{2,14},{6,10},... | collective-permute-start | bytes 245768 | tf_op jit(solution)/shard_map/ppermute | solution.py:225
  21.0 1.6 %collective-permute-start.3 = (bf16[80,512]{1,0:T(8,128)(2,1)S(1)}, bf16[80,512]{1,0:T(8,128)(2,1)S(1)}, u32[]{:S(2)}, u32[]{:S(2)}) collective-permute-start(bf16[80,512]{1,0:T(8,128)(2,1)S(1)} %get-tuple-element.31.refs_0_), channel_id=1, source_target_pairs={{0,2},{2,0},{1,3},{3,1},{4,6},{6,4},{5,7},{7,5},{8,10},{10,8},{9,1... | collective-permute-start | bytes 245768 | tf_op jit(solution)/shard_map/ppermute | solution.py:185
  27.9 2.2 %collective-permute-done.36.refs_10_ = bf16[80,512]{1,0:T(8,128)(2,1)S(1)} collective-permute-done((bf16[80,512]{1,0:T(8,128)(2,1)S(1)}, bf16[80,512]{1,0:T(8,128)(2,1)S(1)}, u32[]{:S(2)}, u32[]{:S(2)}) %collective-permute-start.36) | collective-permute-done | bytes 81952 | tf_op jit(solution)/shard_map/ppermute | solution.py:185
  40.2 6.7 %hidden.3.own = bf16[160,384]{1,0:T(8,128)(2,1)S(1)} custom-call(s32[3]{0:T(128)S(1)} %pad_add_fusion.pos_ref, bf16[80,512]{1,0:T(8,128)(2,1)S(1)} %get-tuple-element.43.refs_0_, bf16[80,512]{1,0:T(8,128)(2,1)S(1)} %collective-permute-done.27.refs_1_, bf16[80,512]{1,0:T(8,128)(2,1)S(1)} %collective-permute-done.28.refs_2_, ...), custom_call_target="tpu_custom_call" | custom-call | tf_op jit(solution)/shard_map/hidden/pallas_call | solution.py:233
  48.1 6.6 %hidden.2.own = bf16[160,384]{1,0:T(8,128)(2,1)S(1)} custom-call(s32[3]{0:T(128)S(1)} %pad_add_fusion.pos_ref, bf16[80,512]{1,0:T(8,128)(2,1)S(1)} %get-tuple-element.31.refs_0_, bf16[80,512]{1,0:T(8,128)(2,1)S(1)} %collective-permute-done.2.refs_1_, bf16[80,512]{1,0:T(8,128)(2,1)S(1)} %collective-permute-done.3.refs_2_, ...), custom_call_target="tpu_custom_call" | custom-call | tf_op jit(solution)/shard_map/hidden/pallas_call | solution.py:233
  56.1 3.8 %collective-permute-done.17.x = bf16[160,384]{1,0:T(8,128)(2,1)S(1)} collective-permute-done((bf16[160,384]{1,0:T(8,128)(2,1)S(1)}, bf16[160,384]{1,0:T(8,128)(2,1)S(1)}, u32[]{:S(2)}, u32[]{:S(2)}) %collective-permute-start.17) | collective-permute-done | bytes 122912 | tf_op jit(solution)/shard_map/ppermute | solution.py:185
  60.5 4.6 %down.3 = (bf16[40,512]{1,0:T(8,128)(2,1)S(1)}, bf16[40,512]{1,0:T(8,128)(2,1)S(1)}, bf16[40,512]{1,0:T(8,128)(2,1)S(1)}, bf16[40,512]{1,0:T(8,128)(2,1)S(1)}, b...) custom-call(s32[3]{0:T(128)S(1)} %pad_add_fusion.pos_ref, ...), custom_call_target="tpu_custom_call" | custom-call | tf_op jit(solution)/shard_map/down/pallas_call | solution.py:241
  66.0 1.9 %collective-permute-start.46 = (bf16[40,512]{1,0:T(8,128)(2,1)S(1)}, bf16[40,512]{1,0:T(8,128)(2,1)S(1)}, u32[]{:S(2)}, u32[]{:S(2)}) collective-permute-start(bf16[40,512]{1,0:T(8,128)(2,1)S(1)} %get-tuple-element.49), channel_id=1, source_target_pairs={{0,4},{2,6},{4,0},{6,2},{8,12},{10,14},{12,8},{14,10},{1,5},{3,7},... | collective-permute-start | bytes 122888 | tf_op jit(solution)/shard_map/ppermute | solution.py:251
  70.1 4.6 %down.2 = (bf16[40,512]{1,0:T(8,128)(2,1)S(1)}, bf16[40,512]{1,0:T(8,128)(2,1)S(1)}, bf16[40,512]{1,0:T(8,128)(2,1)S(1)}, bf16[40,512]{1,0:T(8,128)(2,1)S(1)}, b...) custom-call(s32[3]{0:T(128)S(1)} %pad_add_fusion.pos_ref, ...), custom_call_target="tpu_custom_call" | custom-call | tf_op jit(solution)/shard_map/down/pallas_call | solution.py:241
  74.8 1.8 %collective-permute-start.49 = (bf16[40,512]{1,0:T(8,128)(2,1)S(1)}, bf16[40,512]{1,0:T(8,128)(2,1)S(1)}, u32[]{:S(2)}, u32[]{:S(2)}) collective-permute-start(bf16[40,512]{1,0:T(8,128)(2,1)S(1)} %get-tuple-element.52), channel_id=1, source_target_pairs={{0,10},{2,8},{4,14},{6,12},{8,2},{10,0},{12,6},{14,4},{1,11},{3,9}... | collective-permute-start | bytes 122888 | tf_op jit(solution)/shard_map/ppermute | solution.py:251
  76.6 2.2 %collective-permute-start.50 = (bf16[40,512]{1,0:T(8,128)(2,1)S(1)}, bf16[40,512]{1,0:T(8,128)(2,1)S(1)}, u32[]{:S(2)}, u32[]{:S(2)}) collective-permute-start(bf16[40,512]{1,0:T(8,128)(2,1)S(1)} %get-tuple-element.53), channel_id=1, source_target_pairs={{0,12},{2,14},{4,8},{6,10},{8,4},{10,6},{12,0},{14,2},{1,13},{3,15... | collective-permute-start | bytes 122888 | tf_op jit(solution)/shard_map/ppermute | solution.py:251
  78.9 2.2 %collective-permute-start.51 = (bf16[40,512]{1,0:T(8,128)(2,1)S(1)}, bf16[40,512]{1,0:T(8,128)(2,1)S(1)}, u32[]{:S(2)}, u32[]{:S(2)}) collective-permute-start(bf16[40,512]{1,0:T(8,128)(2,1)S(1)} %get-tuple-element.54), channel_id=1, source_target_pairs={{0,14},{2,12},{4,10},{6,8},{8,6},{10,4},{12,2},{14,0},{1,15},{3,13... | collective-permute-start | bytes 122888 | tf_op jit(solution)/shard_map/ppermute | solution.py:251
  82.0 2.5 %collective-permute-start.22 = (bf16[40,512]{1,0:T(8,128)(2,1)S(1)}, bf16[40,512]{1,0:T(8,128)(2,1)S(1)}, u32[]{:S(2)}, u32[]{:S(2)}) collective-permute-start(bf16[40,512]{1,0:T(8,128)(2,1)S(1)} %get-tuple-element.38), channel_id=1, source_target_pairs={{0,6},{2,4},{4,2},{6,0},{8,14},{10,12},{12,10},{14,8},{1,7},{3,5},... | collective-permute-start | bytes 122888 | tf_op jit(solution)/shard_map/ppermute | solution.py:251
  85.9 1.9 %collective-permute-start.24 = (bf16[40,512]{1,0:T(8,128)(2,1)S(1)}, bf16[40,512]{1,0:T(8,128)(2,1)S(1)}, u32[]{:S(2)}, u32[]{:S(2)}) collective-permute-start(bf16[40,512]{1,0:T(8,128)(2,1)S(1)} %get-tuple-element.40), channel_id=1, source_target_pairs={{0,10},{2,8},{4,14},{6,12},{8,2},{10,0},{12,6},{14,4},{1,11},{3,9}... | collective-permute-start | bytes 122888 | tf_op jit(solution)/shard_map/ppermute | solution.py:251
  87.8 2.2 %collective-permute-start.25 = (bf16[40,512]{1,0:T(8,128)(2,1)S(1)}, bf16[40,512]{1,0:T(8,128)(2,1)S(1)}, u32[]{:S(2)}, u32[]{:S(2)}) collective-permute-start(bf16[40,512]{1,0:T(8,128)(2,1)S(1)} %get-tuple-element.41), channel_id=1, source_target_pairs={{0,12},{2,14},{4,8},{6,10},{8,4},{10,6},{12,0},{14,2},{1,13},{3,15... | collective-permute-start | bytes 122888 | tf_op jit(solution)/shard_map/ppermute | solution.py:251
  90.0 2.2 %collective-permute-start.26 = (bf16[40,512]{1,0:T(8,128)(2,1)S(1)}, bf16[40,512]{1,0:T(8,128)(2,1)S(1)}, u32[]{:S(2)}, u32[]{:S(2)}) collective-permute-start(bf16[40,512]{1,0:T(8,128)(2,1)S(1)} %get-tuple-element.42), channel_id=1, source_target_pairs={{0,14},{2,12},{4,10},{6,8},{8,6},{10,4},{12,2},{14,0},{1,15},{3,13... | collective-permute-start | bytes 122888 | tf_op jit(solution)/shard_map/ppermute | solution.py:251
  93.9 2.8 %collective-permute-done.26.refs_7_ = bf16[40,512]{1,0:T(8,128)(2,1)S(1)} collective-permute-done((bf16[40,512]{1,0:T(8,128)(2,1)S(1)}, bf16[40,512]{1,0:T(8,128)(2,1)S(1)}, u32[]{:S(2)}, u32[]{:S(2)}) %collective-permute-start.26) | collective-permute-done | bytes 40992 | tf_op jit(solution)/shard_map/ppermute | solution.py:251
  98.0 1.5 %collective-permute-done.52.other = bf16[64,2048]{1,0:T(8,128)(2,1)S(1)} collective-permute-done((bf16[64,2048]{1,0:T(8,128)(2,1)S(1)}, bf16[64,2048]{1,0:T(8,128)(2,1)S(1)}, u32[]{:S(2)}, u32[]{:S(2)}) %collective-permute-start.52) | collective-permute-done | bytes 262176 | tf_op jit(solution)/shard_map/ppermute | solution.py:185
  (96 shorter events, 30.2 us)
Async XLA Ops:
  3.3 7.4 %collective-permute-start.30 = (bf16[80,512]{1,0:T(8,128)(2,1)S(1)}, bf16[80,512]{1,0:T(8,128)(2,1)S(1)}, u32[]{:S(2)}, u32[]{:S(2)}) collective-permute-start(bf16[80,512]{1,0:T(8,128)(2,1)S(1)} %get-tuple-element.44), channel_id=1, source_target_pairs={{0,4},{4,0},{8,12},{12,8},{1,5},{5,1},{9,13},{13,9},{2,6},{6,2},{1... | collective-permute-start | bytes 245768 | tf_op jit(solution)/shard_map/ppermute | solution.py:225
  6.4 12.0 %collective-permute-start.34 = (bf16[80,512]{1,0:T(8,128)(2,1)S(1)}, bf16[80,512]{1,0:T(8,128)(2,1)S(1)}, u32[]{:S(2)}, u32[]{:S(2)}) collective-permute-start(bf16[80,512]{1,0:T(8,128)(2,1)S(1)} %get-tuple-element.45), channel_id=1, source_target_pairs={{0,8},{4,12},{8,0},{12,4},{1,9},{5,13},{9,1},{13,5},{2,10},{6,14},... | collective-permute-start | bytes 245768 | tf_op jit(solution)/shard_map/ppermute | solution.py:225
  9.0 12.0 %collective-permute-start.38 = (bf16[80,512]{1,0:T(8,128)(2,1)S(1)}, bf16[80,512]{1,0:T(8,128)(2,1)S(1)}, u32[]{:S(2)}, u32[]{:S(2)}) collective-permute-start(bf16[80,512]{1,0:T(8,128)(2,1)S(1)} %get-tuple-element.46), channel_id=1, source_target_pairs={{0,12},{4,8},{8,4},{12,0},{1,13},{5,9},{9,5},{13,1},{2,14},{6,10},... | collective-permute-start | bytes 245768 | tf_op jit(solution)/shard_map/ppermute | solution.py:225
  9.0 12.0 %collective-permute-start.28 = (bf16[80,512]{1,0:T(8,128)(2,1)S(1)}, bf16[80,512]{1,0:T(8,128)(2,1)S(1)}, u32[]{:S(2)}, u32[]{:S(2)}) collective-permute-start(bf16[80,512]{1,0:T(8,128)(2,1)S(1)} %get-tuple-element.43.refs_0_), channel_id=1, source_target_pairs={{0,2},{2,0},{1,3},{3,1},{4,6},{6,4},{5,7},{7,5},{8,10},{10,8},{9,1... | collective-permute-start | bytes 245768 | tf_op jit(solution)/shard_map/ppermute | solution.py:185
  10.7 11.9 %collective-permute-start.27 = (bf16[80,512]{1,0:T(8,128)(2,1)S(1)}, bf16[80,512]{1,0:T(8,128)(2,1)S(1)}, u32[]{:S(2)}, u32[]{:S(2)}) collective-permute-start(bf16[80,512]{1,0:T(8,128)(2,1)S(1)} %get-tuple-element.43.refs_0_), channel_id=1, source_target_pairs={{0,1},{1,0},{2,3},{3,2},{4,5},{5,4},{6,7},{7,6},{8,9},{9,8},{10,11... | collective-permute-start | bytes 245768 | tf_op jit(solution)/shard_map/ppermute | solution.py:185
  10.7 11.9 %collective-permute-start.9 = (bf16[80,512]{1,0:T(8,128)(2,1)S(1)}, bf16[80,512]{1,0:T(8,128)(2,1)S(1)}, u32[]{:S(2)}, u32[]{:S(2)}) collective-permute-start(bf16[80,512]{1,0:T(8,128)(2,1)S(1)} %get-tuple-element.33), channel_id=1, source_target_pairs={{0,8},{4,12},{8,0},{12,4},{1,9},{5,13},{9,1},{13,5},{2,10},{6,14},... | collective-permute-start | bytes 245768 | tf_op jit(solution)/shard_map/ppermute | solution.py:225
  38.6 8.2 %collective-permute-start.14 = (bf16[80,512]{1,0:T(8,128)(2,1)S(1)}, bf16[80,512]{1,0:T(8,128)(2,1)S(1)}, u32[]{:S(2)}, u32[]{:S(2)}) collective-permute-start(bf16[80,512]{1,0:T(8,128)(2,1)S(1)} %collective-permute-done.13.refs_12_), channel_id=1, source_target_pairs={{0,1},{1,0},{2,3},{3,2},{4,5},{5,4},{6,7},{7,6},{8,9},{9,8},{10,11... | collective-permute-start | bytes 245768 | tf_op jit(solution)/shard_map/ppermute | solution.py:185
  39.1 8.9 %collective-permute-start.6 = (bf16[80,512]{1,0:T(8,128)(2,1)S(1)}, bf16[80,512]{1,0:T(8,128)(2,1)S(1)}, u32[]{:S(2)}, u32[]{:S(2)}) collective-permute-start(bf16[80,512]{1,0:T(8,128)(2,1)S(1)} %collective-permute-done.5.refs_4_), channel_id=1, source_target_pairs={{0,1},{1,0},{2,3},{3,2},{4,5},{5,4},{6,7},{7,6},{8,9},{9,8},{10,11... | collective-permute-start | bytes 245768 | tf_op jit(solution)/shard_map/ppermute | solution.py:185
  39.2 8.9 %collective-permute-start.12 = (bf16[80,512]{1,0:T(8,128)(2,1)S(1)}, bf16[80,512]{1,0:T(8,128)(2,1)S(1)}, u32[]{:S(2)}, u32[]{:S(2)}) collective-permute-start(bf16[80,512]{1,0:T(8,128)(2,1)S(1)} %collective-permute-done.11.refs_10_), channel_id=1, source_target_pairs={{0,1},{1,0},{2,3},{3,2},{4,5},{5,4},{6,7},{7,6},{8,9},{9,8},{10,11... | collective-permute-start | bytes 245768 | tf_op jit(solution)/shard_map/ppermute | solution.py:185
  39.7 8.4 %collective-permute-start.16 = (bf16[80,512]{1,0:T(8,128)(2,1)S(1)}, bf16[80,512]{1,0:T(8,128)(2,1)S(1)}, u32[]{:S(2)}, u32[]{:S(2)}) collective-permute-start(bf16[80,512]{1,0:T(8,128)(2,1)S(1)} %collective-permute-done.15.refs_14_), channel_id=1, source_target_pairs={{0,1},{1,0},{2,3},{3,2},{4,5},{5,4},{6,7},{7,6},{8,9},{9,8},{10,11... | collective-permute-start | bytes 245768 | tf_op jit(solution)/shard_map/ppermute | solution.py:185
  39.9 8.2 %collective-permute-start.8 = (bf16[80,512]{1,0:T(8,128)(2,1)S(1)}, bf16[80,512]{1,0:T(8,128)(2,1)S(1)}, u32[]{:S(2)}, u32[]{:S(2)}) collective-permute-start(bf16[80,512]{1,0:T(8,128)(2,1)S(1)} %collective-permute-done.7.refs_6_), channel_id=1, source_target_pairs={{0,1},{1,0},{2,3},{3,2},{4,5},{5,4},{6,7},{7,6},{8,9},{9,8},{10,11... | collective-permute-start | bytes 245768 | tf_op jit(solution)/shard_map/ppermute | solution.py:185
  46.9 8.8 %collective-permute-start.42 = (bf16[160,384]{1,0:T(8,128)(2,1)S(1)}, bf16[160,384]{1,0:T(8,128)(2,1)S(1)}, u32[]{:S(2)}, u32[]{:S(2)}) collective-permute-start(bf16[160,384]{1,0:T(8,128)(2,1)S(1)} %hidden.3.own), channel_id=1, source_target_pairs={{0,2},{2,0},{1,3},{3,1},{4,6},{6,4},{5,7},{7,5},{8,10},{10,8},{9,1... | collective-permute-start | bytes 368648 | tf_op jit(solution)/shard_map/ppermute | solution.py:185
  56.1 12.5 %collective-permute-start.18 = (bf16[160,384]{1,0:T(8,128)(2,1)S(1)}, bf16[160,384]{1,0:T(8,128)(2,1)S(1)}, u32[]{:S(2)}, u32[]{:S(2)}) collective-permute-start(bf16[160,384]{1,0:T(8,128)(2,1)S(1)} %hidden.2.own), channel_id=1, source_target_pairs={{0,1},{1,0},{2,3},{3,2},{4,5},{5,4},{6,7},{7,6},{8,9},{9,8},{10,11... | collective-permute-start | bytes 368648 | tf_op jit(solution)/shard_map/ppermute | solution.py:185
  59.9 10.2 %collective-permute-start.19 = (bf16[160,384]{1,0:T(8,128)(2,1)S(1)}, bf16[160,384]{1,0:T(8,128)(2,1)S(1)}, u32[]{:S(2)}, u32[]{:S(2)}) collective-permute-start(bf16[160,384]{1,0:T(8,128)(2,1)S(1)} %collective-permute-done.17.x), channel_id=1, source_target_pairs={{0,1},{1,0},{2,3},{3,2},{4,5},{5,4},{6,7},{7,6},{8,9},{9,8},{10,11... | collective-permute-start | bytes 368648 | tf_op jit(solution)/shard_map/ppermute | solution.py:185
  60.0 8.0 %collective-permute-start = (s32[1,64]{1,0:T(1,128)S(1)}, s32[1,64]{1,0:T(1,128)S(1)}, u32[]{:S(2)}, u32[]{:S(2)}) collective-permute-start(s32[1,64]{1,0:T(1,128)S(1)} %bitcast.6), channel_id=1, source_target_pairs={{0,1},{1,0},{2,3},{3,2},{4,5},{5,4},{6,7},{7,6},{8,9},{9,8},{10,11... | collective-permute-start | bytes 776 | tf_op jit(solution)/shard_map/ppermute | solution.py:185
  65.1 11.5 %collective-permute-start.45 = (bf16[40,512]{1,0:T(8,128)(2,1)S(1)}, bf16[40,512]{1,0:T(8,128)(2,1)S(1)}, u32[]{:S(2)}, u32[]{:S(2)}) collective-permute-start(bf16[40,512]{1,0:T(8,128)(2,1)S(1)} %get-tuple-element.48), channel_id=1, source_target_pairs={{0,2},{2,0},{4,6},{6,4},{8,10},{10,8},{12,14},{14,12},{1,3},{3,1},... | collective-permute-start | bytes 122888 | tf_op jit(solution)/shard_map/ppermute | solution.py:251
  66.0 12.8 %collective-permute-start.46 = (bf16[40,512]{1,0:T(8,128)(2,1)S(1)}, bf16[40,512]{1,0:T(8,128)(2,1)S(1)}, u32[]{:S(2)}, u32[]{:S(2)}) collective-permute-start(bf16[40,512]{1,0:T(8,128)(2,1)S(1)} %get-tuple-element.49), channel_id=1, source_target_pairs={{0,4},{2,6},{4,0},{6,2},{8,12},{10,14},{12,8},{14,10},{1,5},{3,7},... | collective-permute-start | bytes 122888 | tf_op jit(solution)/shard_map/ppermute | solution.py:251
  67.9 13.1 %collective-permute-start.47 = (bf16[40,512]{1,0:T(8,128)(2,1)S(1)}, bf16[40,512]{1,0:T(8,128)(2,1)S(1)}, u32[]{:S(2)}, u32[]{:S(2)}) collective-permute-start(bf16[40,512]{1,0:T(8,128)(2,1)S(1)} %get-tuple-element.50), channel_id=1, source_target_pairs={{0,6},{2,4},{4,2},{6,0},{8,14},{10,12},{12,10},{14,8},{1,7},{3,5},... | collective-permute-start | bytes 122888 | tf_op jit(solution)/shard_map/ppermute | solution.py:251
  68.7 13.3 %collective-permute-start.48 = (bf16[40,512]{1,0:T(8,128)(2,1)S(1)}, bf16[40,512]{1,0:T(8,128)(2,1)S(1)}, u32[]{:S(2)}, u32[]{:S(2)}) collective-permute-start(bf16[40,512]{1,0:T(8,128)(2,1)S(1)} %get-tuple-element.51), channel_id=1, source_target_pairs={{0,8},{2,10},{4,12},{6,14},{8,0},{10,2},{12,4},{14,6},{1,9},{3,11}... | collective-permute-start | bytes 122888 | tf_op jit(solution)/shard_map/ppermute | solution.py:251
  74.8 7.2 %collective-permute-start.49 = (bf16[40,512]{1,0:T(8,128)(2,1)S(1)}, bf16[40,512]{1,0:T(8,128)(2,1)S(1)}, u32[]{:S(2)}, u32[]{:S(2)}) collective-permute-start(bf16[40,512]{1,0:T(8,128)(2,1)S(1)} %get-tuple-element.52), channel_id=1, source_target_pairs={{0,10},{2,8},{4,14},{6,12},{8,2},{10,0},{12,6},{14,4},{1,11},{3,9}... | collective-permute-start | bytes 122888 | tf_op jit(solution)/shard_map/ppermute | solution.py:251
  76.6 7.9 %collective-permute-start.50 = (bf16[40,512]{1,0:T(8,128)(2,1)S(1)}, bf16[40,512]{1,0:T(8,128)(2,1)S(1)}, u32[]{:S(2)}, u32[]{:S(2)}) collective-permute-start(bf16[40,512]{1,0:T(8,128)(2,1)S(1)} %get-tuple-element.53), channel_id=1, source_target_pairs={{0,12},{2,14},{4,8},{6,10},{8,4},{10,6},{12,0},{14,2},{1,13},{3,15... | collective-permute-start | bytes 122888 | tf_op jit(solution)/shard_map/ppermute | solution.py:251
  81.9 8.1 %collective-permute-start.21 = (bf16[40,512]{1,0:T(8,128)(2,1)S(1)}, bf16[40,512]{1,0:T(8,128)(2,1)S(1)}, u32[]{:S(2)}, u32[]{:S(2)}) collective-permute-start(bf16[40,512]{1,0:T(8,128)(2,1)S(1)} %get-tuple-element.37), channel_id=1, source_target_pairs={{0,4},{2,6},{4,0},{6,2},{8,12},{10,14},{12,8},{14,10},{1,5},{3,7},... | collective-permute-start | bytes 122888 | tf_op jit(solution)/shard_map/ppermute | solution.py:251
  82.0 10.2 %collective-permute-start.22 = (bf16[40,512]{1,0:T(8,128)(2,1)S(1)}, bf16[40,512]{1,0:T(8,128)(2,1)S(1)}, u32[]{:S(2)}, u32[]{:S(2)}) collective-permute-start(bf16[40,512]{1,0:T(8,128)(2,1)S(1)} %get-tuple-element.38), channel_id=1, source_target_pairs={{0,6},{2,4},{4,2},{6,0},{8,14},{10,12},{12,10},{14,8},{1,7},{3,5},... | collective-permute-start | bytes 122888 | tf_op jit(solution)/shard_map/ppermute | solution.py:251
  84.5 7.7 %collective-permute-start.23 = (bf16[40,512]{1,0:T(8,128)(2,1)S(1)}, bf16[40,512]{1,0:T(8,128)(2,1)S(1)}, u32[]{:S(2)}, u32[]{:S(2)}) collective-permute-start(bf16[40,512]{1,0:T(8,128)(2,1)S(1)} %get-tuple-element.39), channel_id=1, source_target_pairs={{0,8},{2,10},{4,12},{6,14},{8,0},{10,2},{12,4},{14,6},{1,9},{3,11}... | collective-permute-start | bytes 122888 | tf_op jit(solution)/shard_map/ppermute | solution.py:251
  (32 other events, 162.7 us)

commit v2 on v1

--- a/solution.py
+++ b/solution.py
@@ -7,8 +7,9 @@
 from jax.sharding import PartitionSpec as P
 
 BIG = 4096
-PARTS = 2
-VMEM_LIMIT = 48 * 1024 * 1024
+PARTS = 1
+LEAD = 20 * 10**9
+VMEM_LIMIT = 16 * 1024 * 1024
 F32, BF16, I32 = jnp.float32, jnp.bfloat16, jnp.int32
 
 
@@ -59,19 +60,7 @@
 
 def hidden_kernel(cfg, h, pos_ref, *refs):
     srcs = refs[: cfg.sources]
-    gate_hbm, up_hbm, out_ref, gate, up, rows, sems = refs[cfg.sources:]
-    kb = cfg.kb
-    depth = gate.shape[1] // kb
-    copies = []
-    for e in range(cfg.ne):
-        for k in range(kb):
-            part = pl.ds(k * depth, depth)
-            pair = []
-            for m, (src, dst) in enumerate(((gate_hbm, gate), (up_hbm, up))):
-                cp = pltpu.make_async_copy(src.at[h * cfg.ne + e, part], dst.at[e, part], sems.at[(e * kb + k) * 2 + m])
-                cp.start()
-                pair.append(cp)
-            copies.append(pair)
+    gate, up, out_ref, rows = refs[cfg.sources:]
     je = cfg.nd * cfg.ne
     i, c = iota((je * 16, 1), 0), iota((1, 2 * cfg.rp), 1)
     slot = i & 7
@@ -91,26 +80,16 @@
     rel = jnp.bitwise_xor(s, pos_ref[1] * 2 + pos_ref[2])
     compact = onehot(iota((1, cfg.sources * 8), 1) == rel * 8 + slot)
     for e in range(cfg.ne):
-        g = u = 0.0
-        for k in range(kb):
-            for cp in copies[e * kb + k]:
-                cp.wait()
-            x = rows[e, :, k * depth:(k + 1) * depth]
-            g = g + dot(x, gate[e, k * depth:(k + 1) * depth])
-            u = u + dot(x, up[e, k * depth:(k + 1) * depth])
+        both = dot(rows[e], jnp.concatenate([gate[h * cfg.ne + e], up[h * cfg.ne + e]], axis=1))
+        g, u = jnp.split(both, 2, axis=1)
         hid = (g / (1.0 + jnp.exp(-g)) * u).astype(BF16)
         out_ref[e * per:(e + 1) * per] = dot(compact, hid).astype(BF16)
 
 
-def down_kernel(cfg, h, pos_ref, own, x, core, xcore, down_hbm, *refs):
+def down_kernel(cfg, h, pos_ref, own, x, core, xcore, down, *refs):
     outs = refs[: cfg.groups * 2]
-    down, full, sems = refs[cfg.groups * 2:]
+    full = refs[cfg.groups * 2]
     c, t = pos_ref[1], pos_ref[2]
-    copies = []
-    for e in range(cfg.ne):
-        cp = pltpu.make_async_copy(down_hbm.at[h * cfg.ne + e], down.at[e], sems.at[e])
-        cp.start()
-        copies.append(cp)
     f = own.shape[1]
     for ref, dc, dt in ((own, 0, 0), (x, 1, 0), (core, 0, 1), (xcore, 1, 1)):
         at = (jnp.bitwise_xor(c, dc) * 2 + jnp.bitwise_xor(t, dt)) * f
@@ -118,8 +97,7 @@
     per = cfg.sources * cfg.cap
     results = []
     for e in range(cfg.ne):
-        copies[e].wait()
-        results.append(dot(full[e * per:(e + 1) * per], down[e]).astype(BF16))
+        results.append(dot(full[e * per:(e + 1) * per], down[h * cfg.ne + e]).astype(BF16))
     width = down.shape[2] // 2
     stacked = jnp.concatenate([v[:, q * width:(q + 1) * width] for q in range(2) for v in results], axis=0)
     m = iota((4 * cfg.rows, 1), 0)
@@ -198,7 +176,6 @@
     cfg.w = width // cfg.nd
     cfg.rp = cfg.rows * cfg.nd
     cfg.sources = cfg.groups * 4
-    cfg.kb = 4
     f = gate_weight.shape[2]
     ff, wide = down_weight.shape[1:]
     per = cfg.sources * cfg.cap
@@ -209,16 +186,16 @@
     route = route_weights.reshape(1, n)
     smem = pl.BlockSpec(memory_space=pltpu.SMEM)
     vmem = pl.BlockSpec(memory_space=pltpu.VMEM)
-    hbm = pl.BlockSpec(memory_space=pl.ANY)
     params = pltpu.CompilerParams(vmem_limit_bytes=VMEM_LIMIT)
 
-    def call(kernel, ins, outs, scratch=(), name=None):
+    def call(kernel, ins, outs, scratch=(), name=None, cost=None):
         return pl.pallas_call(kernel, in_specs=ins, out_specs=[vmem] * len(outs), out_shape=outs,
-                              scratch_shapes=scratch, compiler_params=params, name=name)
+                              scratch_shapes=scratch, compiler_params=params, name=name, cost_estimate=cost)
 
     shape = jax.ShapeDtypeStruct
     blocks = call(functools.partial(dispatch_kernel, cfg), [smem, vmem, vmem],
-                  [shape((cfg.rp, cfg.w), BF16)] * (PARTS * cfg.groups), name="dispatch")(pos, ids, tokens)
+                  [shape((cfg.rp, cfg.w), BF16)] * (PARTS * cfg.groups), name="dispatch",
+                  cost=pl.CostEstimate(flops=LEAD, bytes_accessed=0, transcendentals=0))(pos, ids, tokens)
     ids_peer, route_peer = swap(ids, "tensor"), swap(route, "tensor")
 
     arrived = [[blocks[h * cfg.groups]] + [
@@ -226,23 +203,27 @@
         for r in range(1, cfg.groups)] for h in range(PARTS)]
     returned = []
     for h in range(PARTS):
+        near = [swap(a, "context") for a in arrived[h][:2]]
+        far = arrived[h][2:]
+        far2 = []
+        for a in far:
+            a, n1 = lax.optimization_barrier((a, near[1]))
+            far2.append(a)
+            near[1] = n1
+        far = far2
         sources = []
-        for a in arrived[h]:
-            ax = swap(a, "context")
+        for a, ax in zip(arrived[h][:2] + far, near + [swap(a, "context") for a in far]):
             sources += [a, swap(a, "tensor"), ax, swap(ax, "tensor")]
         hid = call(
-            functools.partial(hidden_kernel, cfg, h), [smem] + [vmem] * cfg.sources + [hbm, hbm],
+            functools.partial(hidden_kernel, cfg, h), [smem] + [vmem] * (cfg.sources + 2),
             [shape((cfg.ne * per, f), BF16)],
-            [pltpu.VMEM((cfg.ne, width, f), BF16), pltpu.VMEM((cfg.ne, width, f), BF16),
-             pltpu.VMEM((cfg.ne, cfg.sources * 8, width), BF16),
-             pltpu.SemaphoreType.DMA((cfg.ne * cfg.kb * 2,))], name="hidden",
+            [pltpu.VMEM((cfg.ne, cfg.sources * 8, width), BF16)], name="hidden",
         )(pos, *sources, gate_weight, up_weight)[0]
         hx = swap(hid, "context")
         outs = call(
-            functools.partial(down_kernel, cfg, h), [smem] + [vmem] * 4 + [hbm],
+            functools.partial(down_kernel, cfg, h), [smem] + [vmem] * 5,
             [shape((4 * cfg.rows, wide // 2), BF16)] * (cfg.groups * 2),
-            [pltpu.VMEM((cfg.ne, ff, wide), BF16), pltpu.VMEM((cfg.ne * per, ff), BF16),
-             pltpu.SemaphoreType.DMA((cfg.ne,))], name="down",
+            [pltpu.VMEM((cfg.ne * per, ff), BF16)], name="down",
         )(pos, hid, hx, swap(hid, "tensor"), swap(hx, "tensor"), down_weight)
         for r in range(cfg.groups):
             for dc in range(2):

time: 101 us -> 77.9 us (0.77); the launches traced: 101 us -> 76.6 us
  starting transfers between devices: 47.1 us -> 28.1 us
  Pallas kernels: 26.5 us -> 14.6 us
  waiting for transfers between devices: 25.3 us -> 32 us
    pallas_call x4 -> x2, Pallas kernels: 22.5 us -> 10.9 us  [the longest x1 6.93 us: on_device(): call(functools.partial(hidden_kernel, cfg, h), [smem] + [vmem] * (cfg.sou...]
    ppermute x14 -> x7, starting transfers between devices: 21.9 us -> 12.5 us  [on_device(): lax.ppermute(o, ('expert', 'context'), [(i * 2 + k, (i ^ r) * 2 + (k ^ dc...]
    ppermute x33 -> x18, starting transfers between devices: 15.2 us -> 7.41 us  [swap(): return lax.ppermute(x, axis, [(0, 1), (1, 0)])]
    ppermute x33 -> x18, waiting for transfers between devices: 12.8 us -> 17.6 us  [swap(): return lax.ppermute(x, axis, [(0, 1), (1, 0)])]
    ppermute x14 -> x7, waiting for transfers between devices: 5.08 us -> 7.33 us  [on_device(): lax.ppermute(o, ('expert', 'context'), [(i * 2 + k, (i ^ r) * 2 + (k ^ dc...]
    ppermute x6 -> x3, starting transfers between devices: 10 us -> 8.15 us  [on_device(): lax.ppermute(blocks[h * cfg.groups + r], 'expert', [(i, i ^ r) for i in r...]
    ppermute x6 -> x3, waiting for transfers between devices: 7.4 us -> 7.08 us  [on_device(): lax.ppermute(blocks[h * cfg.groups + r], 'expert', [(i, i ^ r) for i in r...]
  transfers between devices with their start and end apart: 53 -> 28, of which waited for: 15 -> 12; matrix products, arithmetic and copies ran while one was open for 0% -> 0% of each run, Pallas kernels for 22% -> 0%
where the time goes in v2:
time: 77.9 us; the launch traced here: 76.6 us
  waiting for transfers between devices  32 us (41%)
  starting transfers between devices  28.1 us (36%)
  Pallas kernels  14.6 us (19%)
  local copies, waits for them, and re-layouts  1.72 us (2%)
    ppermute x18, waiting for transfers between devices, swap(): return lax.ppermute(x, axis, [(0, 1), (1, 0)])  17.6 us
    ppermute x7, starting transfers between devices, on_device(): lax.ppermute(o, ('expert', 'context'), [(i * 2 + k, (i ^ r) * 2 + (k ^ dc...  12.5 us
    ppermute x3, starting transfers between devices, on_device(): lax.ppermute(blocks[h * cfg.groups + r], 'expert', [(i, i ^ r) for i in r...  8.15 us
    ppermute x18, starting transfers between devices, swap(): return lax.ppermute(x, axis, [(0, 1), (1, 0)])  7.41 us
    ppermute x7, waiting for transfers between devices, on_device(): lax.ppermute(o, ('expert', 'context'), [(i * 2 + k, (i ^ r) * 2 + (k ^ dc...  7.33 us
    ppermute x3, waiting for transfers between devices, on_device(): lax.ppermute(blocks[h * cfg.groups + r], 'expert', [(i, i ^ r) for i in r...  7.08 us
    pallas_call x1, Pallas kernels, on_device(): call(functools.partial(hidden_kernel, cfg, h), [smem] + [vmem] * (cfg.sou...  6.93 us
    pallas_call x1, Pallas kernels, on_device(): call(functools.partial(down_kernel, cfg, h), [smem] + [vmem] * 5, [shape(...  3.98 us
  transfers between devices with their start and end apart: 28, of which 12 were waited for; matrix products, arithmetic and copies ran while one was open for 0% of the time, Pallas kernels for 0%

profile of v2, /device:TPU:0, one launch (start us, length us, event | category | flops | bytes accessed | tf_op | source)
XLA Modules:
  0.0 76.6 jit_solution(16758530991389147087)
XLA Ops:
  3.0 3.1 %collective-permute-start.5 = (bf16[80,1024]{1,0:T(8,128)(2,1)S(1)}, bf16[80,1024]{1,0:T(8,128)(2,1)S(1)}, u32[]{:S(2)}, u32[]{:S(2)}) collective-permute-start(bf16[80,1024]{1,0:T(8,128)(2,1)S(1)} %get-tuple-element.24), channel_id=1, source_target_pairs={{0,4},{4,0},{8,12},{12,8},{1,5},{5,1},{9,13},{13,9},{2,6},{6,2},{1... | collective-permute-start | bytes 491528 | tf_op jit(solution)/shard_map/ppermute | solution.py:202
  6.1 2.6 %collective-permute-start.8 = (bf16[80,1024]{1,0:T(8,128)(2,1)S(1)}, bf16[80,1024]{1,0:T(8,128)(2,1)S(1)}, u32[]{:S(2)}, u32[]{:S(2)}) collective-permute-start(bf16[80,1024]{1,0:T(8,128)(2,1)S(1)} %get-tuple-element.26), channel_id=1, source_target_pairs={{0,8},{4,12},{8,0},{12,4},{1,9},{5,13},{9,1},{13,5},{2,10},{6,14},... | collective-permute-start | bytes 491528 | tf_op jit(solution)/shard_map/ppermute | solution.py:202
  8.6 1.5 %collective-permute-start.3 = (bf16[80,1024]{1,0:T(8,128)(2,1)S(1)}, bf16[80,1024]{1,0:T(8,128)(2,1)S(1)}, u32[]{:S(2)}, u32[]{:S(2)}) collective-permute-start(bf16[80,1024]{1,0:T(8,128)(2,1)S(1)} %get-tuple-element.23.refs_0_), channel_id=1, source_target_pairs={{0,2},{2,0},{1,3},{3,1},{4,6},{6,4},{5,7},{7,5},{8,10},{10,8},{9,1... | collective-permute-start | bytes 491528 | tf_op jit(solution)/shard_map/ppermute | solution.py:163
  10.1 3.4 %collective-permute-done.5.refs_4_ = bf16[80,1024]{1,0:T(8,128)(2,1)S(1)} collective-permute-done((bf16[80,1024]{1,0:T(8,128)(2,1)S(1)}, bf16[80,1024]{1,0:T(8,128)(2,1)S(1)}, u32[]{:S(2)}, u32[]{:S(2)}) %collective-permute-start.5) | collective-permute-done | bytes 163872 | tf_op jit(solution)/shard_map/ppermute | solution.py:202
  13.5 1.8 %collective-permute-start.9 = (bf16[80,1024]{1,0:T(8,128)(2,1)S(1)}, bf16[80,1024]{1,0:T(8,128)(2,1)S(1)}, u32[]{:S(2)}, u32[]{:S(2)}) collective-permute-start(bf16[80,1024]{1,0:T(8,128)(2,1)S(1)} %collective-permute-done.5.refs_4_), channel_id=1, source_target_pairs={{0,2},{2,0},{1,3},{3,1},{4,6},{6,4},{5,7},{7,5},{8,10},{10,8},{9,1... | collective-permute-start | bytes 491528 | tf_op jit(solution)/shard_map/ppermute | solution.py:163
  15.3 2.5 %collective-permute-start.7 = (bf16[80,1024]{1,0:T(8,128)(2,1)S(1)}, bf16[80,1024]{1,0:T(8,128)(2,1)S(1)}, u32[]{:S(2)}, u32[]{:S(2)}) collective-permute-start(bf16[80,1024]{1,0:T(8,128)(2,1)S(1)} %get-tuple-element.25), channel_id=1, source_target_pairs={{0,12},{4,8},{8,4},{12,0},{1,13},{5,9},{9,5},{13,1},{2,14},{6,10},... | collective-permute-start | bytes 491528 | tf_op jit(solution)/shard_map/ppermute | solution.py:202
  18.8 3.7 %collective-permute-done.7.refs_12_ = bf16[80,1024]{1,0:T(8,128)(2,1)S(1)} collective-permute-done((bf16[80,1024]{1,0:T(8,128)(2,1)S(1)}, bf16[80,1024]{1,0:T(8,128)(2,1)S(1)}, u32[]{:S(2)}, u32[]{:S(2)}) %collective-permute-start.7) | collective-permute-done | bytes 163872 | tf_op jit(solution)/shard_map/ppermute | solution.py:202
  22.7 1.8 %collective-permute-start.12 = (bf16[80,1024]{1,0:T(8,128)(2,1)S(1)}, bf16[80,1024]{1,0:T(8,128)(2,1)S(1)}, u32[]{:S(2)}, u32[]{:S(2)}) collective-permute-start(bf16[80,1024]{1,0:T(8,128)(2,1)S(1)} %collective-permute-done.8.refs_8_), channel_id=1, source_target_pairs={{0,2},{2,0},{1,3},{3,1},{4,6},{6,4},{5,7},{7,5},{8,10},{10,8},{9,1... | collective-permute-start | bytes 491528 | tf_op jit(solution)/shard_map/ppermute | solution.py:163
  25.1 2.7 %collective-permute-done.15.refs_14_ = bf16[80,1024]{1,0:T(8,128)(2,1)S(1)} collective-permute-done((bf16[80,1024]{1,0:T(8,128)(2,1)S(1)}, bf16[80,1024]{1,0:T(8,128)(2,1)S(1)}, u32[]{:S(2)}, u32[]{:S(2)}) %collective-permute-start.15) | collective-permute-done | bytes 163872 | tf_op jit(solution)/shard_map/ppermute | solution.py:163
  27.9 1.8 %collective-permute-done.12.refs_10_ = bf16[80,1024]{1,0:T(8,128)(2,1)S(1)} collective-permute-done((bf16[80,1024]{1,0:T(8,128)(2,1)S(1)}, bf16[80,1024]{1,0:T(8,128)(2,1)S(1)}, u32[]{:S(2)}, u32[]{:S(2)}) %collective-permute-start.12) | collective-permute-done | bytes 163872 | tf_op jit(solution)/shard_map/ppermute | solution.py:163
  29.6 1.4 %collective-permute-done.13.refs_11_ = bf16[80,1024]{1,0:T(8,128)(2,1)S(1)} collective-permute-done((bf16[80,1024]{1,0:T(8,128)(2,1)S(1)}, bf16[80,1024]{1,0:T(8,128)(2,1)S(1)}, u32[]{:S(2)}, u32[]{:S(2)}) %collective-permute-start.13) | collective-permute-done | bytes 163872 | tf_op jit(solution)/shard_map/ppermute | solution.py:163
  31.0 6.9 %hidden.1.own = bf16[320,384]{1,0:T(8,128)(2,1)S(1)} custom-call(s32[3]{0:T(128)S(1)} %pad_add_fusion.pos_ref, bf16[80,1024]{1,0:T(8,128)(2,1)S(1)} %get-tuple-element.23.refs_0_, bf16[80,1024]{1,0:T(8,128)(2,1)S(1)} %collective-permute-done.2.refs_1_, bf16[80,1024]{1,0:T(8,128)(2,1)S(1)} %collective-permute-done.3.refs_2_, ...), custom_call_target="tpu_custom_call" | custom-call | tf_op jit(solution)/shard_map/hidden/pallas_call | solution.py:217
  38.3 7.7 %collective-permute-done.17.x = bf16[320,384]{1,0:T(8,128)(2,1)S(1)} collective-permute-done((bf16[320,384]{1,0:T(8,128)(2,1)S(1)}, bf16[320,384]{1,0:T(8,128)(2,1)S(1)}, u32[]{:S(2)}, u32[]{:S(2)}) %collective-permute-start.17) | collective-permute-done | bytes 245792 | tf_op jit(solution)/shard_map/ppermute | solution.py:163
  46.0 1.5 %collective-permute-done.19.xcore = bf16[320,384]{1,0:T(8,128)(2,1)S(1)} collective-permute-done((bf16[320,384]{1,0:T(8,128)(2,1)S(1)}, bf16[320,384]{1,0:T(8,128)(2,1)S(1)}, u32[]{:S(2)}, u32[]{:S(2)}) %collective-permute-start.19) | collective-permute-done | bytes 245792 | tf_op jit(solution)/shard_map/ppermute | solution.py:163
  47.5 4.0 %down.2 = (bf16[80,512]{1,0:T(8,128)(2,1)S(1)}, bf16[80,512]{1,0:T(8,128)(2,1)S(1)}, bf16[80,512]{1,0:T(8,128)(2,1)S(1)}, bf16[80,512]{1,0:T(8,128)(2,1)S(1)}, b...) custom-call(s32[3]{0:T(128)S(1)} %pad_add_fusion.pos_ref, ...), custom_call_target="tpu_custom_call" | custom-call | tf_op jit(solution)/shard_map/down/pallas_call | solution.py:223
  51.9 4.5 %collective-permute-start.21 = (bf16[80,512]{1,0:T(8,128)(2,1)S(1)}, bf16[80,512]{1,0:T(8,128)(2,1)S(1)}, u32[]{:S(2)}, u32[]{:S(2)}) collective-permute-start(bf16[80,512]{1,0:T(8,128)(2,1)S(1)} %get-tuple-element.33), channel_id=1, source_target_pairs={{0,4},{2,6},{4,0},{6,2},{8,12},{10,14},{12,8},{14,10},{1,5},{3,7},... | collective-permute-start | bytes 245768 | tf_op jit(solution)/shard_map/ppermute | solution.py:232
  57.5 1.6 %collective-permute-start.23 = (bf16[80,512]{1,0:T(8,128)(2,1)S(1)}, bf16[80,512]{1,0:T(8,128)(2,1)S(1)}, u32[]{:S(2)}, u32[]{:S(2)}) collective-permute-start(bf16[80,512]{1,0:T(8,128)(2,1)S(1)} %get-tuple-element.35), channel_id=1, source_target_pairs={{0,8},{2,10},{4,12},{6,14},{8,0},{10,2},{12,4},{14,6},{1,9},{3,11}... | collective-permute-start | bytes 245768 | tf_op jit(solution)/shard_map/ppermute | solution.py:232
  59.1 1.7 %collective-permute-start.24 = (bf16[80,512]{1,0:T(8,128)(2,1)S(1)}, bf16[80,512]{1,0:T(8,128)(2,1)S(1)}, u32[]{:S(2)}, u32[]{:S(2)}) collective-permute-start(bf16[80,512]{1,0:T(8,128)(2,1)S(1)} %get-tuple-element.36), channel_id=1, source_target_pairs={{0,10},{2,8},{4,14},{6,12},{8,2},{10,0},{12,6},{14,4},{1,11},{3,9}... | collective-permute-start | bytes 245768 | tf_op jit(solution)/shard_map/ppermute | solution.py:232
  60.7 1.9 %collective-permute-start.25 = (bf16[80,512]{1,0:T(8,128)(2,1)S(1)}, bf16[80,512]{1,0:T(8,128)(2,1)S(1)}, u32[]{:S(2)}, u32[]{:S(2)}) collective-permute-start(bf16[80,512]{1,0:T(8,128)(2,1)S(1)} %get-tuple-element.37), channel_id=1, source_target_pairs={{0,12},{2,14},{4,8},{6,10},{8,4},{10,6},{12,0},{14,2},{1,13},{3,15... | collective-permute-start | bytes 245768 | tf_op jit(solution)/shard_map/ppermute | solution.py:232
  62.6 2.6 %collective-permute-start.26 = (bf16[80,512]{1,0:T(8,128)(2,1)S(1)}, bf16[80,512]{1,0:T(8,128)(2,1)S(1)}, u32[]{:S(2)}, u32[]{:S(2)}) collective-permute-start(bf16[80,512]{1,0:T(8,128)(2,1)S(1)} %get-tuple-element.38), channel_id=1, source_target_pairs={{0,14},{2,12},{4,10},{6,8},{8,6},{10,4},{12,2},{14,0},{1,15},{3,13... | collective-permute-start | bytes 245768 | tf_op jit(solution)/shard_map/ppermute | solution.py:232
  65.2 5.2 %collective-permute-done.23.refs_4_ = bf16[80,512]{1,0:T(8,128)(2,1)S(1)} collective-permute-done((bf16[80,512]{1,0:T(8,128)(2,1)S(1)}, bf16[80,512]{1,0:T(8,128)(2,1)S(1)}, u32[]{:S(2)}, u32[]{:S(2)}) %collective-permute-start.23) | collective-permute-done | bytes 81952 | tf_op jit(solution)/shard_map/ppermute | solution.py:232
  70.4 2.1 %collective-permute-done.24.refs_5_ = bf16[80,512]{1,0:T(8,128)(2,1)S(1)} collective-permute-done((bf16[80,512]{1,0:T(8,128)(2,1)S(1)}, bf16[80,512]{1,0:T(8,128)(2,1)S(1)}, u32[]{:S(2)}, u32[]{:S(2)}) %collective-permute-start.24) | collective-permute-done | bytes 81952 | tf_op jit(solution)/shard_map/ppermute | solution.py:232
  73.7 1.5 %collective-permute-done.27.other = bf16[64,2048]{1,0:T(8,128)(2,1)S(1)} collective-permute-done((bf16[64,2048]{1,0:T(8,128)(2,1)S(1)}, bf16[64,2048]{1,0:T(8,128)(2,1)S(1)}, u32[]{:S(2)}, u32[]{:S(2)}) %collective-permute-start.27) | collective-permute-done | bytes 262176 | tf_op jit(solution)/shard_map/ppermute | solution.py:163
  75.3 1.4 %join.1 = bf16[64,4096]{1,0:T(8,128)(2,1)} custom-call(s32[3]{0:T(128)S(1)} %pad_add_fusion.pos_ref, bf16[64,2048]{1,0:T(8,128)(2,1)S(1)} %get-tuple-element.39.mine, bf16[64,2048]{1,0:T(8,128)(2,1)S(1)} %collective-permute-done.27.other), custom_call_target="tpu_custom_call" | custom-call | tf_op jit(solution)/shard_map/join/pallas_call | solution.py:238
  (55 shorter events, 7.9 us)
Async XLA Ops:
  3.0 10.5 %collective-permute-start.5 = (bf16[80,1024]{1,0:T(8,128)(2,1)S(1)}, bf16[80,1024]{1,0:T(8,128)(2,1)S(1)}, u32[]{:S(2)}, u32[]{:S(2)}) collective-permute-start(bf16[80,1024]{1,0:T(8,128)(2,1)S(1)} %get-tuple-element.24), channel_id=1, source_target_pairs={{0,4},{4,0},{8,12},{12,8},{1,5},{5,1},{9,13},{13,9},{2,6},{6,2},{1... | collective-permute-start | bytes 491528 | tf_op jit(solution)/shard_map/ppermute | solution.py:202
  6.1 11.7 %collective-permute-start.8 = (bf16[80,1024]{1,0:T(8,128)(2,1)S(1)}, bf16[80,1024]{1,0:T(8,128)(2,1)S(1)}, u32[]{:S(2)}, u32[]{:S(2)}) collective-permute-start(bf16[80,1024]{1,0:T(8,128)(2,1)S(1)} %get-tuple-element.26), channel_id=1, source_target_pairs={{0,8},{4,12},{8,0},{12,4},{1,9},{5,13},{9,1},{13,5},{2,10},{6,14},... | collective-permute-start | bytes 491528 | tf_op jit(solution)/shard_map/ppermute | solution.py:202
  8.6 9.7 %collective-permute-start.3 = (bf16[80,1024]{1,0:T(8,128)(2,1)S(1)}, bf16[80,1024]{1,0:T(8,128)(2,1)S(1)}, u32[]{:S(2)}, u32[]{:S(2)}) collective-permute-start(bf16[80,1024]{1,0:T(8,128)(2,1)S(1)} %get-tuple-element.23.refs_0_), channel_id=1, source_target_pairs={{0,2},{2,0},{1,3},{3,1},{4,6},{6,4},{5,7},{7,5},{8,10},{10,8},{9,1... | collective-permute-start | bytes 491528 | tf_op jit(solution)/shard_map/ppermute | solution.py:163
  13.5 5.3 %collective-permute-start.9 = (bf16[80,1024]{1,0:T(8,128)(2,1)S(1)}, bf16[80,1024]{1,0:T(8,128)(2,1)S(1)}, u32[]{:S(2)}, u32[]{:S(2)}) collective-permute-start(bf16[80,1024]{1,0:T(8,128)(2,1)S(1)} %collective-permute-done.5.refs_4_), channel_id=1, source_target_pairs={{0,2},{2,0},{1,3},{3,1},{4,6},{6,4},{5,7},{7,5},{8,10},{10,8},{9,1... | collective-permute-start | bytes 491528 | tf_op jit(solution)/shard_map/ppermute | solution.py:163
  15.3 7.2 %collective-permute-start.7 = (bf16[80,1024]{1,0:T(8,128)(2,1)S(1)}, bf16[80,1024]{1,0:T(8,128)(2,1)S(1)}, u32[]{:S(2)}, u32[]{:S(2)}) collective-permute-start(bf16[80,1024]{1,0:T(8,128)(2,1)S(1)} %get-tuple-element.25), channel_id=1, source_target_pairs={{0,12},{4,8},{8,4},{12,0},{1,13},{5,9},{9,5},{13,1},{2,14},{6,10},... | collective-permute-start | bytes 491528 | tf_op jit(solution)/shard_map/ppermute | solution.py:202
  17.8 6.8 %collective-permute-start.2 = (bf16[80,1024]{1,0:T(8,128)(2,1)S(1)}, bf16[80,1024]{1,0:T(8,128)(2,1)S(1)}, u32[]{:S(2)}, u32[]{:S(2)}) collective-permute-start(bf16[80,1024]{1,0:T(8,128)(2,1)S(1)} %get-tuple-element.23.refs_0_), channel_id=1, source_target_pairs={{0,1},{1,0},{2,3},{3,2},{4,5},{5,4},{6,7},{7,6},{8,9},{9,8},{10,11... | collective-permute-start | bytes 491528 | tf_op jit(solution)/shard_map/ppermute | solution.py:163
  17.8 7.3 %collective-permute-start.6 = (bf16[80,1024]{1,0:T(8,128)(2,1)S(1)}, bf16[80,1024]{1,0:T(8,128)(2,1)S(1)}, u32[]{:S(2)}, u32[]{:S(2)}) collective-permute-start(bf16[80,1024]{1,0:T(8,128)(2,1)S(1)} %collective-permute-done.5.refs_4_), channel_id=1, source_target_pairs={{0,1},{1,0},{2,3},{3,2},{4,5},{5,4},{6,7},{7,6},{8,9},{9,8},{10,11... | collective-permute-start | bytes 491528 | tf_op jit(solution)/shard_map/ppermute | solution.py:163
  18.3 6.3 %collective-permute-start.4 = (bf16[80,1024]{1,0:T(8,128)(2,1)S(1)}, bf16[80,1024]{1,0:T(8,128)(2,1)S(1)}, u32[]{:S(2)}, u32[]{:S(2)}) collective-permute-start(bf16[80,1024]{1,0:T(8,128)(2,1)S(1)} %collective-permute-done.3.refs_2_), channel_id=1, source_target_pairs={{0,1},{1,0},{2,3},{3,2},{4,5},{5,4},{6,7},{7,6},{8,9},{9,8},{10,11... | collective-permute-start | bytes 491528 | tf_op jit(solution)/shard_map/ppermute | solution.py:163
  22.5 5.3 %collective-permute-start.15 = (bf16[80,1024]{1,0:T(8,128)(2,1)S(1)}, bf16[80,1024]{1,0:T(8,128)(2,1)S(1)}, u32[]{:S(2)}, u32[]{:S(2)}) collective-permute-start(bf16[80,1024]{1,0:T(8,128)(2,1)S(1)} %collective-permute-done.7.refs_12_), channel_id=1, source_target_pairs={{0,2},{2,0},{1,3},{3,1},{4,6},{6,4},{5,7},{7,5},{8,10},{10,8},{9,1... | collective-permute-start | bytes 491528 | tf_op jit(solution)/shard_map/ppermute | solution.py:163
  22.7 6.9 %collective-permute-start.12 = (bf16[80,1024]{1,0:T(8,128)(2,1)S(1)}, bf16[80,1024]{1,0:T(8,128)(2,1)S(1)}, u32[]{:S(2)}, u32[]{:S(2)}) collective-permute-start(bf16[80,1024]{1,0:T(8,128)(2,1)S(1)} %collective-permute-done.8.refs_8_), channel_id=1, source_target_pairs={{0,2},{2,0},{1,3},{3,1},{4,6},{6,4},{5,7},{7,5},{8,10},{10,8},{9,1... | collective-permute-start | bytes 491528 | tf_op jit(solution)/shard_map/ppermute | solution.py:163
  24.6 5.1 %collective-permute-start.14 = (bf16[80,1024]{1,0:T(8,128)(2,1)S(1)}, bf16[80,1024]{1,0:T(8,128)(2,1)S(1)}, u32[]{:S(2)}, u32[]{:S(2)}) collective-permute-start(bf16[80,1024]{1,0:T(8,128)(2,1)S(1)} %collective-permute-done.7.refs_12_), channel_id=1, source_target_pairs={{0,1},{1,0},{2,3},{3,2},{4,5},{5,4},{6,7},{7,6},{8,9},{9,8},{10,11... | collective-permute-start | bytes 491528 | tf_op jit(solution)/shard_map/ppermute | solution.py:163
  24.6 5.1 %collective-permute-start.11 = (bf16[80,1024]{1,0:T(8,128)(2,1)S(1)}, bf16[80,1024]{1,0:T(8,128)(2,1)S(1)}, u32[]{:S(2)}, u32[]{:S(2)}) collective-permute-start(bf16[80,1024]{1,0:T(8,128)(2,1)S(1)} %collective-permute-done.8.refs_8_), channel_id=1, source_target_pairs={{0,1},{1,0},{2,3},{3,2},{4,5},{5,4},{6,7},{7,6},{8,9},{9,8},{10,11... | collective-permute-start | bytes 491528 | tf_op jit(solution)/shard_map/ppermute | solution.py:163
  25.1 4.5 %collective-permute-start.10 = (bf16[80,1024]{1,0:T(8,128)(2,1)S(1)}, bf16[80,1024]{1,0:T(8,128)(2,1)S(1)}, u32[]{:S(2)}, u32[]{:S(2)}) collective-permute-start(bf16[80,1024]{1,0:T(8,128)(2,1)S(1)} %collective-permute-done.9.refs_6_), channel_id=1, source_target_pairs={{0,1},{1,0},{2,3},{3,2},{4,5},{5,4},{6,7},{7,6},{8,9},{9,8},{10,11... | collective-permute-start | bytes 491528 | tf_op jit(solution)/shard_map/ppermute | solution.py:163
  27.9 1.8 %collective-permute-start.16 = (bf16[80,1024]{1,0:T(8,128)(2,1)S(1)}, bf16[80,1024]{1,0:T(8,128)(2,1)S(1)}, u32[]{:S(2)}, u32[]{:S(2)}) collective-permute-start(bf16[80,1024]{1,0:T(8,128)(2,1)S(1)} %collective-permute-done.15.refs_14_), channel_id=1, source_target_pairs={{0,1},{1,0},{2,3},{3,2},{4,5},{5,4},{6,7},{7,6},{8,9},{9,8},{10,11... | collective-permute-start | bytes 491528 | tf_op jit(solution)/shard_map/ppermute | solution.py:163
  38.0 8.1 %collective-permute-start.17 = (bf16[320,384]{1,0:T(8,128)(2,1)S(1)}, bf16[320,384]{1,0:T(8,128)(2,1)S(1)}, u32[]{:S(2)}, u32[]{:S(2)}) collective-permute-start(bf16[320,384]{1,0:T(8,128)(2,1)S(1)} %hidden.1.own), channel_id=1, source_target_pairs={{0,2},{2,0},{1,3},{3,1},{4,6},{6,4},{5,7},{7,5},{8,10},{10,8},{9,1... | collective-permute-start | bytes 737288 | tf_op jit(solution)/shard_map/ppermute | solution.py:163
  38.3 7.7 %collective-permute-start.18 = (bf16[320,384]{1,0:T(8,128)(2,1)S(1)}, bf16[320,384]{1,0:T(8,128)(2,1)S(1)}, u32[]{:S(2)}, u32[]{:S(2)}) collective-permute-start(bf16[320,384]{1,0:T(8,128)(2,1)S(1)} %hidden.1.own), channel_id=1, source_target_pairs={{0,1},{1,0},{2,3},{3,2},{4,5},{5,4},{6,7},{7,6},{8,9},{9,8},{10,11... | collective-permute-start | bytes 737288 | tf_op jit(solution)/shard_map/ppermute | solution.py:163
  51.5 9.2 %collective-permute-start.20 = (bf16[80,512]{1,0:T(8,128)(2,1)S(1)}, bf16[80,512]{1,0:T(8,128)(2,1)S(1)}, u32[]{:S(2)}, u32[]{:S(2)}) collective-permute-start(bf16[80,512]{1,0:T(8,128)(2,1)S(1)} %get-tuple-element.32), channel_id=1, source_target_pairs={{0,2},{2,0},{4,6},{6,4},{8,10},{10,8},{12,14},{14,12},{1,3},{3,1},... | collective-permute-start | bytes 245768 | tf_op jit(solution)/shard_map/ppermute | solution.py:232
  51.9 10.7 %collective-permute-start.21 = (bf16[80,512]{1,0:T(8,128)(2,1)S(1)}, bf16[80,512]{1,0:T(8,128)(2,1)S(1)}, u32[]{:S(2)}, u32[]{:S(2)}) collective-permute-start(bf16[80,512]{1,0:T(8,128)(2,1)S(1)} %get-tuple-element.33), channel_id=1, source_target_pairs={{0,4},{2,6},{4,0},{6,2},{8,12},{10,14},{12,8},{14,10},{1,5},{3,7},... | collective-permute-start | bytes 245768 | tf_op jit(solution)/shard_map/ppermute | solution.py:232
  56.4 2.7 %collective-permute-start.1 = (f32[1,64]{1,0:T(1,128)S(1)}, f32[1,64]{1,0:T(1,128)S(1)}, u32[]{:S(2)}, u32[]{:S(2)}) collective-permute-start(f32[1,64]{1,0:T(1,128)S(1)} %bitcast.10), channel_id=1, source_target_pairs={{0,1},{1,0},{2,3},{3,2},{4,5},{5,4},{6,7},{7,6},{8,9},{9,8},{10,11... | collective-permute-start | bytes 776 | tf_op jit(solution)/shard_map/ppermute | solution.py:163
  56.9 8.3 %collective-permute-start.22 = (bf16[80,512]{1,0:T(8,128)(2,1)S(1)}, bf16[80,512]{1,0:T(8,128)(2,1)S(1)}, u32[]{:S(2)}, u32[]{:S(2)}) collective-permute-start(bf16[80,512]{1,0:T(8,128)(2,1)S(1)} %get-tuple-element.34), channel_id=1, source_target_pairs={{0,6},{2,4},{4,2},{6,0},{8,14},{10,12},{12,10},{14,8},{1,7},{3,5},... | collective-permute-start | bytes 245768 | tf_op jit(solution)/shard_map/ppermute | solution.py:232
  57.5 12.9 %collective-permute-start.23 = (bf16[80,512]{1,0:T(8,128)(2,1)S(1)}, bf16[80,512]{1,0:T(8,128)(2,1)S(1)}, u32[]{:S(2)}, u32[]{:S(2)}) collective-permute-start(bf16[80,512]{1,0:T(8,128)(2,1)S(1)} %get-tuple-element.35), channel_id=1, source_target_pairs={{0,8},{2,10},{4,12},{6,14},{8,0},{10,2},{12,4},{14,6},{1,9},{3,11}... | collective-permute-start | bytes 245768 | tf_op jit(solution)/shard_map/ppermute | solution.py:232
  59.1 13.4 %collective-permute-start.24 = (bf16[80,512]{1,0:T(8,128)(2,1)S(1)}, bf16[80,512]{1,0:T(8,128)(2,1)S(1)}, u32[]{:S(2)}, u32[]{:S(2)}) collective-permute-start(bf16[80,512]{1,0:T(8,128)(2,1)S(1)} %get-tuple-element.36), channel_id=1, source_target_pairs={{0,10},{2,8},{4,14},{6,12},{8,2},{10,0},{12,6},{14,4},{1,11},{3,9}... | collective-permute-start | bytes 245768 | tf_op jit(solution)/shard_map/ppermute | solution.py:232
  60.7 11.8 %collective-permute-start.25 = (bf16[80,512]{1,0:T(8,128)(2,1)S(1)}, bf16[80,512]{1,0:T(8,128)(2,1)S(1)}, u32[]{:S(2)}, u32[]{:S(2)}) collective-permute-start(bf16[80,512]{1,0:T(8,128)(2,1)S(1)} %get-tuple-element.37), channel_id=1, source_target_pairs={{0,12},{2,14},{4,8},{6,10},{8,4},{10,6},{12,0},{14,2},{1,13},{3,15... | collective-permute-start | bytes 245768 | tf_op jit(solution)/shard_map/ppermute | solution.py:232
  62.6 9.9 %collective-permute-start.26 = (bf16[80,512]{1,0:T(8,128)(2,1)S(1)}, bf16[80,512]{1,0:T(8,128)(2,1)S(1)}, u32[]{:S(2)}, u32[]{:S(2)}) collective-permute-start(bf16[80,512]{1,0:T(8,128)(2,1)S(1)} %get-tuple-element.38), channel_id=1, source_target_pairs={{0,14},{2,12},{4,10},{6,8},{8,6},{10,4},{12,2},{14,0},{1,15},{3,13... | collective-permute-start | bytes 245768 | tf_op jit(solution)/shard_map/ppermute | solution.py:232
  (12 other events, 180.9 us)

commit v3 on v2

v3 whole, which is shorter than its diff:
```python
import functools
import jax
import jax.numpy as jnp
from jax import lax
from jax.experimental import pallas as pl
from jax.experimental.pallas import tpu as pltpu
from jax.sharding import PartitionSpec as P

BIG = 4096
ORDER = (0, 3, 2, 1, 5, 4, 7, 6)
LEAD = 20 * 10**9
STEP = 10 * 10**9
VMEM_LIMIT = 8 * 1024 * 1024
F32, BF16, I32 = jnp.float32, jnp.bfloat16, jnp.int32


def div(x, by):
    return ((x.astype(F32) + 0.5) * (1.0 / by)).astype(I32)


def onehot(cond):
    return jnp.where(cond, 1.0, 0.0).astype(BF16)


def dot(a, b):
    return jnp.dot(a, b, preferred_element_type=F32)


def iota(shape, dim):
    return lax.broadcasted_iota(I32, shape, dim)


def as_column(row):
    n = row.shape[1]
    square = jnp.broadcast_to(row, (n, n))
    return jnp.sum(jnp.where(iota((n, n), 0) == iota((n, n), 1), square, jnp.zeros((), row.dtype)), axis=1, keepdims=True)


def slot_keys(ids_row, cap):
    n = ids_row.shape[1]
    ids_col = as_column(ids_row)
    earlier = (ids_col == ids_row) & (iota((n, n), 0) < iota((n, n), 1))
    rank = jnp.sum(jnp.where(earlier, 1, 0), axis=0, keepdims=True)
    return ids_row * cap + rank


def dispatch_kernel(cfg, pos_ref, ids_ref, route_ref, tok_ref, *outs):
    z = pos_ref[0]
    keys = slot_keys(ids_ref[...], cfg.cap)
    outs[-1][0:1] = keys.astype(F32)
    outs[-1][1:2] = route_ref[...]
    keys = jnp.concatenate([keys + j * BIG for j in range(cfg.nd)], axis=1)
    stacked = jnp.concatenate([tok_ref[:, j * cfg.w:(j + 1) * cfg.w] for j in range(cfg.nd)], axis=0)
    i = iota((cfg.rp, 1), 0)
    j = div(i, cfg.rows)
    target = i - j * cfg.rows + j * BIG
    for r in range(cfg.groups):
        base = jnp.bitwise_xor(z, r) * cfg.local * cfg.cap
        outs[r][...] = dot(onehot(keys - base == target), stacked).astype(BF16)


def place(cfg, srcs, store):
    i, c = iota((cfg.nd * cfg.ne * 16, 1), 0), iota((1, 2 * cfg.rp), 1)
    slot = i & 7
    want = ((i >> 3) & 1) * cfg.rp + (i >> 4) * cfg.cap + slot
    spread = onehot((want == c) & (slot < cfg.cap))
    for k in range(len(srcs) // 2):
        pair = jnp.concatenate([srcs[2 * k][...], srcs[2 * k + 1][...]], axis=0)
        spaced = dot(spread, pair).astype(BF16)
        for j in range(cfg.nd):
            for e in range(cfg.ne):
                at = (j * cfg.ne + e) * 16
                store(e, k, j, spaced[at:at + 16])


def near_kernel(cfg, pos_ref, *refs):
    rows = refs[-1]

    def store(e, k, j, v):
        rows[e, k * 16:(k + 1) * 16, j * cfg.w:(j + 1) * cfg.w] = v

    place(cfg, refs[:cfg.early * 4], store)


def hidden_rows(cfg, pos_ref, near, far, gate, up, out_ref, first):
    per = cfg.sources * cfg.cap
    i = iota((per, 1), 0)
    s = div(i, cfg.cap)
    slot = i - s * cfg.cap
    rel = jnp.bitwise_xor(s, pos_ref[1] * 2 + pos_ref[2])
    compact = onehot(iota((1, cfg.sources * 8), 1) == rel * 8 + slot)
    for k in range(cfg.ne // 2):
        e = first + k
        x = jnp.concatenate([near[e], far[k]], axis=0)
        both = dot(x, jnp.concatenate([gate[e], up[e]], axis=1))
        g, u = jnp.split(both, 2, axis=1)
        hid = (g / (1.0 + jnp.exp(-g)) * u).astype(BF16)
        out_ref[k * per:(k + 1) * per] = dot(compact, hid).astype(BF16)


def hidden_first_kernel(cfg, pos_ref, *refs):
    late = cfg.sources - cfg.early * 4
    near, gate, up, out_ref, later, now = refs[late:]

    def store(e, k, j, v):
        ref = now if e < cfg.ne // 2 else later
        ref[e % (cfg.ne // 2), k * 16:(k + 1) * 16, j * cfg.w:(j + 1) * cfg.w] = v

    place(cfg, refs[:late], store)
    hidden_rows(cfg, pos_ref, near, now, gate, up, out_ref, 0)


def hidden_second_kernel(cfg, pos_ref, near, far, gate, up, out_ref):
    hidden_rows(cfg, pos_ref, near, far, gate, up, out_ref, cfg.ne // 2)


def down_rows(cfg, pos_ref, parts, down, full, out, first):
    c, t = pos_ref[1], pos_ref[2]
    f = parts[0].shape[1]
    for ref, dc, dt in zip(parts, (0, 1, 0, 1), (0, 0, 1, 1)):
        at = (jnp.bitwise_xor(c, dc) * 2 + jnp.bitwise_xor(t, dt)) * f
        full[:, pl.ds(pl.multiple_of(at, 128), f)] = ref[...]
    per = cfg.sources * cfg.cap
    for k in range(cfg.ne // 2):
        out[k * per:(k + 1) * per] = dot(full[k * per:(k + 1) * per], down[first + k]).astype(BF16)


def sort_rows(cfg, pos_ref, halves, outs):
    per = cfg.sources * cfg.cap
    width = halves[0].shape[1] // 2
    stacked = jnp.concatenate([v[:, q * width:(q + 1) * width] for q in range(2) for v in halves], axis=0)
    m = iota((4 * cfg.rows, 1), 0)
    qt = div(m, cfg.rows)
    p = m - qt * cfg.rows
    e = div(p, cfg.cap)
    slot = p - e * cfg.cap
    want = (qt >> 1) * (cfg.ne * per) + e * per + (qt & 1) * cfg.cap + slot
    lane = iota((1, 2 * cfg.ne * per), 1)
    for k, out in enumerate(outs):
        r, dc = divmod(k, 2)
        place_at = (r * 2 + jnp.bitwise_xor(pos_ref[1], dc)) * 2 * cfg.cap
        out[...] = dot(onehot(lane - place_at == want), stacked).astype(BF16)


def down_first_kernel(cfg, pos_ref, own, x, core, xcore, down, out, full):
    down_rows(cfg, pos_ref, (own, x, core, xcore), down, full, out, 0)


def down_second_kernel(cfg, pos_ref, own, x, core, xcore, down, before, *refs):
    outs, full, out = refs[:-2], refs[-2], refs[-1]
    down_rows(cfg, pos_ref, (own, x, core, xcore), down, full, out, cfg.ne // 2)
    sort_rows(cfg, pos_ref, (before, out), outs)


def combine_kernel(cfg, pos_ref, info_own, info_peer, *refs):
    msgs, (mine, other) = refs[:-2], refs[-2:]
    z, c, t = pos_ref[0], pos_ref[1], pos_ref[2]
    block = 4 * cfg.rows
    lanes = iota((1, cfg.groups * block), 1)
    r = div(lanes, block)
    m = lanes - r * block
    qt = div(m, cfg.rows)
    code = jnp.bitwise_xor(r, z) * cfg.local * cfg.cap + m - qt * cfg.rows + qt * BIG
    picks, weights = [], []
    for rel, info in enumerate((info_own, info_peer)):
        key = as_column(info[0:1]).astype(I32)
        weights.append(as_column(info[1:2]))
        picks += [onehot(key + (q * 2 + jnp.bitwise_xor(t, rel)) * BIG == code) for q in range(2)]
    picks = jnp.concatenate(picks, axis=0)
    n = info_own.shape[1]
    for dc in range(2):
        stacked = jnp.concatenate([msgs[k * 2 + dc][...] for k in range(cfg.groups)], axis=0)
        got = dot(picks, stacked)
        width = got.shape[1]
        at = jnp.bitwise_xor(c, dc) * (2 * width)
        for rel, out in enumerate((mine, other)):
            for q in range(2):
                k = rel * 2 + q
                out[:, pl.ds(pl.multiple_of(at + q * width, 128), width)] = (weights[rel] * got[k * n:(k + 1) * n]).astype(BF16)


def join_kernel(cfg, pos_ref, mine, other, out):
    t = pos_ref[2]
    width = mine.shape[1] // 2
    for cc in range(2):
        for ref, dt in ((mine, 0), (other, 1)):
            at = cc * 2 * width + jnp.bitwise_xor(t, dt) * width
            out[:, pl.ds(pl.multiple_of(at, 128), width)] = ref[:, cc * width:(cc + 1) * width]


class Sizes:
    pass


def swap(x, axis):
    return lax.ppermute(x, axis, [(0, 1), (1, 0)])


def on_device(tokens, expert_ids, route_weights, gate_weight, up_weight, down_weight):
    cfg = Sizes()
    n, width = tokens.shape
    cfg.groups = lax.axis_size("expert")
    cfg.local = gate_weight.shape[0]
    experts = cfg.groups * cfg.local
    cfg.cap = max(2, n * 5 // (4 * experts))
    cfg.ne = cfg.local
    cfg.rows = cfg.ne * cfg.cap
    cfg.nd = 16 // cfg.ne
    cfg.w = width // cfg.nd
    cfg.rp = cfg.rows * cfg.nd
    cfg.sources = cfg.groups * 4
    cfg.early = cfg.groups - 1
    f = gate_weight.shape[2]
    ff, wide = down_weight.shape[1:]
    per = cfg.sources * cfg.cap

    z, c, t = (lax.axis_index(a) for a in ("expert", "context", "tensor"))
    pos = jnp.stack([z, c, t]).astype(I32)
    ids = expert_ids.reshape(1, n)
    route = route_weights.reshape(1, n)
    smem = pl.BlockSpec(memory_space=pltpu.SMEM)
    vmem = pl.BlockSpec(memory_space=pltpu.VMEM)
    params = pltpu.CompilerParams(vmem_limit_bytes=VMEM_LIMIT)
    shape = jax.ShapeDtypeStruct

    def call(kernel, name, ins, outs, scratch=(), work=10**9):
        args = [pos] + list(ins)
        return list(pl.pallas_call(
            kernel, in_specs=[smem] + [vmem] * len(ins), out_specs=[vmem] * len(outs),
            out_shape=[o if isinstance(o, shape) else shape(o, BF16) for o in outs], scratch_shapes=scratch, compiler_params=params, name=name,
            cost_estimate=pl.CostEstimate(flops=work, bytes_accessed=0, transcendentals=0))(*args))

    def kernel(f):
        return functools.partial(f, cfg)

    *blocks, info = call(kernel(dispatch_kernel), "dispatch", [ids, route, tokens],
                         [(cfg.rp, cfg.w)] * cfg.groups + [shape((2, n), F32)], work=LEAD)
    info_peer = swap(info, "tensor")

    def move(x, r, dc):
        return lax.ppermute(x, ("expert", "context"), [
            (i * 2 + k, (i ^ r) * 2 + (k ^ dc)) for i in range(cfg.groups) for k in range(2)])

    half = cfg.ne // 2
    early, late = cfg.early * 32, (cfg.groups - cfg.early) * 32
    far = move(blocks[3], 3, 0)
    mid = move(blocks[2], 2, 0)
    one = move(blocks[1], 1, 0)
    close = [blocks[0], swap(blocks[0], "context"), one, move(blocks[1], 1, 1), mid, swap(mid, "context")]
    near = call(kernel(near_kernel), "near", [b for a in close for b in (a, swap(a, "tensor"))] + [info_peer],
                [(cfg.ne, early, width)])[0]
    crossed = swap(far, "context")
    near, crossed = lax.optimization_barrier((near, crossed))
    far = [far, swap(far, "tensor"), crossed, swap(crossed, "tensor")]
    hid_a, later = call(kernel(hidden_first_kernel), "hidden_a", far + [near, gate_weight, up_weight],
                        [(half * per, f), (half, late, width)], [pltpu.VMEM((half, late, width), BF16)], work=STEP)
    xa = swap(hid_a, "context")
    hid_b = call(kernel(hidden_second_kernel), "hidden_b", [near, later, gate_weight, up_weight],
                 [(half * per, f)], work=STEP)[0]
    xb = swap(hid_b, "context")
    full = pltpu.VMEM((half * per, ff), BF16)
    out_a = call(kernel(down_first_kernel), "down_a", [hid_a, xa, swap(hid_a, "tensor"), swap(xa, "tensor"), down_weight],
                 [(half * per, wide)], [full], work=STEP)[0]
    message = (4 * cfg.rows, wide // 2)
    outs = call(
        kernel(down_second_kernel), "down_b",
        [hid_b, xb, swap(hid_b, "tensor"), swap(xb, "tensor"), down_weight, out_a],
        [message] * (cfg.groups * 2), [full, pltpu.VMEM((half * per, wide), BF16)], work=STEP)
    returned = [outs[0]] + [move(o, k // 2, k % 2) for k, o in enumerate(outs) if k]
    order = ORDER
    mine, other = call(
        lambda pos_ref, own, peer, *refs: combine_kernel(
            cfg, pos_ref, own, peer, *[refs[order.index(k)] for k in range(len(order))], *refs[len(order):]),
        "combine", [info, info_peer] + [returned[k] for k in order], [(n, 2 * wide)] * 2)
    return call(kernel(join_kernel), "join", [mine, swap(other, "tensor")], [(n, width)])[0]


def by_gathers(tokens, expert_ids, route_weights, gate_weight, up_weight, down_weight):
    n, width = tokens.shape
    local = gate_weight.shape[0]
    groups = lax.axis_size("expert")
    experts = local * groups
    cap = max(2, n * 5 // (4 * experts))
    ids = expert_ids[:, 0]
    member = (ids[:, None] == jnp.arange(experts, dtype=I32)[None, :]).astype(I32)
    rank = jnp.sum((jnp.cumsum(member, axis=0) - 1) * member, axis=1)
    key = ids * cap + rank
    pick = onehot(key[:, None] == jnp.arange(experts * cap, dtype=I32)[None, :])
    out = jnp.dot(pick.T, tokens, preferred_element_type=F32).astype(BF16)
    out = out.reshape(groups, local, cap, width).transpose(1, 0, 2, 3)
    inc = lax.all_to_all(out, "expert", split_axis=1, concat_axis=1, tiled=True)
    inc = inc.reshape(local, groups * cap, width)
    rows = lax.all_gather(inc, ("context", "tensor"), axis=1, tiled=True)
    g = jnp.einsum("end,edf->enf", rows, gate_weight, preferred_element_type=F32)
    u = jnp.einsum("end,edf->enf", rows, up_weight, preferred_element_type=F32)
    hid = (jax.nn.silu(g) * u).astype(BF16)
    hid = lax.all_gather(hid, ("context", "tensor"), axis=2, tiled=True)
    res = jnp.einsum("erf,efd->erd", hid, down_weight, preferred_element_type=F32).astype(BF16)
    back = lax.all_to_all(res, ("context", "tensor"), split_axis=1, concat_axis=2, tiled=True)
    back = back.reshape(local, groups, cap, width)
    back = lax.all_to_all(back, "expert", split_axis=1, concat_axis=1, tiled=True)
    back = back.transpose(1, 0, 2, 3).reshape(experts * cap, width)
    picked = jnp.dot(pick, back, preferred_element_type=F32)
    return (route_weights * picked).astype(BF16)


def solution(mesh):
    size = dict(mesh.shape)
    paired = size["context"] == 2 and size["tensor"] == 2 and size["expert"] == 4
    rows = P(("group", "expert", "context", "tensor"), None)
    weights = P("expert", None, ("context", "tensor"))
    return jax.shard_map(
        on_device if paired else by_gathers,
        mesh=mesh,
        in_specs=(rows, rows, rows, weights, weights, weights),
        out_specs=rows,
        check_vma=False,
    )
```

time: 77.9 us -> 74.2 us (0.953)
  waiting for transfers between devices: 32 us -> 24.5 us
  Pallas kernels: 14.6 us -> 16.5 us
  starting transfers between devices: 28.1 us -> 29.4 us
    ppermute x18 -> x19, waiting for transfers between devices: 17.6 us -> 12.2 us  [swap(): return lax.ppermute(x, axis, [(0, 1), (1, 0)])]
    ppermute x10 -> x11, waiting for transfers between devices: 14.4 us -> 12.2 us  [move(): lax.ppermute(x, ('expert', 'context'), [(i * 2 + k, (i ^ r) * 2 + (k ^ dc...]
    pallas_call x5 -> x8, Pallas kernels: 14.6 us -> 16.5 us  [call(): pl.pallas_call(kernel, in_specs=[smem] + [vmem] * len(ins), out_specs=[vm...]
    ppermute x18 -> x19, starting transfers between devices: 7.41 us -> 8.53 us  [swap(): return lax.ppermute(x, axis, [(0, 1), (1, 0)])]
    ppermute x10 -> x11, starting transfers between devices: 20.7 us -> 20.8 us  [move(): lax.ppermute(x, ('expert', 'context'), [(i * 2 + k, (i ^ r) * 2 + (k ^ dc...]
  transfers between devices with their start and end apart: 28 -> 30, of which waited for: 12 -> 10; matrix products, arithmetic and copies ran while one was open for 0% -> 0% of each run, Pallas kernels for 0% -> 9%
where the time goes in v3:
time: 74.2 us; the launch traced here: 72.9 us
  starting transfers between devices  29.4 us (40%)
  waiting for transfers between devices  24.5 us (33%)
  Pallas kernels  16.5 us (22%)
  local copies, waits for them, and re-layouts  2.37 us (3%)
    ppermute x11, starting transfers between devices, move(): lax.ppermute(x, ('expert', 'context'), [(i * 2 + k, (i ^ r) * 2 + (k ^ dc...  20.8 us
    pallas_call x8, Pallas kernels, call(): pl.pallas_call(kernel, in_specs=[smem] + [vmem] * len(ins), out_specs=[vm...  16.5 us
    ppermute x11, waiting for transfers between devices, move(): lax.ppermute(x, ('expert', 'context'), [(i * 2 + k, (i ^ r) * 2 + (k ^ dc...  12.2 us
    ppermute x19, waiting for transfers between devices, swap(): return lax.ppermute(x, axis, [(0, 1), (1, 0)])  12.2 us
    ppermute x19, starting transfers between devices, swap(): return lax.ppermute(x, axis, [(0, 1), (1, 0)])  8.53 us
    unnamed x16, local copies, waits for them, and re-layouts  2.37 us
  transfers between devices with their start and end apart: 30, of which 10 were waited for; matrix products, arithmetic and copies ran while one was open for 0% of the time, Pallas kernels for 9%

profile of v3, /device:TPU:0, one launch (start us, length us, event | category | flops | bytes accessed | tf_op | source)
XLA Modules:
  0.0 72.9 jit_solution(2164127750488648329)
XLA Ops:
  3.6 4.1 %collective-permute-start.8 = (bf16[80,1024]{1,0:T(8,128)(2,1)S(1)}, bf16[80,1024]{1,0:T(8,128)(2,1)S(1)}, u32[]{:S(2)}, u32[]{:S(2)}) collective-permute-start(bf16[80,1024]{1,0:T(8,128)(2,1)S(1)} %get-tuple-element.27), channel_id=1, source_target_pairs={{0,8},{2,10},{4,12},{6,14},{8,0},{10,2},{12,4},{14,6},{1,9},{3,11}... | collective-permute-start | bytes 491528 | tf_op jit(solution)/shard_map/ppermute | solution.py:241
  7.7 1.5 %collective-permute-start.2 = (bf16[80,1024]{1,0:T(8,128)(2,1)S(1)}, bf16[80,1024]{1,0:T(8,128)(2,1)S(1)}, u32[]{:S(2)}, u32[]{:S(2)}) collective-permute-start(bf16[80,1024]{1,0:T(8,128)(2,1)S(1)} %get-tuple-element.25.refs_0_), channel_id=1, source_target_pairs={{0,2},{2,0},{1,3},{3,1},{4,6},{6,4},{5,7},{7,5},{8,10},{10,8},{9,1... | collective-permute-start | bytes 491528 | tf_op jit(solution)/shard_map/ppermute | solution.py:196
  9.2 1.6 %collective-permute-start.4 = (bf16[80,1024]{1,0:T(8,128)(2,1)S(1)}, bf16[80,1024]{1,0:T(8,128)(2,1)S(1)}, u32[]{:S(2)}, u32[]{:S(2)}) collective-permute-start(bf16[80,1024]{1,0:T(8,128)(2,1)S(1)} %get-tuple-element.26), channel_id=1, source_target_pairs={{0,4},{2,6},{4,0},{6,2},{8,12},{10,14},{12,8},{14,10},{1,5},{3,7},... | collective-permute-start | bytes 491528 | tf_op jit(solution)/shard_map/ppermute | solution.py:241
  12.1 3.4 %collective-permute-done.8.refs_8_ = bf16[80,1024]{1,0:T(8,128)(2,1)S(1)} collective-permute-done((bf16[80,1024]{1,0:T(8,128)(2,1)S(1)}, bf16[80,1024]{1,0:T(8,128)(2,1)S(1)}, u32[]{:S(2)}, u32[]{:S(2)}) %collective-permute-start.8) | collective-permute-done | bytes 163872 | tf_op jit(solution)/shard_map/ppermute | solution.py:241
  15.5 3.5 %collective-permute-start.12 = (bf16[80,1024]{1,0:T(8,128)(2,1)S(1)}, bf16[80,1024]{1,0:T(8,128)(2,1)S(1)}, u32[]{:S(2)}, u32[]{:S(2)}) collective-permute-start(bf16[80,1024]{1,0:T(8,128)(2,1)S(1)} %get-tuple-element.28), channel_id=1, source_target_pairs={{0,12},{2,14},{4,8},{6,10},{8,4},{10,6},{12,0},{14,2},{1,13},{3,15... | collective-permute-start | bytes 491528 | tf_op jit(solution)/shard_map/ppermute | solution.py:241
  19.1 1.5 %collective-permute-start.10 = (bf16[80,1024]{1,0:T(8,128)(2,1)S(1)}, bf16[80,1024]{1,0:T(8,128)(2,1)S(1)}, u32[]{:S(2)}, u32[]{:S(2)}) collective-permute-start(bf16[80,1024]{1,0:T(8,128)(2,1)S(1)} %collective-permute-done.8.refs_8_), channel_id=1, source_target_pairs={{0,2},{2,0},{1,3},{3,1},{4,6},{6,4},{5,7},{7,5},{8,10},{10,8},{9,1... | collective-permute-start | bytes 491528 | tf_op jit(solution)/shard_map/ppermute | solution.py:196
  21.2 2.5 %collective-permute-done.12.refs_0_ = bf16[80,1024]{1,0:T(8,128)(2,1)S(1)} collective-permute-done((bf16[80,1024]{1,0:T(8,128)(2,1)S(1)}, bf16[80,1024]{1,0:T(8,128)(2,1)S(1)}, u32[]{:S(2)}, u32[]{:S(2)}) %collective-permute-start.12) | collective-permute-done | bytes 163872 | tf_op jit(solution)/shard_map/ppermute | solution.py:241
  24.9 1.8 %collective-permute-start.13 = (bf16[80,1024]{1,0:T(8,128)(2,1)S(1)}, bf16[80,1024]{1,0:T(8,128)(2,1)S(1)}, u32[]{:S(2)}, u32[]{:S(2)}) collective-permute-start(bf16[80,1024]{1,0:T(8,128)(2,1)S(1)} %collective-permute-done.12.refs_0_), channel_id=1, source_target_pairs={{0,2},{2,0},{1,3},{3,1},{4,6},{6,4},{5,7},{7,5},{8,10},{10,8},{9,1... | collective-permute-start | bytes 491528 | tf_op jit(solution)/shard_map/ppermute | solution.py:196
  26.9 1.5 %near.1.refs_4_ = bf16[4,96,4096]{2,1,0:T(8,128)(2,1)S(1)} custom-call(s32[3]{0:T(128)S(1)} %pad_add_fusion.pos_ref, bf16[80,1024]{1,0:T(8,128)(2,1)S(1)} %get-tuple-element.25.refs_0_, bf16[80,1024]{1,0:T(8,128)(2,1)S(1)} %collective-permute-done.1.refs_1_, bf16[80,1024]{1,0:T(8,128)(2,1)S(1)} %collective-permute-done.2.refs_2_, ...), custom_call_target="tpu_custom_call" | custom-call | flops 1000000000 | tf_op jit(solution)/shard_map/near/pallas_call | solution.py:228
  28.4 3.1 %collective-permute-done.13.refs_2_ = bf16[80,1024]{1,0:T(8,128)(2,1)S(1)} collective-permute-done((bf16[80,1024]{1,0:T(8,128)(2,1)S(1)}, bf16[80,1024]{1,0:T(8,128)(2,1)S(1)}, u32[]{:S(2)}, u32[]{:S(2)}) %collective-permute-start.13) | collective-permute-done | bytes 163872 | tf_op jit(solution)/shard_map/ppermute | solution.py:196
  31.5 1.4 %collective-permute-done.15.refs_3_ = bf16[80,1024]{1,0:T(8,128)(2,1)S(1)} collective-permute-done((bf16[80,1024]{1,0:T(8,128)(2,1)S(1)}, bf16[80,1024]{1,0:T(8,128)(2,1)S(1)}, u32[]{:S(2)}, u32[]{:S(2)}) %collective-permute-start.15) | collective-permute-done | bytes 163872 | tf_op jit(solution)/shard_map/ppermute | solution.py:196
  32.9 3.5 %hidden_a.1 = (bf16[160,384]{1,0:T(8,128)(2,1)S(1)}, bf16[2,32,4096]{2,1,0:T(8,128)(2,1)S(1)}) custom-call(s32[3]{0:T(128)S(1)} %pad_add_fusion.pos_ref, bf16[80,1024]{1,0:T(8,128)(2,1)S(1)} %collective-permute-done.12.refs_0_, bf16[80,1024]{1,0:T(8,128)(2,1)S(1)} %collective-permute-done.14.refs_1_, bf16[80,1024]{1,0:T(8,128)(2,1)S(1)} %collective-permute-done.13.refs_2_, ...), custom_call_target="tpu_custom_call" | custom-call | flops 10000000000 | tf_op jit(solution)/shard_map/hidden_a/pallas_call | solution.py:228
  36.5 1.8 %collective-permute-start.19 = (bf16[160,384]{1,0:T(8,128)(2,1)S(1)}, bf16[160,384]{1,0:T(8,128)(2,1)S(1)}, u32[]{:S(2)}, u32[]{:S(2)}) collective-permute-start(bf16[160,384]{1,0:T(8,128)(2,1)S(1)} %get-tuple-element.32.own), channel_id=1, source_target_pairs={{0,2},{2,0},{1,3},{3,1},{4,6},{6,4},{5,7},{7,5},{8,10},{10,8},{9,1... | collective-permute-start | bytes 368648 | tf_op jit(solution)/shard_map/ppermute | solution.py:196
  38.3 3.2 %hidden_b.1.own = bf16[160,384]{1,0:T(8,128)(2,1)S(1)} custom-call(s32[3]{0:T(128)S(1)} %pad_add_fusion.pos_ref, bf16[4,96,4096]{2,1,0:T(8,128)(2,1)S(1)} %near.1.refs_4_, bf16[2,32,4096]{2,1,0:T(8,128)(2,1)S(1)} %get-tuple-element.31.far, bf16[4,4096,384]{2,1,0:T(8,128)(2,1)S(1)} %copy-done, bf16[4,4096,384]{2,1,0:T(8,128)(2,1)S(1)} %copy-done.1), custom_call_target="tpu_custom_call" | custom-call | flops 10000000000 | tf_op jit(solution)/shard_map/hidden_b/pallas_call | solution.py:228
  42.4 4.2 %collective-permute-done.16.x = bf16[160,384]{1,0:T(8,128)(2,1)S(1)} collective-permute-done((bf16[160,384]{1,0:T(8,128)(2,1)S(1)}, bf16[160,384]{1,0:T(8,128)(2,1)S(1)}, u32[]{:S(2)}, u32[]{:S(2)}) %collective-permute-start.16) | collective-permute-done | bytes 122912 | tf_op jit(solution)/shard_map/ppermute | solution.py:196
  46.7 1.8 %down_a.1.before = bf16[160,1024]{1,0:T(8,128)(2,1)S(1)} custom-call(s32[3]{0:T(128)S(1)} %pad_add_fusion.pos_ref, bf16[160,384]{1,0:T(8,128)(2,1)S(1)} %get-tuple-element.32.own, bf16[160,384]{1,0:T(8,128)(2,1)S(1)} %collective-permute-done.19.x, bf16[160,384]{1,0:T(8,128)(2,1)S(1)} %collective-permute-done.20.core, ...), custom_call_target="tpu_custom_call" | custom-call | flops 10000000000 | tf_op jit(solution)/shard_map/down_a/pallas_call | solution.py:228
  48.6 2.8 %down_b.1 = (bf16[80,512]{1,0:T(8,128)(2,1)S(1)}, bf16[80,512]{1,0:T(8,128)(2,1)S(1)}, bf16[80,512]{1,0:T(8,128)(2,1)S(1)}, bf16[80,512]{1,0:T(8,128)(2,1)S(1)},...) custom-call(s32[3]{0:T(128)S(1)} %pad_add_fusion.pos_ref, ...), custom_call_target="tpu_custom_call" | custom-call | flops 10000000000 | tf_op jit(solution)/shard_map/down_b/pallas_call | solution.py:228
  53.2 1.7 %collective-permute-start.24 = (bf16[80,512]{1,0:T(8,128)(2,1)S(1)}, bf16[80,512]{1,0:T(8,128)(2,1)S(1)}, u32[]{:S(2)}, u32[]{:S(2)}) collective-permute-start(bf16[80,512]{1,0:T(8,128)(2,1)S(1)} %get-tuple-element.36), channel_id=1, source_target_pairs={{0,2},{2,0},{4,6},{6,4},{8,10},{10,8},{12,14},{14,12},{1,3},{3,1},... | collective-permute-start | bytes 245768 | tf_op jit(solution)/shard_map/ppermute | solution.py:241
  55.4 2.2 %collective-permute-start.26 = (bf16[80,512]{1,0:T(8,128)(2,1)S(1)}, bf16[80,512]{1,0:T(8,128)(2,1)S(1)}, u32[]{:S(2)}, u32[]{:S(2)}) collective-permute-start(bf16[80,512]{1,0:T(8,128)(2,1)S(1)} %get-tuple-element.38), channel_id=1, source_target_pairs={{0,8},{2,10},{4,12},{6,14},{8,0},{10,2},{12,4},{14,6},{1,9},{3,11}... | collective-permute-start | bytes 245768 | tf_op jit(solution)/shard_map/ppermute | solution.py:241
  57.6 3.0 %collective-permute-start.27 = (bf16[80,512]{1,0:T(8,128)(2,1)S(1)}, bf16[80,512]{1,0:T(8,128)(2,1)S(1)}, u32[]{:S(2)}, u32[]{:S(2)}) collective-permute-start(bf16[80,512]{1,0:T(8,128)(2,1)S(1)} %get-tuple-element.39), channel_id=1, source_target_pairs={{0,14},{2,12},{4,10},{6,8},{8,6},{10,4},{12,2},{14,0},{1,15},{3,13... | collective-permute-start | bytes 245768 | tf_op jit(solution)/shard_map/ppermute | solution.py:241
  60.6 2.0 %collective-permute-start.28 = (bf16[80,512]{1,0:T(8,128)(2,1)S(1)}, bf16[80,512]{1,0:T(8,128)(2,1)S(1)}, u32[]{:S(2)}, u32[]{:S(2)}) collective-permute-start(bf16[80,512]{1,0:T(8,128)(2,1)S(1)} %get-tuple-element.40), channel_id=1, source_target_pairs={{0,12},{2,14},{4,8},{6,10},{8,4},{10,6},{12,0},{14,2},{1,13},{3,15... | collective-permute-start | bytes 245768 | tf_op jit(solution)/shard_map/ppermute | solution.py:241
  62.6 5.6 %collective-permute-done.25.refs_4_ = bf16[80,512]{1,0:T(8,128)(2,1)S(1)} collective-permute-done((bf16[80,512]{1,0:T(8,128)(2,1)S(1)}, bf16[80,512]{1,0:T(8,128)(2,1)S(1)}, u32[]{:S(2)}, u32[]{:S(2)}) %collective-permute-start.25) | collective-permute-done | bytes 81952 | tf_op jit(solution)/shard_map/ppermute | solution.py:241
  70.0 1.5 %collective-permute-done.29.other = bf16[64,2048]{1,0:T(8,128)(2,1)S(1)} collective-permute-done((bf16[64,2048]{1,0:T(8,128)(2,1)S(1)}, bf16[64,2048]{1,0:T(8,128)(2,1)S(1)}, u32[]{:S(2)}, u32[]{:S(2)}) %collective-permute-start.29) | collective-permute-done | bytes 262176 | tf_op jit(solution)/shard_map/ppermute | solution.py:196
  71.5 1.4 %join.1 = bf16[64,4096]{1,0:T(8,128)(2,1)} custom-call(s32[3]{0:T(128)S(1)} %pad_add_fusion.pos_ref, bf16[64,2048]{1,0:T(8,128)(2,1)S(1)} %get-tuple-element.41.mine, bf16[64,2048]{1,0:T(8,128)(2,1)S(1)} %collective-permute-done.29.other), custom_call_target="tpu_custom_call" | custom-call | flops 1000000000 | tf_op jit(solution)/shard_map/join/pallas_call | solution.py:228
  (62 shorter events, 12.0 us)
Async XLA Ops:
  3.6 11.9 %collective-permute-start.8 = (bf16[80,1024]{1,0:T(8,128)(2,1)S(1)}, bf16[80,1024]{1,0:T(8,128)(2,1)S(1)}, u32[]{:S(2)}, u32[]{:S(2)}) collective-permute-start(bf16[80,1024]{1,0:T(8,128)(2,1)S(1)} %get-tuple-element.27), channel_id=1, source_target_pairs={{0,8},{2,10},{4,12},{6,14},{8,0},{10,2},{12,4},{14,6},{1,9},{3,11}... | collective-permute-start | bytes 491528 | tf_op jit(solution)/shard_map/ppermute | solution.py:241
  7.7 11.3 %collective-permute-start.2 = (bf16[80,1024]{1,0:T(8,128)(2,1)S(1)}, bf16[80,1024]{1,0:T(8,128)(2,1)S(1)}, u32[]{:S(2)}, u32[]{:S(2)}) collective-permute-start(bf16[80,1024]{1,0:T(8,128)(2,1)S(1)} %get-tuple-element.25.refs_0_), channel_id=1, source_target_pairs={{0,2},{2,0},{1,3},{3,1},{4,6},{6,4},{5,7},{7,5},{8,10},{10,8},{9,1... | collective-permute-start | bytes 491528 | tf_op jit(solution)/shard_map/ppermute | solution.py:196
  9.2 11.4 %collective-permute-start.4 = (bf16[80,1024]{1,0:T(8,128)(2,1)S(1)}, bf16[80,1024]{1,0:T(8,128)(2,1)S(1)}, u32[]{:S(2)}, u32[]{:S(2)}) collective-permute-start(bf16[80,1024]{1,0:T(8,128)(2,1)S(1)} %get-tuple-element.26), channel_id=1, source_target_pairs={{0,4},{2,6},{4,0},{6,2},{8,12},{10,14},{12,8},{14,10},{1,5},{3,7},... | collective-permute-start | bytes 491528 | tf_op jit(solution)/shard_map/ppermute | solution.py:241
  10.8 9.8 %collective-permute-start.6 = (bf16[80,1024]{1,0:T(8,128)(2,1)S(1)}, bf16[80,1024]{1,0:T(8,128)(2,1)S(1)}, u32[]{:S(2)}, u32[]{:S(2)}) collective-permute-start(bf16[80,1024]{1,0:T(8,128)(2,1)S(1)} %get-tuple-element.26), channel_id=1, source_target_pairs={{0,6},{2,4},{4,2},{6,0},{8,14},{10,12},{12,10},{14,8},{1,7},{3,5},... | collective-permute-start | bytes 491528 | tf_op jit(solution)/shard_map/ppermute | solution.py:241
  11.9 9.2 %collective-permute-start.1 = (bf16[80,1024]{1,0:T(8,128)(2,1)S(1)}, bf16[80,1024]{1,0:T(8,128)(2,1)S(1)}, u32[]{:S(2)}, u32[]{:S(2)}) collective-permute-start(bf16[80,1024]{1,0:T(8,128)(2,1)S(1)} %get-tuple-element.25.refs_0_), channel_id=1, source_target_pairs={{0,1},{1,0},{2,3},{3,2},{4,5},{5,4},{6,7},{7,6},{8,9},{9,8},{10,11... | collective-permute-start | bytes 491528 | tf_op jit(solution)/shard_map/ppermute | solution.py:196
  15.5 8.1 %collective-permute-start.12 = (bf16[80,1024]{1,0:T(8,128)(2,1)S(1)}, bf16[80,1024]{1,0:T(8,128)(2,1)S(1)}, u32[]{:S(2)}, u32[]{:S(2)}) collective-permute-start(bf16[80,1024]{1,0:T(8,128)(2,1)S(1)} %get-tuple-element.28), channel_id=1, source_target_pairs={{0,12},{2,14},{4,8},{6,10},{8,4},{10,6},{12,0},{14,2},{1,13},{3,15... | collective-permute-start | bytes 491528 | tf_op jit(solution)/shard_map/ppermute | solution.py:241
  19.1 5.8 %collective-permute-start.10 = (bf16[80,1024]{1,0:T(8,128)(2,1)S(1)}, bf16[80,1024]{1,0:T(8,128)(2,1)S(1)}, u32[]{:S(2)}, u32[]{:S(2)}) collective-permute-start(bf16[80,1024]{1,0:T(8,128)(2,1)S(1)} %collective-permute-done.8.refs_8_), channel_id=1, source_target_pairs={{0,2},{2,0},{1,3},{3,1},{4,6},{6,4},{5,7},{7,5},{8,10},{10,8},{9,1... | collective-permute-start | bytes 491528 | tf_op jit(solution)/shard_map/ppermute | solution.py:196
  20.6 4.3 %collective-permute-start.3 = (bf16[80,1024]{1,0:T(8,128)(2,1)S(1)}, bf16[80,1024]{1,0:T(8,128)(2,1)S(1)}, u32[]{:S(2)}, u32[]{:S(2)}) collective-permute-start(bf16[80,1024]{1,0:T(8,128)(2,1)S(1)} %collective-permute-done.2.refs_2_), channel_id=1, source_target_pairs={{0,1},{1,0},{2,3},{3,2},{4,5},{5,4},{6,7},{7,6},{8,9},{9,8},{10,11... | collective-permute-start | bytes 491528 | tf_op jit(solution)/shard_map/ppermute | solution.py:196
  20.6 6.3 %collective-permute-start.9 = (bf16[80,1024]{1,0:T(8,128)(2,1)S(1)}, bf16[80,1024]{1,0:T(8,128)(2,1)S(1)}, u32[]{:S(2)}, u32[]{:S(2)}) collective-permute-start(bf16[80,1024]{1,0:T(8,128)(2,1)S(1)} %collective-permute-done.8.refs_8_), channel_id=1, source_target_pairs={{0,1},{1,0},{2,3},{3,2},{4,5},{5,4},{6,7},{7,6},{8,9},{9,8},{10,11... | collective-permute-start | bytes 491528 | tf_op jit(solution)/shard_map/ppermute | solution.py:196
  21.1 5.6 %collective-permute-start.5 = (bf16[80,1024]{1,0:T(8,128)(2,1)S(1)}, bf16[80,1024]{1,0:T(8,128)(2,1)S(1)}, u32[]{:S(2)}, u32[]{:S(2)}) collective-permute-start(bf16[80,1024]{1,0:T(8,128)(2,1)S(1)} %collective-permute-done.4.refs_4_), channel_id=1, source_target_pairs={{0,1},{1,0},{2,3},{3,2},{4,5},{5,4},{6,7},{7,6},{8,9},{9,8},{10,11... | collective-permute-start | bytes 491528 | tf_op jit(solution)/shard_map/ppermute | solution.py:196
  24.9 6.7 %collective-permute-start.13 = (bf16[80,1024]{1,0:T(8,128)(2,1)S(1)}, bf16[80,1024]{1,0:T(8,128)(2,1)S(1)}, u32[]{:S(2)}, u32[]{:S(2)}) collective-permute-start(bf16[80,1024]{1,0:T(8,128)(2,1)S(1)} %collective-permute-done.12.refs_0_), channel_id=1, source_target_pairs={{0,2},{2,0},{1,3},{3,1},{4,6},{6,4},{5,7},{7,5},{8,10},{10,8},{9,1... | collective-permute-start | bytes 491528 | tf_op jit(solution)/shard_map/ppermute | solution.py:196
  26.7 4.9 %collective-permute-start.14 = (bf16[80,1024]{1,0:T(8,128)(2,1)S(1)}, bf16[80,1024]{1,0:T(8,128)(2,1)S(1)}, u32[]{:S(2)}, u32[]{:S(2)}) collective-permute-start(bf16[80,1024]{1,0:T(8,128)(2,1)S(1)} %collective-permute-done.12.refs_0_), channel_id=1, source_target_pairs={{0,1},{1,0},{2,3},{3,2},{4,5},{5,4},{6,7},{7,6},{8,9},{9,8},{10,11... | collective-permute-start | bytes 491528 | tf_op jit(solution)/shard_map/ppermute | solution.py:196
  36.5 5.4 %collective-permute-start.19 = (bf16[160,384]{1,0:T(8,128)(2,1)S(1)}, bf16[160,384]{1,0:T(8,128)(2,1)S(1)}, u32[]{:S(2)}, u32[]{:S(2)}) collective-permute-start(bf16[160,384]{1,0:T(8,128)(2,1)S(1)} %get-tuple-element.32.own), channel_id=1, source_target_pairs={{0,2},{2,0},{1,3},{3,1},{4,6},{6,4},{5,7},{7,5},{8,10},{10,8},{9,1... | collective-permute-start | bytes 368648 | tf_op jit(solution)/shard_map/ppermute | solution.py:196
  41.5 5.2 %collective-permute-start.16 = (bf16[160,384]{1,0:T(8,128)(2,1)S(1)}, bf16[160,384]{1,0:T(8,128)(2,1)S(1)}, u32[]{:S(2)}, u32[]{:S(2)}) collective-permute-start(bf16[160,384]{1,0:T(8,128)(2,1)S(1)} %hidden_b.1.own), channel_id=1, source_target_pairs={{0,2},{2,0},{1,3},{3,1},{4,6},{6,4},{5,7},{7,5},{8,10},{10,8},{9,1... | collective-permute-start | bytes 368648 | tf_op jit(solution)/shard_map/ppermute | solution.py:196
  41.9 4.8 %collective-permute-start.20 = (bf16[160,384]{1,0:T(8,128)(2,1)S(1)}, bf16[160,384]{1,0:T(8,128)(2,1)S(1)}, u32[]{:S(2)}, u32[]{:S(2)}) collective-permute-start(bf16[160,384]{1,0:T(8,128)(2,1)S(1)} %get-tuple-element.32.own), channel_id=1, source_target_pairs={{0,1},{1,0},{2,3},{3,2},{4,5},{5,4},{6,7},{7,6},{8,9},{9,8},{10,11... | collective-permute-start | bytes 368648 | tf_op jit(solution)/shard_map/ppermute | solution.py:196
  41.9 4.8 %collective-permute-start.21 = (bf16[160,384]{1,0:T(8,128)(2,1)S(1)}, bf16[160,384]{1,0:T(8,128)(2,1)S(1)}, u32[]{:S(2)}, u32[]{:S(2)}) collective-permute-start(bf16[160,384]{1,0:T(8,128)(2,1)S(1)} %collective-permute-done.19.x), channel_id=1, source_target_pairs={{0,1},{1,0},{2,3},{3,2},{4,5},{5,4},{6,7},{7,6},{8,9},{9,8},{10,11... | collective-permute-start | bytes 368648 | tf_op jit(solution)/shard_map/ppermute | solution.py:196
  42.4 6.2 %collective-permute-start.17 = (bf16[160,384]{1,0:T(8,128)(2,1)S(1)}, bf16[160,384]{1,0:T(8,128)(2,1)S(1)}, u32[]{:S(2)}, u32[]{:S(2)}) collective-permute-start(bf16[160,384]{1,0:T(8,128)(2,1)S(1)} %hidden_b.1.own), channel_id=1, source_target_pairs={{0,1},{1,0},{2,3},{3,2},{4,5},{5,4},{6,7},{7,6},{8,9},{9,8},{10,11... | collective-permute-start | bytes 368648 | tf_op jit(solution)/shard_map/ppermute | solution.py:196
  51.4 6.2 %collective-permute-start.22 = (bf16[80,512]{1,0:T(8,128)(2,1)S(1)}, bf16[80,512]{1,0:T(8,128)(2,1)S(1)}, u32[]{:S(2)}, u32[]{:S(2)}) collective-permute-start(bf16[80,512]{1,0:T(8,128)(2,1)S(1)} %get-tuple-element.34), channel_id=1, source_target_pairs={{0,6},{2,4},{4,2},{6,0},{8,14},{10,12},{12,10},{14,8},{1,7},{3,5},... | collective-permute-start | bytes 245768 | tf_op jit(solution)/shard_map/ppermute | solution.py:241
  52.1 8.5 %collective-permute-start.23 = (bf16[80,512]{1,0:T(8,128)(2,1)S(1)}, bf16[80,512]{1,0:T(8,128)(2,1)S(1)}, u32[]{:S(2)}, u32[]{:S(2)}) collective-permute-start(bf16[80,512]{1,0:T(8,128)(2,1)S(1)} %get-tuple-element.35), channel_id=1, source_target_pairs={{0,4},{2,6},{4,0},{6,2},{8,12},{10,14},{12,8},{14,10},{1,5},{3,7},... | collective-permute-start | bytes 245768 | tf_op jit(solution)/shard_map/ppermute | solution.py:241
  53.2 9.4 %collective-permute-start.24 = (bf16[80,512]{1,0:T(8,128)(2,1)S(1)}, bf16[80,512]{1,0:T(8,128)(2,1)S(1)}, u32[]{:S(2)}, u32[]{:S(2)}) collective-permute-start(bf16[80,512]{1,0:T(8,128)(2,1)S(1)} %get-tuple-element.36), channel_id=1, source_target_pairs={{0,2},{2,0},{4,6},{6,4},{8,10},{10,8},{12,14},{14,12},{1,3},{3,1},... | collective-permute-start | bytes 245768 | tf_op jit(solution)/shard_map/ppermute | solution.py:241
  54.9 13.3 %collective-permute-start.25 = (bf16[80,512]{1,0:T(8,128)(2,1)S(1)}, bf16[80,512]{1,0:T(8,128)(2,1)S(1)}, u32[]{:S(2)}, u32[]{:S(2)}) collective-permute-start(bf16[80,512]{1,0:T(8,128)(2,1)S(1)} %get-tuple-element.37), channel_id=1, source_target_pairs={{0,10},{2,8},{4,14},{6,12},{8,2},{10,0},{12,6},{14,4},{1,11},{3,9}... | collective-permute-start | bytes 245768 | tf_op jit(solution)/shard_map/ppermute | solution.py:241
  55.4 13.5 %collective-permute-start.26 = (bf16[80,512]{1,0:T(8,128)(2,1)S(1)}, bf16[80,512]{1,0:T(8,128)(2,1)S(1)}, u32[]{:S(2)}, u32[]{:S(2)}) collective-permute-start(bf16[80,512]{1,0:T(8,128)(2,1)S(1)} %get-tuple-element.38), channel_id=1, source_target_pairs={{0,8},{2,10},{4,12},{6,14},{8,0},{10,2},{12,4},{14,6},{1,9},{3,11}... | collective-permute-start | bytes 245768 | tf_op jit(solution)/shard_map/ppermute | solution.py:241
  57.6 11.3 %collective-permute-start.27 = (bf16[80,512]{1,0:T(8,128)(2,1)S(1)}, bf16[80,512]{1,0:T(8,128)(2,1)S(1)}, u32[]{:S(2)}, u32[]{:S(2)}) collective-permute-start(bf16[80,512]{1,0:T(8,128)(2,1)S(1)} %get-tuple-element.39), channel_id=1, source_target_pairs={{0,14},{2,12},{4,10},{6,8},{8,6},{10,4},{12,2},{14,0},{1,15},{3,13... | collective-permute-start | bytes 245768 | tf_op jit(solution)/shard_map/ppermute | solution.py:241
  60.6 8.3 %collective-permute-start.28 = (bf16[80,512]{1,0:T(8,128)(2,1)S(1)}, bf16[80,512]{1,0:T(8,128)(2,1)S(1)}, u32[]{:S(2)}, u32[]{:S(2)}) collective-permute-start(bf16[80,512]{1,0:T(8,128)(2,1)S(1)} %get-tuple-element.40), channel_id=1, source_target_pairs={{0,12},{2,14},{4,8},{6,10},{8,4},{10,6},{12,0},{14,2},{1,13},{3,15... | collective-permute-start | bytes 245768 | tf_op jit(solution)/shard_map/ppermute | solution.py:241
  (14 other events, 110.6 us)

commit v4 on v3

--- a/solution.py
+++ b/solution.py
@@ -7,7 +7,7 @@
 from jax.sharding import PartitionSpec as P
 
 BIG = 4096
-ORDER = (0, 3, 2, 1, 5, 4, 7, 6)
+ORDER = (0, 7, 5, 3, 1, 6, 4, 2)
 LEAD = 20 * 10**9
 STEP = 10 * 10**9
 VMEM_LIMIT = 8 * 1024 * 1024
@@ -44,11 +44,9 @@
     return ids_row * cap + rank
 
 
-def dispatch_kernel(cfg, pos_ref, ids_ref, route_ref, tok_ref, *outs):
+def dispatch_kernel(cfg, pos_ref, ids_ref, tok_ref, *outs):
     z = pos_ref[0]
     keys = slot_keys(ids_ref[...], cfg.cap)
-    outs[-1][0:1] = keys.astype(F32)
-    outs[-1][1:2] = route_ref[...]
     keys = jnp.concatenate([keys + j * BIG for j in range(cfg.nd)], axis=1)
     stacked = jnp.concatenate([tok_ref[:, j * cfg.w:(j + 1) * cfg.w] for j in range(cfg.nd)], axis=0)
     i = iota((cfg.rp, 1), 0)
@@ -74,7 +72,9 @@
 
 
 def near_kernel(cfg, pos_ref, *refs):
-    rows = refs[-1]
+    ids_ref, route_ref, rows, info = refs[-4:]
+    info[0:1] = slot_keys(ids_ref[...], cfg.cap).astype(F32)
+    info[1:2] = route_ref[...]
 
     def store(e, k, j, v):
         rows[e, k * 16:(k + 1) * 16, j * cfg.w:(j + 1) * cfg.w] = v
@@ -87,7 +87,9 @@
     i = iota((per, 1), 0)
     s = div(i, cfg.cap)
     slot = i - s * cfg.cap
-    rel = jnp.bitwise_xor(s, pos_ref[1] * 2 + pos_ref[2])
+    rel = jnp.bitwise_xor(s & 3, pos_ref[1] * 2 + pos_ref[2])
+    for k, r in enumerate(cfg.visits):
+        rel = rel + jnp.where((s >> 2) == r, 4 * k, 0)
     compact = onehot(iota((1, cfg.sources * 8), 1) == rel * 8 + slot)
     for k in range(cfg.ne // 2):
         e = first + k
@@ -142,7 +144,7 @@
         out[...] = dot(onehot(lane - place_at == want), stacked).astype(BF16)
 
 
-def down_first_kernel(cfg, pos_ref, own, x, core, xcore, down, out, full):
+def down_first_kernel(cfg, pos_ref, own, x, core, xcore, down, info, out, full):
     down_rows(cfg, pos_ref, (own, x, core, xcore), down, full, out, 0)
 
 
@@ -209,7 +211,8 @@
     cfg.w = width // cfg.nd
     cfg.rp = cfg.rows * cfg.nd
     cfg.sources = cfg.groups * 4
-    cfg.early = cfg.groups - 1
+    cfg.early = 3
+    cfg.visits = (0, 1, 2, 3)
     f = gate_weight.shape[2]
     ff, wide = down_weight.shape[1:]
     per = cfg.sources * cfg.cap
@@ -233,9 +236,7 @@
     def kernel(f):
         return functools.partial(f, cfg)
 
-    *blocks, info = call(kernel(dispatch_kernel), "dispatch", [ids, route, tokens],
-                         [(cfg.rp, cfg.w)] * cfg.groups + [shape((2, n), F32)], work=LEAD)
-    info_peer = swap(info, "tensor")
+    blocks = call(kernel(dispatch_kernel), "dispatch", [ids, tokens], [(cfg.rp, cfg.w)] * cfg.groups, work=LEAD)
 
     def move(x, r, dc):
         return lax.ppermute(x, ("expert", "context"), [
@@ -243,15 +244,17 @@
 
     half = cfg.ne // 2
     early, late = cfg.early * 32, (cfg.groups - cfg.early) * 32
-    far = move(blocks[3], 3, 0)
-    mid = move(blocks[2], 2, 0)
-    one = move(blocks[1], 1, 0)
-    close = [blocks[0], swap(blocks[0], "context"), one, move(blocks[1], 1, 1), mid, swap(mid, "context")]
-    near = call(kernel(near_kernel), "near", [b for a in close for b in (a, swap(a, "tensor"))] + [info_peer],
-                [(cfg.ne, early, width)])[0]
-    crossed = swap(far, "context")
-    near, crossed = lax.optimization_barrier((near, crossed))
-    far = [far, swap(far, "tensor"), crossed, swap(crossed, "tensor")]
+    held = [blocks[0]] + [move(blocks[r], r, 0) for r in range(1, cfg.groups)]
+    crossed = [swap(x, "context") for x in held]
+
+
+    def four(r):
+        return [held[r], swap(held[r], "tensor"), crossed[r], swap(crossed[r], "tensor")]
+
+    near, info = call(kernel(near_kernel), "near", [b for r in cfg.visits[:cfg.early] for b in four(r)] + [ids, route],
+                      [(cfg.ne, early, width), shape((2, n), F32)])
+    info_peer = swap(info, "tensor")
+    far = [b for r in cfg.visits[cfg.early:] for b in four(r)]
     hid_a, later = call(kernel(hidden_first_kernel), "hidden_a", far + [near, gate_weight, up_weight],
                         [(half * per, f), (half, late, width)], [pltpu.VMEM((half, late, width), BF16)], work=STEP)
     xa = swap(hid_a, "context")
@@ -259,7 +262,7 @@
                  [(half * per, f)], work=STEP)[0]
     xb = swap(hid_b, "context")
     full = pltpu.VMEM((half * per, ff), BF16)
-    out_a = call(kernel(down_first_kernel), "down_a", [hid_a, xa, swap(hid_a, "tensor"), swap(xa, "tensor"), down_weight],
+    out_a = call(kernel(down_first_kernel), "down_a", [hid_a, xa, swap(hid_a, "tensor"), swap(xa, "tensor"), down_weight, info_peer],
                  [(half * per, wide)], [full], work=STEP)[0]
     message = (4 * cfg.rows, wide // 2)
     outs = call(

time: 74.2 us -> 70.6 us (0.951); the launches traced: 72.9 us -> 70.4 us
  starting transfers between devices: 29.4 us -> 28.2 us
  waiting for transfers between devices: 24.5 us -> 23.7 us
    ppermute x11 -> x10, starting transfers between devices: 20.8 us -> 18.7 us  [move(): lax.ppermute(x, ('expert', 'context'), [(i * 2 + k, (i ^ r) * 2 + (k ^ dc...]
    ppermute x19 -> x20, starting transfers between devices: 8.53 us -> 9.56 us  [swap(): return lax.ppermute(x, axis, [(0, 1), (1, 0)])]
    ppermute x19 -> x20, waiting for transfers between devices: 12.2 us -> 11.8 us  [swap(): return lax.ppermute(x, axis, [(0, 1), (1, 0)])]
    ppermute x11 -> x10, waiting for transfers between devices: 12.2 us -> 11.9 us  [move(): lax.ppermute(x, ('expert', 'context'), [(i * 2 + k, (i ^ r) * 2 + (k ^ dc...]
  transfers between devices with their start and end apart: 30 -> 30, of which waited for: 10 -> 12; matrix products, arithmetic and copies ran while one was open for 0% -> 0% of each run, Pallas kernels for 9% -> 9%
where the time goes in v4:
time: 70.6 us; the launch traced here: 70.4 us
  starting transfers between devices  28.2 us (40%)
  waiting for transfers between devices  23.7 us (34%)
  Pallas kernels  16.4 us (23%)
  local copies, waits for them, and re-layouts  1.72 us (2%)
    ppermute x10, starting transfers between devices, move(): lax.ppermute(x, ('expert', 'context'), [(i * 2 + k, (i ^ r) * 2 + (k ^ dc...  18.7 us
    pallas_call x8, Pallas kernels, call(): pl.pallas_call(kernel, in_specs=[smem] + [vmem] * len(ins), out_specs=[vm...  16.4 us
    ppermute x10, waiting for transfers between devices, move(): lax.ppermute(x, ('expert', 'context'), [(i * 2 + k, (i ^ r) * 2 + (k ^ dc...  11.9 us
    ppermute x20, waiting for transfers between devices, swap(): return lax.ppermute(x, axis, [(0, 1), (1, 0)])  11.8 us
    ppermute x20, starting transfers between devices, swap(): return lax.ppermute(x, axis, [(0, 1), (1, 0)])  9.56 us
    unnamed x16, local copies, waits for them, and re-layouts  1.72 us
  transfers between devices with their start and end apart: 30, of which 12 were waited for; matrix products, arithmetic and copies ran while one was open for 0% of the time, Pallas kernels for 9%

profile of v4, /device:TPU:0, one launch (start us, length us, event | category | flops | bytes accessed | tf_op | source)
XLA Modules:
  0.0 70.4 jit_solution(9900644743892655022)
XLA Ops:
  1.8 1.2 %dispatch.1 = (bf16[80,1024]{1,0:T(8,128)(2,1)S(1)}, bf16[80,1024]{1,0:T(8,128)(2,1)S(1)}, bf16[80,1024]{1,0:T(8,128)(2,1)S(1)}, bf16[80,1024]{1,0:T(8,128)(2,1)S(1)}) custom-call(s32[3]{0:T(128)S(1)} %pad_add_fusion.pos_ref, s32[1,64]{1,0:T(1,128)S(1)} %bitcast.7, bf16[64,4096]{1,0:T(8,128)(2,1)S(1)} %copy-done.2), custom_call_target="tpu_custom_call" | custom-call | flops 20000000000 | tf_op jit(solution)/shard_map/dispatch/pallas_call | solution.py:231
  3.0 4.1 %collective-permute-start.7 = (bf16[80,1024]{1,0:T(8,128)(2,1)S(1)}, bf16[80,1024]{1,0:T(8,128)(2,1)S(1)}, u32[]{:S(2)}, u32[]{:S(2)}) collective-permute-start(bf16[80,1024]{1,0:T(8,128)(2,1)S(1)} %get-tuple-element.25), channel_id=1, source_target_pairs={{0,8},{2,10},{4,12},{6,14},{8,0},{10,2},{12,4},{14,6},{1,9},{3,11}... | collective-permute-start | bytes 491528 | tf_op jit(solution)/shard_map/ppermute | solution.py:242
  7.1 1.6 %collective-permute-start.3 = (bf16[80,1024]{1,0:T(8,128)(2,1)S(1)}, bf16[80,1024]{1,0:T(8,128)(2,1)S(1)}, u32[]{:S(2)}, u32[]{:S(2)}) collective-permute-start(bf16[80,1024]{1,0:T(8,128)(2,1)S(1)} %get-tuple-element.24), channel_id=1, source_target_pairs={{0,4},{2,6},{4,0},{6,2},{8,12},{10,14},{12,8},{14,10},{1,5},{3,7},... | collective-permute-start | bytes 491528 | tf_op jit(solution)/shard_map/ppermute | solution.py:242
  8.6 1.5 %collective-permute-start.1 = (bf16[80,1024]{1,0:T(8,128)(2,1)S(1)}, bf16[80,1024]{1,0:T(8,128)(2,1)S(1)}, u32[]{:S(2)}, u32[]{:S(2)}) collective-permute-start(bf16[80,1024]{1,0:T(8,128)(2,1)S(1)} %get-tuple-element.23.refs_0_), channel_id=1, source_target_pairs={{0,2},{2,0},{1,3},{3,1},{4,6},{6,4},{5,7},{7,5},{8,10},{10,8},{9,1... | collective-permute-start | bytes 491528 | tf_op jit(solution)/shard_map/ppermute | solution.py:198
  10.4 5.7 %collective-permute-done.7.refs_8_ = bf16[80,1024]{1,0:T(8,128)(2,1)S(1)} collective-permute-done((bf16[80,1024]{1,0:T(8,128)(2,1)S(1)}, bf16[80,1024]{1,0:T(8,128)(2,1)S(1)}, u32[]{:S(2)}, u32[]{:S(2)}) %collective-permute-start.7) | collective-permute-done | bytes 163872 | tf_op jit(solution)/shard_map/ppermute | solution.py:242
  16.1 2.4 %collective-permute-start.9 = (bf16[80,1024]{1,0:T(8,128)(2,1)S(1)}, bf16[80,1024]{1,0:T(8,128)(2,1)S(1)}, u32[]{:S(2)}, u32[]{:S(2)}) collective-permute-start(bf16[80,1024]{1,0:T(8,128)(2,1)S(1)} %collective-permute-done.7.refs_8_), channel_id=1, source_target_pairs={{0,2},{2,0},{1,3},{3,1},{4,6},{6,4},{5,7},{7,5},{8,10},{10,8},{9,1... | collective-permute-start | bytes 491528 | tf_op jit(solution)/shard_map/ppermute | solution.py:198
  19.5 1.6 %collective-permute-start.14 = (bf16[80,1024]{1,0:T(8,128)(2,1)S(1)}, bf16[80,1024]{1,0:T(8,128)(2,1)S(1)}, u32[]{:S(2)}, u32[]{:S(2)}) collective-permute-start(bf16[80,1024]{1,0:T(8,128)(2,1)S(1)} %collective-permute-done.12.refs_0_), channel_id=1, source_target_pairs={{0,2},{2,0},{1,3},{3,1},{4,6},{6,4},{5,7},{7,5},{8,10},{10,8},{9,1... | collective-permute-start | bytes 491528 | tf_op jit(solution)/shard_map/ppermute | solution.py:198
  21.9 3.6 %collective-permute-done.5.refs_6_ = bf16[80,1024]{1,0:T(8,128)(2,1)S(1)} collective-permute-done((bf16[80,1024]{1,0:T(8,128)(2,1)S(1)}, bf16[80,1024]{1,0:T(8,128)(2,1)S(1)}, u32[]{:S(2)}, u32[]{:S(2)}) %collective-permute-start.5) | collective-permute-done | bytes 163872 | tf_op jit(solution)/shard_map/ppermute | solution.py:198
  26.1 1.2 %collective-permute-done.14.refs_2_ = bf16[80,1024]{1,0:T(8,128)(2,1)S(1)} collective-permute-done((bf16[80,1024]{1,0:T(8,128)(2,1)S(1)}, bf16[80,1024]{1,0:T(8,128)(2,1)S(1)}, u32[]{:S(2)}, u32[]{:S(2)}) %collective-permute-start.14) | collective-permute-done | bytes 163872 | tf_op jit(solution)/shard_map/ppermute | solution.py:198
  27.3 1.5 %near.1 = (bf16[4,96,4096]{2,1,0:T(8,128)(2,1)S(1)}, f32[2,64]{1,0:T(2,128)S(1)}) custom-call(s32[3]{0:T(128)S(1)} %pad_add_fusion.pos_ref, bf16[80,1024]{1,0:T(8,128)(2,1)S(1)} %get-tuple-element.23.refs_0_, bf16[80,1024]{1,0:T(8,128)(2,1)S(1)} %collective-permute-done.refs_1_, bf16[80,1024]{1,0:T(8,128)(2,1)S(1)} %collective-permute-done.1.refs_2_, ...), custom_call_target="tpu_custom_call" | custom-call | flops 1000000000 | tf_op jit(solution)/shard_map/near/pallas_call | solution.py:231
  28.9 3.5 %hidden_a.1 = (bf16[160,384]{1,0:T(8,128)(2,1)S(1)}, bf16[2,32,4096]{2,1,0:T(8,128)(2,1)S(1)}) custom-call(s32[3]{0:T(128)S(1)} %pad_add_fusion.pos_ref, bf16[80,1024]{1,0:T(8,128)(2,1)S(1)} %collective-permute-done.12.refs_0_, bf16[80,1024]{1,0:T(8,128)(2,1)S(1)} %collective-permute-done.13.refs_1_, bf16[80,1024]{1,0:T(8,128)(2,1)S(1)} %collective-permute-done.14.refs_2_, ...), custom_call_target="tpu_custom_call" | custom-call | flops 10000000000 | tf_op jit(solution)/shard_map/hidden_a/pallas_call | solution.py:231
  32.4 1.9 %collective-permute-start.19 = (bf16[160,384]{1,0:T(8,128)(2,1)S(1)}, bf16[160,384]{1,0:T(8,128)(2,1)S(1)}, u32[]{:S(2)}, u32[]{:S(2)}) collective-permute-start(bf16[160,384]{1,0:T(8,128)(2,1)S(1)} %get-tuple-element.30.own), channel_id=1, source_target_pairs={{0,2},{2,0},{1,3},{3,1},{4,6},{6,4},{5,7},{7,5},{8,10},{10,8},{9,1... | collective-permute-start | bytes 368648 | tf_op jit(solution)/shard_map/ppermute | solution.py:198
  34.3 3.2 %hidden_b.1.own = bf16[160,384]{1,0:T(8,128)(2,1)S(1)} custom-call(s32[3]{0:T(128)S(1)} %pad_add_fusion.pos_ref, bf16[4,96,4096]{2,1,0:T(8,128)(2,1)S(1)} %get-tuple-element.27.refs_4_.near, bf16[2,32,4096]{2,1,0:T(8,128)(2,1)S(1)} %get-tuple-element.29.far, bf16[4,4096,384]{2,1,0:T(8,128)(2,1)S(1)} %copy-done, bf16[4,4096,384]{2,1,0:T(8,128)(2,1)S(1)} %copy-done.1), custom_call_target="tpu_custom_call" | custom-call | flops 10000000000 | tf_op jit(solution)/shard_map/hidden_b/pallas_call | solution.py:231
  38.8 4.2 %collective-permute-done.16.x = bf16[160,384]{1,0:T(8,128)(2,1)S(1)} collective-permute-done((bf16[160,384]{1,0:T(8,128)(2,1)S(1)}, bf16[160,384]{1,0:T(8,128)(2,1)S(1)}, u32[]{:S(2)}, u32[]{:S(2)}) %collective-permute-start.16) | collective-permute-done | bytes 122912 | tf_op jit(solution)/shard_map/ppermute | solution.py:198
  43.1 1.8 %down_a.1.before = bf16[160,1024]{1,0:T(8,128)(2,1)S(1)} custom-call(s32[3]{0:T(128)S(1)} %pad_add_fusion.pos_ref, bf16[160,384]{1,0:T(8,128)(2,1)S(1)} %get-tuple-element.30.own, bf16[160,384]{1,0:T(8,128)(2,1)S(1)} %collective-permute-done.19.x, bf16[160,384]{1,0:T(8,128)(2,1)S(1)} %collective-permute-done.20.core, ...), custom_call_target="tpu_custom_call" | custom-call | flops 10000000000 | tf_op jit(solution)/shard_map/down_a/pallas_call | solution.py:231
  45.0 2.8 %down_b.1 = (bf16[80,512]{1,0:T(8,128)(2,1)S(1)}, bf16[80,512]{1,0:T(8,128)(2,1)S(1)}, bf16[80,512]{1,0:T(8,128)(2,1)S(1)}, bf16[80,512]{1,0:T(8,128)(2,1)S(1)},...) custom-call(s32[3]{0:T(128)S(1)} %pad_add_fusion.pos_ref, ...), custom_call_target="tpu_custom_call" | custom-call | flops 10000000000 | tf_op jit(solution)/shard_map/down_b/pallas_call | solution.py:231
  47.8 4.8 %collective-permute-start.22 = (bf16[80,512]{1,0:T(8,128)(2,1)S(1)}, bf16[80,512]{1,0:T(8,128)(2,1)S(1)}, u32[]{:S(2)}, u32[]{:S(2)}) collective-permute-start(bf16[80,512]{1,0:T(8,128)(2,1)S(1)} %get-tuple-element.32), channel_id=1, source_target_pairs={{0,14},{2,12},{4,10},{6,8},{8,6},{10,4},{12,2},{14,0},{1,15},{3,13... | collective-permute-start | bytes 245768 | tf_op jit(solution)/shard_map/ppermute | solution.py:242
  52.6 1.6 %collective-permute-start.24 = (bf16[80,512]{1,0:T(8,128)(2,1)S(1)}, bf16[80,512]{1,0:T(8,128)(2,1)S(1)}, u32[]{:S(2)}, u32[]{:S(2)}) collective-permute-start(bf16[80,512]{1,0:T(8,128)(2,1)S(1)} %get-tuple-element.34), channel_id=1, source_target_pairs={{0,6},{2,4},{4,2},{6,0},{8,14},{10,12},{12,10},{14,8},{1,7},{3,5},... | collective-permute-start | bytes 245768 | tf_op jit(solution)/shard_map/ppermute | solution.py:242
  54.7 4.7 %collective-permute-start.26 = (bf16[80,512]{1,0:T(8,128)(2,1)S(1)}, bf16[80,512]{1,0:T(8,128)(2,1)S(1)}, u32[]{:S(2)}, u32[]{:S(2)}) collective-permute-start(bf16[80,512]{1,0:T(8,128)(2,1)S(1)} %get-tuple-element.36), channel_id=1, source_target_pairs={{0,12},{2,14},{4,8},{6,10},{8,4},{10,6},{12,0},{14,2},{1,13},{3,15... | collective-permute-start | bytes 245768 | tf_op jit(solution)/shard_map/ppermute | solution.py:242
  60.2 1.1 %collective-permute-start.28 = (bf16[80,512]{1,0:T(8,128)(2,1)S(1)}, bf16[80,512]{1,0:T(8,128)(2,1)S(1)}, u32[]{:S(2)}, u32[]{:S(2)}) collective-permute-start(bf16[80,512]{1,0:T(8,128)(2,1)S(1)} %get-tuple-element.38), channel_id=1, source_target_pairs={{0,4},{2,6},{4,0},{6,2},{8,12},{10,14},{12,8},{14,10},{1,5},{3,7},... | collective-permute-start | bytes 245768 | tf_op jit(solution)/shard_map/ppermute | solution.py:242
  61.6 1.3 %collective-permute-done.26.refs_5_ = bf16[80,512]{1,0:T(8,128)(2,1)S(1)} collective-permute-done((bf16[80,512]{1,0:T(8,128)(2,1)S(1)}, bf16[80,512]{1,0:T(8,128)(2,1)S(1)}, u32[]{:S(2)}, u32[]{:S(2)}) %collective-permute-start.26) | collective-permute-done | bytes 81952 | tf_op jit(solution)/shard_map/ppermute | solution.py:242
  62.9 3.5 %collective-permute-done.27.refs_6_ = bf16[80,512]{1,0:T(8,128)(2,1)S(1)} collective-permute-done((bf16[80,512]{1,0:T(8,128)(2,1)S(1)}, bf16[80,512]{1,0:T(8,128)(2,1)S(1)}, u32[]{:S(2)}, u32[]{:S(2)}) %collective-permute-start.27) | collective-permute-done | bytes 81952 | tf_op jit(solution)/shard_map/ppermute | solution.py:242
  67.5 1.5 %collective-permute-done.29.other = bf16[64,2048]{1,0:T(8,128)(2,1)S(1)} collective-permute-done((bf16[64,2048]{1,0:T(8,128)(2,1)S(1)}, bf16[64,2048]{1,0:T(8,128)(2,1)S(1)}, u32[]{:S(2)}, u32[]{:S(2)}) %collective-permute-start.29) | collective-permute-done | bytes 262176 | tf_op jit(solution)/shard_map/ppermute | solution.py:198
  69.0 1.4 %join.1 = bf16[64,4096]{1,0:T(8,128)(2,1)} custom-call(s32[3]{0:T(128)S(1)} %pad_add_fusion.pos_ref, bf16[64,2048]{1,0:T(8,128)(2,1)S(1)} %get-tuple-element.39.mine, bf16[64,2048]{1,0:T(8,128)(2,1)S(1)} %collective-permute-done.29.other), custom_call_target="tpu_custom_call" | custom-call | flops 1000000000 | tf_op jit(solution)/shard_map/join/pallas_call | solution.py:231
  (62 shorter events, 8.3 us)
Async XLA Ops:
  3.0 13.1 %collective-permute-start.7 = (bf16[80,1024]{1,0:T(8,128)(2,1)S(1)}, bf16[80,1024]{1,0:T(8,128)(2,1)S(1)}, u32[]{:S(2)}, u32[]{:S(2)}) collective-permute-start(bf16[80,1024]{1,0:T(8,128)(2,1)S(1)} %get-tuple-element.25), channel_id=1, source_target_pairs={{0,8},{2,10},{4,12},{6,14},{8,0},{10,2},{12,4},{14,6},{1,9},{3,11}... | collective-permute-start | bytes 491528 | tf_op jit(solution)/shard_map/ppermute | solution.py:242
  7.1 11.5 %collective-permute-start.3 = (bf16[80,1024]{1,0:T(8,128)(2,1)S(1)}, bf16[80,1024]{1,0:T(8,128)(2,1)S(1)}, u32[]{:S(2)}, u32[]{:S(2)}) collective-permute-start(bf16[80,1024]{1,0:T(8,128)(2,1)S(1)} %get-tuple-element.24), channel_id=1, source_target_pairs={{0,4},{2,6},{4,0},{6,2},{8,12},{10,14},{12,8},{14,10},{1,5},{3,7},... | collective-permute-start | bytes 491528 | tf_op jit(solution)/shard_map/ppermute | solution.py:242
  8.6 9.9 %collective-permute-start.1 = (bf16[80,1024]{1,0:T(8,128)(2,1)S(1)}, bf16[80,1024]{1,0:T(8,128)(2,1)S(1)}, u32[]{:S(2)}, u32[]{:S(2)}) collective-permute-start(bf16[80,1024]{1,0:T(8,128)(2,1)S(1)} %get-tuple-element.23.refs_0_), channel_id=1, source_target_pairs={{0,2},{2,0},{1,3},{3,1},{4,6},{6,4},{5,7},{7,5},{8,10},{10,8},{9,1... | collective-permute-start | bytes 491528 | tf_op jit(solution)/shard_map/ppermute | solution.py:198
  10.1 8.5 %collective-permute-start = (bf16[80,1024]{1,0:T(8,128)(2,1)S(1)}, bf16[80,1024]{1,0:T(8,128)(2,1)S(1)}, u32[]{:S(2)}, u32[]{:S(2)}) collective-permute-start(bf16[80,1024]{1,0:T(8,128)(2,1)S(1)} %get-tuple-element.23.refs_0_), channel_id=1, source_target_pairs={{0,1},{1,0},{2,3},{3,2},{4,5},{5,4},{6,7},{7,6},{8,9},{9,8},{10,11... | collective-permute-start | bytes 491528 | tf_op jit(solution)/shard_map/ppermute | solution.py:198
  10.1 9.4 %collective-permute-start.12 = (bf16[80,1024]{1,0:T(8,128)(2,1)S(1)}, bf16[80,1024]{1,0:T(8,128)(2,1)S(1)}, u32[]{:S(2)}, u32[]{:S(2)}) collective-permute-start(bf16[80,1024]{1,0:T(8,128)(2,1)S(1)} %get-tuple-element.28), channel_id=1, source_target_pairs={{0,12},{2,14},{4,8},{6,10},{8,4},{10,6},{12,0},{14,2},{1,13},{3,15... | collective-permute-start | bytes 491528 | tf_op jit(solution)/shard_map/ppermute | solution.py:242
  16.1 5.8 %collective-permute-start.9 = (bf16[80,1024]{1,0:T(8,128)(2,1)S(1)}, bf16[80,1024]{1,0:T(8,128)(2,1)S(1)}, u32[]{:S(2)}, u32[]{:S(2)}) collective-permute-start(bf16[80,1024]{1,0:T(8,128)(2,1)S(1)} %collective-permute-done.7.refs_8_), channel_id=1, source_target_pairs={{0,2},{2,0},{1,3},{3,1},{4,6},{6,4},{5,7},{7,5},{8,10},{10,8},{9,1... | collective-permute-start | bytes 491528 | tf_op jit(solution)/shard_map/ppermute | solution.py:198
  18.6 7.0 %collective-permute-start.5 = (bf16[80,1024]{1,0:T(8,128)(2,1)S(1)}, bf16[80,1024]{1,0:T(8,128)(2,1)S(1)}, u32[]{:S(2)}, u32[]{:S(2)}) collective-permute-start(bf16[80,1024]{1,0:T(8,128)(2,1)S(1)} %collective-permute-done.3.refs_4_), channel_id=1, source_target_pairs={{0,2},{2,0},{1,3},{3,1},{4,6},{6,4},{5,7},{7,5},{8,10},{10,8},{9,1... | collective-permute-start | bytes 491528 | tf_op jit(solution)/shard_map/ppermute | solution.py:198
  18.6 7.0 %collective-permute-start.2 = (bf16[80,1024]{1,0:T(8,128)(2,1)S(1)}, bf16[80,1024]{1,0:T(8,128)(2,1)S(1)}, u32[]{:S(2)}, u32[]{:S(2)}) collective-permute-start(bf16[80,1024]{1,0:T(8,128)(2,1)S(1)} %collective-permute-done.1.refs_2_), channel_id=1, source_target_pairs={{0,1},{1,0},{2,3},{3,2},{4,5},{5,4},{6,7},{7,6},{8,9},{9,8},{10,11... | collective-permute-start | bytes 491528 | tf_op jit(solution)/shard_map/ppermute | solution.py:198
  18.7 7.4 %collective-permute-start.4 = (bf16[80,1024]{1,0:T(8,128)(2,1)S(1)}, bf16[80,1024]{1,0:T(8,128)(2,1)S(1)}, u32[]{:S(2)}, u32[]{:S(2)}) collective-permute-start(bf16[80,1024]{1,0:T(8,128)(2,1)S(1)} %collective-permute-done.3.refs_4_), channel_id=1, source_target_pairs={{0,1},{1,0},{2,3},{3,2},{4,5},{5,4},{6,7},{7,6},{8,9},{9,8},{10,11... | collective-permute-start | bytes 491528 | tf_op jit(solution)/shard_map/ppermute | solution.py:198
  19.5 7.8 %collective-permute-start.14 = (bf16[80,1024]{1,0:T(8,128)(2,1)S(1)}, bf16[80,1024]{1,0:T(8,128)(2,1)S(1)}, u32[]{:S(2)}, u32[]{:S(2)}) collective-permute-start(bf16[80,1024]{1,0:T(8,128)(2,1)S(1)} %collective-permute-done.12.refs_0_), channel_id=1, source_target_pairs={{0,2},{2,0},{1,3},{3,1},{4,6},{6,4},{5,7},{7,5},{8,10},{10,8},{9,1... | collective-permute-start | bytes 491528 | tf_op jit(solution)/shard_map/ppermute | solution.py:198
  21.9 5.4 %collective-permute-start.8 = (bf16[80,1024]{1,0:T(8,128)(2,1)S(1)}, bf16[80,1024]{1,0:T(8,128)(2,1)S(1)}, u32[]{:S(2)}, u32[]{:S(2)}) collective-permute-start(bf16[80,1024]{1,0:T(8,128)(2,1)S(1)} %collective-permute-done.7.refs_8_), channel_id=1, source_target_pairs={{0,1},{1,0},{2,3},{3,2},{4,5},{5,4},{6,7},{7,6},{8,9},{9,8},{10,11... | collective-permute-start | bytes 491528 | tf_op jit(solution)/shard_map/ppermute | solution.py:198
  32.4 5.9 %collective-permute-start.19 = (bf16[160,384]{1,0:T(8,128)(2,1)S(1)}, bf16[160,384]{1,0:T(8,128)(2,1)S(1)}, u32[]{:S(2)}, u32[]{:S(2)}) collective-permute-start(bf16[160,384]{1,0:T(8,128)(2,1)S(1)} %get-tuple-element.30.own), channel_id=1, source_target_pairs={{0,2},{2,0},{1,3},{3,1},{4,6},{6,4},{5,7},{7,5},{8,10},{10,8},{9,1... | collective-permute-start | bytes 368648 | tf_op jit(solution)/shard_map/ppermute | solution.py:198
  37.6 5.5 %collective-permute-start.16 = (bf16[160,384]{1,0:T(8,128)(2,1)S(1)}, bf16[160,384]{1,0:T(8,128)(2,1)S(1)}, u32[]{:S(2)}, u32[]{:S(2)}) collective-permute-start(bf16[160,384]{1,0:T(8,128)(2,1)S(1)} %hidden_b.1.own), channel_id=1, source_target_pairs={{0,2},{2,0},{1,3},{3,1},{4,6},{6,4},{5,7},{7,5},{8,10},{10,8},{9,1... | collective-permute-start | bytes 368648 | tf_op jit(solution)/shard_map/ppermute | solution.py:198
  37.8 5.3 %collective-permute-start.20 = (bf16[160,384]{1,0:T(8,128)(2,1)S(1)}, bf16[160,384]{1,0:T(8,128)(2,1)S(1)}, u32[]{:S(2)}, u32[]{:S(2)}) collective-permute-start(bf16[160,384]{1,0:T(8,128)(2,1)S(1)} %get-tuple-element.30.own), channel_id=1, source_target_pairs={{0,1},{1,0},{2,3},{3,2},{4,5},{5,4},{6,7},{7,6},{8,9},{9,8},{10,11... | collective-permute-start | bytes 368648 | tf_op jit(solution)/shard_map/ppermute | solution.py:198
  38.3 4.8 %collective-permute-start.21 = (bf16[160,384]{1,0:T(8,128)(2,1)S(1)}, bf16[160,384]{1,0:T(8,128)(2,1)S(1)}, u32[]{:S(2)}, u32[]{:S(2)}) collective-permute-start(bf16[160,384]{1,0:T(8,128)(2,1)S(1)} %collective-permute-done.19.x), channel_id=1, source_target_pairs={{0,1},{1,0},{2,3},{3,2},{4,5},{5,4},{6,7},{7,6},{8,9},{9,8},{10,11... | collective-permute-start | bytes 368648 | tf_op jit(solution)/shard_map/ppermute | solution.py:198
  38.3 4.7 %collective-permute-start.11 = (f32[2,64]{1,0:T(2,128)S(1)}, f32[2,64]{1,0:T(2,128)S(1)}, u32[]{:S(2)}, u32[]{:S(2)}) collective-permute-start(f32[2,64]{1,0:T(2,128)S(1)} %get-tuple-element.26.own), channel_id=1, source_target_pairs={{0,1},{1,0},{2,3},{3,2},{4,5},{5,4},{6,7},{7,6},{8,9},{9,8},{10,11... | collective-permute-start | bytes 1544 | tf_op jit(solution)/shard_map/ppermute | solution.py:198
  38.8 6.1 %collective-permute-start.17 = (bf16[160,384]{1,0:T(8,128)(2,1)S(1)}, bf16[160,384]{1,0:T(8,128)(2,1)S(1)}, u32[]{:S(2)}, u32[]{:S(2)}) collective-permute-start(bf16[160,384]{1,0:T(8,128)(2,1)S(1)} %hidden_b.1.own), channel_id=1, source_target_pairs={{0,1},{1,0},{2,3},{3,2},{4,5},{5,4},{6,7},{7,6},{8,9},{9,8},{10,11... | collective-permute-start | bytes 368648 | tf_op jit(solution)/shard_map/ppermute | solution.py:198
  47.8 11.6 %collective-permute-start.22 = (bf16[80,512]{1,0:T(8,128)(2,1)S(1)}, bf16[80,512]{1,0:T(8,128)(2,1)S(1)}, u32[]{:S(2)}, u32[]{:S(2)}) collective-permute-start(bf16[80,512]{1,0:T(8,128)(2,1)S(1)} %get-tuple-element.32), channel_id=1, source_target_pairs={{0,14},{2,12},{4,10},{6,8},{8,6},{10,4},{12,2},{14,0},{1,15},{3,13... | collective-permute-start | bytes 245768 | tf_op jit(solution)/shard_map/ppermute | solution.py:242
  52.6 7.6 %collective-permute-start.23 = (bf16[80,512]{1,0:T(8,128)(2,1)S(1)}, bf16[80,512]{1,0:T(8,128)(2,1)S(1)}, u32[]{:S(2)}, u32[]{:S(2)}) collective-permute-start(bf16[80,512]{1,0:T(8,128)(2,1)S(1)} %get-tuple-element.33), channel_id=1, source_target_pairs={{0,10},{2,8},{4,14},{6,12},{8,2},{10,0},{12,6},{14,4},{1,11},{3,9}... | collective-permute-start | bytes 245768 | tf_op jit(solution)/shard_map/ppermute | solution.py:242
  52.6 8.7 %collective-permute-start.24 = (bf16[80,512]{1,0:T(8,128)(2,1)S(1)}, bf16[80,512]{1,0:T(8,128)(2,1)S(1)}, u32[]{:S(2)}, u32[]{:S(2)}) collective-permute-start(bf16[80,512]{1,0:T(8,128)(2,1)S(1)} %get-tuple-element.34), channel_id=1, source_target_pairs={{0,6},{2,4},{4,2},{6,0},{8,14},{10,12},{12,10},{14,8},{1,7},{3,5},... | collective-permute-start | bytes 245768 | tf_op jit(solution)/shard_map/ppermute | solution.py:242
  54.2 7.4 %collective-permute-start.25 = (bf16[80,512]{1,0:T(8,128)(2,1)S(1)}, bf16[80,512]{1,0:T(8,128)(2,1)S(1)}, u32[]{:S(2)}, u32[]{:S(2)}) collective-permute-start(bf16[80,512]{1,0:T(8,128)(2,1)S(1)} %get-tuple-element.35), channel_id=1, source_target_pairs={{0,2},{2,0},{4,6},{6,4},{8,10},{10,8},{12,14},{14,12},{1,3},{3,1},... | collective-permute-start | bytes 245768 | tf_op jit(solution)/shard_map/ppermute | solution.py:242
  54.7 8.2 %collective-permute-start.26 = (bf16[80,512]{1,0:T(8,128)(2,1)S(1)}, bf16[80,512]{1,0:T(8,128)(2,1)S(1)}, u32[]{:S(2)}, u32[]{:S(2)}) collective-permute-start(bf16[80,512]{1,0:T(8,128)(2,1)S(1)} %get-tuple-element.36), channel_id=1, source_target_pairs={{0,12},{2,14},{4,8},{6,10},{8,4},{10,6},{12,0},{14,2},{1,13},{3,15... | collective-permute-start | bytes 245768 | tf_op jit(solution)/shard_map/ppermute | solution.py:242
  59.4 7.0 %collective-permute-start.27 = (bf16[80,512]{1,0:T(8,128)(2,1)S(1)}, bf16[80,512]{1,0:T(8,128)(2,1)S(1)}, u32[]{:S(2)}, u32[]{:S(2)}) collective-permute-start(bf16[80,512]{1,0:T(8,128)(2,1)S(1)} %get-tuple-element.37), channel_id=1, source_target_pairs={{0,8},{2,10},{4,12},{6,14},{8,0},{10,2},{12,4},{14,6},{1,9},{3,11}... | collective-permute-start | bytes 245768 | tf_op jit(solution)/shard_map/ppermute | solution.py:242
  60.2 6.2 %collective-permute-start.28 = (bf16[80,512]{1,0:T(8,128)(2,1)S(1)}, bf16[80,512]{1,0:T(8,128)(2,1)S(1)}, u32[]{:S(2)}, u32[]{:S(2)}) collective-permute-start(bf16[80,512]{1,0:T(8,128)(2,1)S(1)} %get-tuple-element.38), channel_id=1, source_target_pairs={{0,4},{2,6},{4,0},{6,2},{8,12},{10,14},{12,8},{14,10},{1,5},{3,7},... | collective-permute-start | bytes 245768 | tf_op jit(solution)/shard_map/ppermute | solution.py:242
  (14 other events, 130.1 us)

commit v5 on v4

--- a/solution.py
+++ b/solution.py
@@ -7,7 +7,7 @@
 from jax.sharding import PartitionSpec as P
 
 BIG = 4096
-ORDER = (0, 7, 5, 3, 1, 6, 4, 2)
+ORDER = (0, 4, 1, 5, 3, 6, 7, 2)
 LEAD = 20 * 10**9
 STEP = 10 * 10**9
 VMEM_LIMIT = 8 * 1024 * 1024
@@ -212,7 +212,7 @@
     cfg.rp = cfg.rows * cfg.nd
     cfg.sources = cfg.groups * 4
     cfg.early = 3
-    cfg.visits = (0, 1, 2, 3)
+    cfg.visits = (0, 1, 3, 2)
     f = gate_weight.shape[2]
     ff, wide = down_weight.shape[1:]
     per = cfg.sources * cfg.cap

time: 70.6 us -> 68.1 us (0.965)
  starting transfers between devices: 28.2 us -> 26.1 us
    ppermute x20, waiting for transfers between devices: 11.8 us -> 8.64 us  [swap(): return lax.ppermute(x, axis, [(0, 1), (1, 0)])]
    ppermute x10, starting transfers between devices: 18.7 us -> 15.6 us  [move(): lax.ppermute(x, ('expert', 'context'), [(i * 2 + k, (i ^ r) * 2 + (k ^ dc...]
    ppermute x10, waiting for transfers between devices: 11.9 us -> 14.8 us  [move(): lax.ppermute(x, ('expert', 'context'), [(i * 2 + k, (i ^ r) * 2 + (k ^ dc...]
    ppermute x20, starting transfers between devices: 9.56 us -> 10.5 us  [swap(): return lax.ppermute(x, axis, [(0, 1), (1, 0)])]
  transfers between devices with their start and end apart: 30 -> 30, of which waited for: 12 -> 11; matrix products, arithmetic and copies ran while one was open for 0% -> 0% of each run, Pallas kernels for 9% -> 10%
where the time goes in v5:
time: 68.1 us; the launch traced here: 68 us
  starting transfers between devices  26.1 us (38%)
  waiting for transfers between devices  23.5 us (35%)
  Pallas kernels  16.4 us (24%)
  local copies, waits for them, and re-layouts  1.72 us (3%)
    pallas_call x8, Pallas kernels, call(): pl.pallas_call(kernel, in_specs=[smem] + [vmem] * len(ins), out_specs=[vm...  16.4 us
    ppermute x10, starting transfers between devices, move(): lax.ppermute(x, ('expert', 'context'), [(i * 2 + k, (i ^ r) * 2 + (k ^ dc...  15.6 us
    ppermute x10, waiting for transfers between devices, move(): lax.ppermute(x, ('expert', 'context'), [(i * 2 + k, (i ^ r) * 2 + (k ^ dc...  14.8 us
    ppermute x20, starting transfers between devices, swap(): return lax.ppermute(x, axis, [(0, 1), (1, 0)])  10.5 us
    ppermute x20, waiting for transfers between devices, swap(): return lax.ppermute(x, axis, [(0, 1), (1, 0)])  8.64 us
    unnamed x16, local copies, waits for them, and re-layouts  1.72 us
  transfers between devices with their start and end apart: 30, of which 11 were waited for; matrix products, arithmetic and copies ran while one was open for 0% of the time, Pallas kernels for 10%

profile of v5, /device:TPU:0, one launch (start us, length us, event | category | flops | bytes accessed | tf_op | source)
XLA Modules:
  0.0 68.0 jit_solution(9428639648624648050)
XLA Ops:
  3.0 5.1 %collective-permute-start.7 = (bf16[80,1024]{1,0:T(8,128)(2,1)S(1)}, bf16[80,1024]{1,0:T(8,128)(2,1)S(1)}, u32[]{:S(2)}, u32[]{:S(2)}) collective-permute-start(bf16[80,1024]{1,0:T(8,128)(2,1)S(1)} %get-tuple-element.25), channel_id=1, source_target_pairs={{0,12},{2,14},{4,8},{6,10},{8,4},{10,6},{12,0},{14,2},{1,13},{3,15... | collective-permute-start | bytes 491528 | tf_op jit(solution)/shard_map/ppermute | solution.py:242
  8.1 1.5 %collective-permute-start.1 = (bf16[80,1024]{1,0:T(8,128)(2,1)S(1)}, bf16[80,1024]{1,0:T(8,128)(2,1)S(1)}, u32[]{:S(2)}, u32[]{:S(2)}) collective-permute-start(bf16[80,1024]{1,0:T(8,128)(2,1)S(1)} %get-tuple-element.23.refs_0_), channel_id=1, source_target_pairs={{0,2},{2,0},{1,3},{3,1},{4,6},{6,4},{5,7},{7,5},{8,10},{10,8},{9,1... | collective-permute-start | bytes 491528 | tf_op jit(solution)/shard_map/ppermute | solution.py:198
  10.4 2.8 %collective-permute-done.7.refs_8_ = bf16[80,1024]{1,0:T(8,128)(2,1)S(1)} collective-permute-done((bf16[80,1024]{1,0:T(8,128)(2,1)S(1)}, bf16[80,1024]{1,0:T(8,128)(2,1)S(1)}, u32[]{:S(2)}, u32[]{:S(2)}) %collective-permute-start.7) | collective-permute-done | bytes 163872 | tf_op jit(solution)/shard_map/ppermute | solution.py:242
  13.2 1.7 %collective-permute-start.9 = (bf16[80,1024]{1,0:T(8,128)(2,1)S(1)}, bf16[80,1024]{1,0:T(8,128)(2,1)S(1)}, u32[]{:S(2)}, u32[]{:S(2)}) collective-permute-start(bf16[80,1024]{1,0:T(8,128)(2,1)S(1)} %collective-permute-done.7.refs_8_), channel_id=1, source_target_pairs={{0,2},{2,0},{1,3},{3,1},{4,6},{6,4},{5,7},{7,5},{8,10},{10,8},{9,1... | collective-permute-start | bytes 491528 | tf_op jit(solution)/shard_map/ppermute | solution.py:198
  14.8 2.0 %collective-permute-done.3.refs_4_ = bf16[80,1024]{1,0:T(8,128)(2,1)S(1)} collective-permute-done((bf16[80,1024]{1,0:T(8,128)(2,1)S(1)}, bf16[80,1024]{1,0:T(8,128)(2,1)S(1)}, u32[]{:S(2)}, u32[]{:S(2)}) %collective-permute-start.3) | collective-permute-done | bytes 163872 | tf_op jit(solution)/shard_map/ppermute | solution.py:242
  16.9 1.4 %collective-permute-start.5 = (bf16[80,1024]{1,0:T(8,128)(2,1)S(1)}, bf16[80,1024]{1,0:T(8,128)(2,1)S(1)}, u32[]{:S(2)}, u32[]{:S(2)}) collective-permute-start(bf16[80,1024]{1,0:T(8,128)(2,1)S(1)} %collective-permute-done.3.refs_4_), channel_id=1, source_target_pairs={{0,2},{2,0},{1,3},{3,1},{4,6},{6,4},{5,7},{7,5},{8,10},{10,8},{9,1... | collective-permute-start | bytes 491528 | tf_op jit(solution)/shard_map/ppermute | solution.py:198
  18.8 3.2 %collective-permute-done.12.refs_0_ = bf16[80,1024]{1,0:T(8,128)(2,1)S(1)} collective-permute-done((bf16[80,1024]{1,0:T(8,128)(2,1)S(1)}, bf16[80,1024]{1,0:T(8,128)(2,1)S(1)}, u32[]{:S(2)}, u32[]{:S(2)}) %collective-permute-start.12) | collective-permute-done | bytes 163872 | tf_op jit(solution)/shard_map/ppermute | solution.py:242
  22.0 1.5 %collective-permute-start.14 = (bf16[80,1024]{1,0:T(8,128)(2,1)S(1)}, bf16[80,1024]{1,0:T(8,128)(2,1)S(1)}, u32[]{:S(2)}, u32[]{:S(2)}) collective-permute-start(bf16[80,1024]{1,0:T(8,128)(2,1)S(1)} %collective-permute-done.12.refs_0_), channel_id=1, source_target_pairs={{0,2},{2,0},{1,3},{3,1},{4,6},{6,4},{5,7},{7,5},{8,10},{10,8},{9,1... | collective-permute-start | bytes 491528 | tf_op jit(solution)/shard_map/ppermute | solution.py:198
  24.5 2.8 %collective-permute-done.14.refs_2_ = bf16[80,1024]{1,0:T(8,128)(2,1)S(1)} collective-permute-done((bf16[80,1024]{1,0:T(8,128)(2,1)S(1)}, bf16[80,1024]{1,0:T(8,128)(2,1)S(1)}, u32[]{:S(2)}, u32[]{:S(2)}) %collective-permute-start.14) | collective-permute-done | bytes 163872 | tf_op jit(solution)/shard_map/ppermute | solution.py:198
  27.3 1.5 %near.1 = (bf16[4,96,4096]{2,1,0:T(8,128)(2,1)S(1)}, f32[2,64]{1,0:T(2,128)S(1)}) custom-call(s32[3]{0:T(128)S(1)} %pad_add_fusion.pos_ref, bf16[80,1024]{1,0:T(8,128)(2,1)S(1)} %get-tuple-element.23.refs_0_, bf16[80,1024]{1,0:T(8,128)(2,1)S(1)} %collective-permute-done.refs_1_, bf16[80,1024]{1,0:T(8,128)(2,1)S(1)} %collective-permute-done.1.refs_2_, ...), custom_call_target="tpu_custom_call" | custom-call | flops 1000000000 | tf_op jit(solution)/shard_map/near/pallas_call | solution.py:231
  28.9 3.5 %hidden_a.1 = (bf16[160,384]{1,0:T(8,128)(2,1)S(1)}, bf16[2,32,4096]{2,1,0:T(8,128)(2,1)S(1)}) custom-call(s32[3]{0:T(128)S(1)} %pad_add_fusion.pos_ref, bf16[80,1024]{1,0:T(8,128)(2,1)S(1)} %collective-permute-done.12.refs_0_, bf16[80,1024]{1,0:T(8,128)(2,1)S(1)} %collective-permute-done.13.refs_1_, bf16[80,1024]{1,0:T(8,128)(2,1)S(1)} %collective-permute-done.14.refs_2_, ...), custom_call_target="tpu_custom_call" | custom-call | flops 10000000000 | tf_op jit(solution)/shard_map/hidden_a/pallas_call | solution.py:231
  32.4 1.6 %collective-permute-start.19 = (bf16[160,384]{1,0:T(8,128)(2,1)S(1)}, bf16[160,384]{1,0:T(8,128)(2,1)S(1)}, u32[]{:S(2)}, u32[]{:S(2)}) collective-permute-start(bf16[160,384]{1,0:T(8,128)(2,1)S(1)} %get-tuple-element.30.own), channel_id=1, source_target_pairs={{0,2},{2,0},{1,3},{3,1},{4,6},{6,4},{5,7},{7,5},{8,10},{10,8},{9,1... | collective-permute-start | bytes 368648 | tf_op jit(solution)/shard_map/ppermute | solution.py:198
  34.0 3.2 %hidden_b.1.own = bf16[160,384]{1,0:T(8,128)(2,1)S(1)} custom-call(s32[3]{0:T(128)S(1)} %pad_add_fusion.pos_ref, bf16[4,96,4096]{2,1,0:T(8,128)(2,1)S(1)} %get-tuple-element.27.refs_4_.near, bf16[2,32,4096]{2,1,0:T(8,128)(2,1)S(1)} %get-tuple-element.29.far, bf16[4,4096,384]{2,1,0:T(8,128)(2,1)S(1)} %copy-done, bf16[4,4096,384]{2,1,0:T(8,128)(2,1)S(1)} %copy-done.1), custom_call_target="tpu_custom_call" | custom-call | flops 10000000000 | tf_op jit(solution)/shard_map/hidden_b/pallas_call | solution.py:231
  38.8 3.9 %collective-permute-done.16.x = bf16[160,384]{1,0:T(8,128)(2,1)S(1)} collective-permute-done((bf16[160,384]{1,0:T(8,128)(2,1)S(1)}, bf16[160,384]{1,0:T(8,128)(2,1)S(1)}, u32[]{:S(2)}, u32[]{:S(2)}) %collective-permute-start.16) | collective-permute-done | bytes 122912 | tf_op jit(solution)/shard_map/ppermute | solution.py:198
  42.8 1.8 %down_a.1.before = bf16[160,1024]{1,0:T(8,128)(2,1)S(1)} custom-call(s32[3]{0:T(128)S(1)} %pad_add_fusion.pos_ref, bf16[160,384]{1,0:T(8,128)(2,1)S(1)} %get-tuple-element.30.own, bf16[160,384]{1,0:T(8,128)(2,1)S(1)} %collective-permute-done.19.x, bf16[160,384]{1,0:T(8,128)(2,1)S(1)} %collective-permute-done.20.core, ...), custom_call_target="tpu_custom_call" | custom-call | flops 10000000000 | tf_op jit(solution)/shard_map/down_a/pallas_call | solution.py:231
  44.6 2.8 %down_b.1 = (bf16[80,512]{1,0:T(8,128)(2,1)S(1)}, bf16[80,512]{1,0:T(8,128)(2,1)S(1)}, bf16[80,512]{1,0:T(8,128)(2,1)S(1)}, bf16[80,512]{1,0:T(8,128)(2,1)S(1)},...) custom-call(s32[3]{0:T(128)S(1)} %pad_add_fusion.pos_ref, ...), custom_call_target="tpu_custom_call" | custom-call | flops 10000000000 | tf_op jit(solution)/shard_map/down_b/pallas_call | solution.py:231
  49.3 2.6 %collective-permute-start.24 = (bf16[80,512]{1,0:T(8,128)(2,1)S(1)}, bf16[80,512]{1,0:T(8,128)(2,1)S(1)}, u32[]{:S(2)}, u32[]{:S(2)}) collective-permute-start(bf16[80,512]{1,0:T(8,128)(2,1)S(1)} %get-tuple-element.34), channel_id=1, source_target_pairs={{0,10},{2,8},{4,14},{6,12},{8,2},{10,0},{12,6},{14,4},{1,11},{3,9}... | collective-permute-start | bytes 245768 | tf_op jit(solution)/shard_map/ppermute | solution.py:242
  52.5 2.0 %collective-permute-start.26 = (bf16[80,512]{1,0:T(8,128)(2,1)S(1)}, bf16[80,512]{1,0:T(8,128)(2,1)S(1)}, u32[]{:S(2)}, u32[]{:S(2)}) collective-permute-start(bf16[80,512]{1,0:T(8,128)(2,1)S(1)} %get-tuple-element.36), channel_id=1, source_target_pairs={{0,12},{2,14},{4,8},{6,10},{8,4},{10,6},{12,0},{14,2},{1,13},{3,15... | collective-permute-start | bytes 245768 | tf_op jit(solution)/shard_map/ppermute | solution.py:242
  54.6 1.8 %collective-permute-done.22.refs_1_ = bf16[80,512]{1,0:T(8,128)(2,1)S(1)} collective-permute-done((bf16[80,512]{1,0:T(8,128)(2,1)S(1)}, bf16[80,512]{1,0:T(8,128)(2,1)S(1)}, u32[]{:S(2)}, u32[]{:S(2)}) %collective-permute-start.22) | collective-permute-done | bytes 81952 | tf_op jit(solution)/shard_map/ppermute | solution.py:242
  56.4 2.5 %collective-permute-start.27 = (bf16[80,512]{1,0:T(8,128)(2,1)S(1)}, bf16[80,512]{1,0:T(8,128)(2,1)S(1)}, u32[]{:S(2)}, u32[]{:S(2)}) collective-permute-start(bf16[80,512]{1,0:T(8,128)(2,1)S(1)} %get-tuple-element.37), channel_id=1, source_target_pairs={{0,14},{2,12},{4,10},{6,8},{8,6},{10,4},{12,2},{14,0},{1,15},{3,13... | collective-permute-start | bytes 245768 | tf_op jit(solution)/shard_map/ppermute | solution.py:242
  58.9 2.4 %collective-permute-done.24.refs_3_ = bf16[80,512]{1,0:T(8,128)(2,1)S(1)} collective-permute-done((bf16[80,512]{1,0:T(8,128)(2,1)S(1)}, bf16[80,512]{1,0:T(8,128)(2,1)S(1)}, u32[]{:S(2)}, u32[]{:S(2)}) %collective-permute-start.24) | collective-permute-done | bytes 81952 | tf_op jit(solution)/shard_map/ppermute | solution.py:242
  61.3 2.3 %collective-permute-done.27.refs_6_ = bf16[80,512]{1,0:T(8,128)(2,1)S(1)} collective-permute-done((bf16[80,512]{1,0:T(8,128)(2,1)S(1)}, bf16[80,512]{1,0:T(8,128)(2,1)S(1)}, u32[]{:S(2)}, u32[]{:S(2)}) %collective-permute-start.27) | collective-permute-done | bytes 81952 | tf_op jit(solution)/shard_map/ppermute | solution.py:242
  65.1 1.5 %collective-permute-done.29.other = bf16[64,2048]{1,0:T(8,128)(2,1)S(1)} collective-permute-done((bf16[64,2048]{1,0:T(8,128)(2,1)S(1)}, bf16[64,2048]{1,0:T(8,128)(2,1)S(1)}, u32[]{:S(2)}, u32[]{:S(2)}) %collective-permute-start.29) | collective-permute-done | bytes 262176 | tf_op jit(solution)/shard_map/ppermute | solution.py:198
  66.6 1.4 %join.1 = bf16[64,4096]{1,0:T(8,128)(2,1)} custom-call(s32[3]{0:T(128)S(1)} %pad_add_fusion.pos_ref, bf16[64,2048]{1,0:T(8,128)(2,1)S(1)} %get-tuple-element.39.mine, bf16[64,2048]{1,0:T(8,128)(2,1)S(1)} %collective-permute-done.29.other), custom_call_target="tpu_custom_call" | custom-call | flops 1000000000 | tf_op jit(solution)/shard_map/join/pallas_call | solution.py:231
  (62 shorter events, 10.9 us)
Async XLA Ops:
  3.0 10.2 %collective-permute-start.7 = (bf16[80,1024]{1,0:T(8,128)(2,1)S(1)}, bf16[80,1024]{1,0:T(8,128)(2,1)S(1)}, u32[]{:S(2)}, u32[]{:S(2)}) collective-permute-start(bf16[80,1024]{1,0:T(8,128)(2,1)S(1)} %get-tuple-element.25), channel_id=1, source_target_pairs={{0,12},{2,14},{4,8},{6,10},{8,4},{10,6},{12,0},{14,2},{1,13},{3,15... | collective-permute-start | bytes 491528 | tf_op jit(solution)/shard_map/ppermute | solution.py:242
  8.1 8.8 %collective-permute-start.3 = (bf16[80,1024]{1,0:T(8,128)(2,1)S(1)}, bf16[80,1024]{1,0:T(8,128)(2,1)S(1)}, u32[]{:S(2)}, u32[]{:S(2)}) collective-permute-start(bf16[80,1024]{1,0:T(8,128)(2,1)S(1)} %get-tuple-element.24), channel_id=1, source_target_pairs={{0,4},{2,6},{4,0},{6,2},{8,12},{10,14},{12,8},{14,10},{1,5},{3,7},... | collective-permute-start | bytes 491528 | tf_op jit(solution)/shard_map/ppermute | solution.py:242
  8.1 10.2 %collective-permute-start.1 = (bf16[80,1024]{1,0:T(8,128)(2,1)S(1)}, bf16[80,1024]{1,0:T(8,128)(2,1)S(1)}, u32[]{:S(2)}, u32[]{:S(2)}) collective-permute-start(bf16[80,1024]{1,0:T(8,128)(2,1)S(1)} %get-tuple-element.23.refs_0_), channel_id=1, source_target_pairs={{0,2},{2,0},{1,3},{3,1},{4,6},{6,4},{5,7},{7,5},{8,10},{10,8},{9,1... | collective-permute-start | bytes 491528 | tf_op jit(solution)/shard_map/ppermute | solution.py:198
  9.6 8.7 %collective-permute-start = (bf16[80,1024]{1,0:T(8,128)(2,1)S(1)}, bf16[80,1024]{1,0:T(8,128)(2,1)S(1)}, u32[]{:S(2)}, u32[]{:S(2)}) collective-permute-start(bf16[80,1024]{1,0:T(8,128)(2,1)S(1)} %get-tuple-element.23.refs_0_), channel_id=1, source_target_pairs={{0,1},{1,0},{2,3},{3,2},{4,5},{5,4},{6,7},{7,6},{8,9},{9,8},{10,11... | collective-permute-start | bytes 491528 | tf_op jit(solution)/shard_map/ppermute | solution.py:198
  9.6 12.4 %collective-permute-start.12 = (bf16[80,1024]{1,0:T(8,128)(2,1)S(1)}, bf16[80,1024]{1,0:T(8,128)(2,1)S(1)}, u32[]{:S(2)}, u32[]{:S(2)}) collective-permute-start(bf16[80,1024]{1,0:T(8,128)(2,1)S(1)} %get-tuple-element.28), channel_id=1, source_target_pairs={{0,8},{2,10},{4,12},{6,14},{8,0},{10,2},{12,4},{14,6},{1,9},{3,11}... | collective-permute-start | bytes 491528 | tf_op jit(solution)/shard_map/ppermute | solution.py:242
  13.2 10.3 %collective-permute-start.9 = (bf16[80,1024]{1,0:T(8,128)(2,1)S(1)}, bf16[80,1024]{1,0:T(8,128)(2,1)S(1)}, u32[]{:S(2)}, u32[]{:S(2)}) collective-permute-start(bf16[80,1024]{1,0:T(8,128)(2,1)S(1)} %collective-permute-done.7.refs_8_), channel_id=1, source_target_pairs={{0,2},{2,0},{1,3},{3,1},{4,6},{6,4},{5,7},{7,5},{8,10},{10,8},{9,1... | collective-permute-start | bytes 491528 | tf_op jit(solution)/shard_map/ppermute | solution.py:198
  16.9 6.6 %collective-permute-start.5 = (bf16[80,1024]{1,0:T(8,128)(2,1)S(1)}, bf16[80,1024]{1,0:T(8,128)(2,1)S(1)}, u32[]{:S(2)}, u32[]{:S(2)}) collective-permute-start(bf16[80,1024]{1,0:T(8,128)(2,1)S(1)} %collective-permute-done.3.refs_4_), channel_id=1, source_target_pairs={{0,2},{2,0},{1,3},{3,1},{4,6},{6,4},{5,7},{7,5},{8,10},{10,8},{9,1... | collective-permute-start | bytes 491528 | tf_op jit(solution)/shard_map/ppermute | solution.py:198
  18.3 5.7 %collective-permute-start.2 = (bf16[80,1024]{1,0:T(8,128)(2,1)S(1)}, bf16[80,1024]{1,0:T(8,128)(2,1)S(1)}, u32[]{:S(2)}, u32[]{:S(2)}) collective-permute-start(bf16[80,1024]{1,0:T(8,128)(2,1)S(1)} %collective-permute-done.1.refs_2_), channel_id=1, source_target_pairs={{0,1},{1,0},{2,3},{3,2},{4,5},{5,4},{6,7},{7,6},{8,9},{9,8},{10,11... | collective-permute-start | bytes 491528 | tf_op jit(solution)/shard_map/ppermute | solution.py:198
  18.3 5.7 %collective-permute-start.4 = (bf16[80,1024]{1,0:T(8,128)(2,1)S(1)}, bf16[80,1024]{1,0:T(8,128)(2,1)S(1)}, u32[]{:S(2)}, u32[]{:S(2)}) collective-permute-start(bf16[80,1024]{1,0:T(8,128)(2,1)S(1)} %collective-permute-done.3.refs_4_), channel_id=1, source_target_pairs={{0,1},{1,0},{2,3},{3,2},{4,5},{5,4},{6,7},{7,6},{8,9},{9,8},{10,11... | collective-permute-start | bytes 491528 | tf_op jit(solution)/shard_map/ppermute | solution.py:198
  22.0 5.3 %collective-permute-start.14 = (bf16[80,1024]{1,0:T(8,128)(2,1)S(1)}, bf16[80,1024]{1,0:T(8,128)(2,1)S(1)}, u32[]{:S(2)}, u32[]{:S(2)}) collective-permute-start(bf16[80,1024]{1,0:T(8,128)(2,1)S(1)} %collective-permute-done.12.refs_0_), channel_id=1, source_target_pairs={{0,2},{2,0},{1,3},{3,1},{4,6},{6,4},{5,7},{7,5},{8,10},{10,8},{9,1... | collective-permute-start | bytes 491528 | tf_op jit(solution)/shard_map/ppermute | solution.py:198
  24.0 4.8 %collective-permute-start.13 = (bf16[80,1024]{1,0:T(8,128)(2,1)S(1)}, bf16[80,1024]{1,0:T(8,128)(2,1)S(1)}, u32[]{:S(2)}, u32[]{:S(2)}) collective-permute-start(bf16[80,1024]{1,0:T(8,128)(2,1)S(1)} %collective-permute-done.12.refs_0_), channel_id=1, source_target_pairs={{0,1},{1,0},{2,3},{3,2},{4,5},{5,4},{6,7},{7,6},{8,9},{9,8},{10,11... | collective-permute-start | bytes 491528 | tf_op jit(solution)/shard_map/ppermute | solution.py:198
  32.4 5.8 %collective-permute-start.19 = (bf16[160,384]{1,0:T(8,128)(2,1)S(1)}, bf16[160,384]{1,0:T(8,128)(2,1)S(1)}, u32[]{:S(2)}, u32[]{:S(2)}) collective-permute-start(bf16[160,384]{1,0:T(8,128)(2,1)S(1)} %get-tuple-element.30.own), channel_id=1, source_target_pairs={{0,2},{2,0},{1,3},{3,1},{4,6},{6,4},{5,7},{7,5},{8,10},{10,8},{9,1... | collective-permute-start | bytes 368648 | tf_op jit(solution)/shard_map/ppermute | solution.py:198
  37.2 5.5 %collective-permute-start.16 = (bf16[160,384]{1,0:T(8,128)(2,1)S(1)}, bf16[160,384]{1,0:T(8,128)(2,1)S(1)}, u32[]{:S(2)}, u32[]{:S(2)}) collective-permute-start(bf16[160,384]{1,0:T(8,128)(2,1)S(1)} %hidden_b.1.own), channel_id=1, source_target_pairs={{0,2},{2,0},{1,3},{3,1},{4,6},{6,4},{5,7},{7,5},{8,10},{10,8},{9,1... | collective-permute-start | bytes 368648 | tf_op jit(solution)/shard_map/ppermute | solution.py:198
  37.8 4.9 %collective-permute-start.20 = (bf16[160,384]{1,0:T(8,128)(2,1)S(1)}, bf16[160,384]{1,0:T(8,128)(2,1)S(1)}, u32[]{:S(2)}, u32[]{:S(2)}) collective-permute-start(bf16[160,384]{1,0:T(8,128)(2,1)S(1)} %get-tuple-element.30.own), channel_id=1, source_target_pairs={{0,1},{1,0},{2,3},{3,2},{4,5},{5,4},{6,7},{7,6},{8,9},{9,8},{10,11... | collective-permute-start | bytes 368648 | tf_op jit(solution)/shard_map/ppermute | solution.py:198
  38.2 4.5 %collective-permute-start.21 = (bf16[160,384]{1,0:T(8,128)(2,1)S(1)}, bf16[160,384]{1,0:T(8,128)(2,1)S(1)}, u32[]{:S(2)}, u32[]{:S(2)}) collective-permute-start(bf16[160,384]{1,0:T(8,128)(2,1)S(1)} %collective-permute-done.19.x), channel_id=1, source_target_pairs={{0,1},{1,0},{2,3},{3,2},{4,5},{5,4},{6,7},{7,6},{8,9},{9,8},{10,11... | collective-permute-start | bytes 368648 | tf_op jit(solution)/shard_map/ppermute | solution.py:198
  38.3 4.4 %collective-permute-start.11 = (f32[2,64]{1,0:T(2,128)S(1)}, f32[2,64]{1,0:T(2,128)S(1)}, u32[]{:S(2)}, u32[]{:S(2)}) collective-permute-start(f32[2,64]{1,0:T(2,128)S(1)} %get-tuple-element.26.own), channel_id=1, source_target_pairs={{0,1},{1,0},{2,3},{3,2},{4,5},{5,4},{6,7},{7,6},{8,9},{9,8},{10,11... | collective-permute-start | bytes 1544 | tf_op jit(solution)/shard_map/ppermute | solution.py:198
  38.7 5.9 %collective-permute-start.17 = (bf16[160,384]{1,0:T(8,128)(2,1)S(1)}, bf16[160,384]{1,0:T(8,128)(2,1)S(1)}, u32[]{:S(2)}, u32[]{:S(2)}) collective-permute-start(bf16[160,384]{1,0:T(8,128)(2,1)S(1)} %hidden_b.1.own), channel_id=1, source_target_pairs={{0,1},{1,0},{2,3},{3,2},{4,5},{5,4},{6,7},{7,6},{8,9},{9,8},{10,11... | collective-permute-start | bytes 368648 | tf_op jit(solution)/shard_map/ppermute | solution.py:198
  47.4 9.0 %collective-permute-start.22 = (bf16[80,512]{1,0:T(8,128)(2,1)S(1)}, bf16[80,512]{1,0:T(8,128)(2,1)S(1)}, u32[]{:S(2)}, u32[]{:S(2)}) collective-permute-start(bf16[80,512]{1,0:T(8,128)(2,1)S(1)} %get-tuple-element.32), channel_id=1, source_target_pairs={{0,8},{2,10},{4,12},{6,14},{8,0},{10,2},{12,4},{14,6},{1,9},{3,11}... | collective-permute-start | bytes 245768 | tf_op jit(solution)/shard_map/ppermute | solution.py:242
  48.7 10.2 %collective-permute-start.23 = (bf16[80,512]{1,0:T(8,128)(2,1)S(1)}, bf16[80,512]{1,0:T(8,128)(2,1)S(1)}, u32[]{:S(2)}, u32[]{:S(2)}) collective-permute-start(bf16[80,512]{1,0:T(8,128)(2,1)S(1)} %get-tuple-element.33), channel_id=1, source_target_pairs={{0,2},{2,0},{4,6},{6,4},{8,10},{10,8},{12,14},{14,12},{1,3},{3,1},... | collective-permute-start | bytes 245768 | tf_op jit(solution)/shard_map/ppermute | solution.py:242
  49.3 12.0 %collective-permute-start.24 = (bf16[80,512]{1,0:T(8,128)(2,1)S(1)}, bf16[80,512]{1,0:T(8,128)(2,1)S(1)}, u32[]{:S(2)}, u32[]{:S(2)}) collective-permute-start(bf16[80,512]{1,0:T(8,128)(2,1)S(1)} %get-tuple-element.34), channel_id=1, source_target_pairs={{0,10},{2,8},{4,14},{6,12},{8,2},{10,0},{12,6},{14,4},{1,11},{3,9}... | collective-permute-start | bytes 245768 | tf_op jit(solution)/shard_map/ppermute | solution.py:242
  51.9 9.5 %collective-permute-start.25 = (bf16[80,512]{1,0:T(8,128)(2,1)S(1)}, bf16[80,512]{1,0:T(8,128)(2,1)S(1)}, u32[]{:S(2)}, u32[]{:S(2)}) collective-permute-start(bf16[80,512]{1,0:T(8,128)(2,1)S(1)} %get-tuple-element.35), channel_id=1, source_target_pairs={{0,6},{2,4},{4,2},{6,0},{8,14},{10,12},{12,10},{14,8},{1,7},{3,5},... | collective-permute-start | bytes 245768 | tf_op jit(solution)/shard_map/ppermute | solution.py:242
  52.5 8.8 %collective-permute-start.26 = (bf16[80,512]{1,0:T(8,128)(2,1)S(1)}, bf16[80,512]{1,0:T(8,128)(2,1)S(1)}, u32[]{:S(2)}, u32[]{:S(2)}) collective-permute-start(bf16[80,512]{1,0:T(8,128)(2,1)S(1)} %get-tuple-element.36), channel_id=1, source_target_pairs={{0,12},{2,14},{4,8},{6,10},{8,4},{10,6},{12,0},{14,2},{1,13},{3,15... | collective-permute-start | bytes 245768 | tf_op jit(solution)/shard_map/ppermute | solution.py:242
  56.4 7.3 %collective-permute-start.27 = (bf16[80,512]{1,0:T(8,128)(2,1)S(1)}, bf16[80,512]{1,0:T(8,128)(2,1)S(1)}, u32[]{:S(2)}, u32[]{:S(2)}) collective-permute-start(bf16[80,512]{1,0:T(8,128)(2,1)S(1)} %get-tuple-element.37), channel_id=1, source_target_pairs={{0,14},{2,12},{4,10},{6,8},{8,6},{10,4},{12,2},{14,0},{1,15},{3,13... | collective-permute-start | bytes 245768 | tf_op jit(solution)/shard_map/ppermute | solution.py:242
  58.9 5.0 %collective-permute-start.28 = (bf16[80,512]{1,0:T(8,128)(2,1)S(1)}, bf16[80,512]{1,0:T(8,128)(2,1)S(1)}, u32[]{:S(2)}, u32[]{:S(2)}) collective-permute-start(bf16[80,512]{1,0:T(8,128)(2,1)S(1)} %get-tuple-element.38), channel_id=1, source_target_pairs={{0,4},{2,6},{4,0},{6,2},{8,12},{10,14},{12,8},{14,10},{1,5},{3,7},... | collective-permute-start | bytes 245768 | tf_op jit(solution)/shard_map/ppermute | solution.py:242
  (14 other events, 133.9 us)

commit v6 on v5

--- a/solution.py
+++ b/solution.py
@@ -7,7 +7,7 @@
 from jax.sharding import PartitionSpec as P
 
 BIG = 4096
-ORDER = (0, 4, 1, 5, 3, 6, 7, 2)
+ORDER = (0, 4, 3, 5, 1, 6, 7, 2)
 LEAD = 20 * 10**9
 STEP = 10 * 10**9
 VMEM_LIMIT = 8 * 1024 * 1024
@@ -181,15 +181,6 @@
                 out[:, pl.ds(pl.multiple_of(at + q * width, 128), width)] = (weights[rel] * got[k * n:(k + 1) * n]).astype(BF16)
 
 
-def join_kernel(cfg, pos_ref, mine, other, out):
-    t = pos_ref[2]
-    width = mine.shape[1] // 2
-    for cc in range(2):
-        for ref, dt in ((mine, 0), (other, 1)):
-            at = cc * 2 * width + jnp.bitwise_xor(t, dt) * width
-            out[:, pl.ds(pl.multiple_of(at, 128), width)] = ref[:, cc * width:(cc + 1) * width]
-
-
 class Sizes:
     pass
 
@@ -275,7 +266,9 @@
         lambda pos_ref, own, peer, *refs: combine_kernel(
             cfg, pos_ref, own, peer, *[refs[order.index(k)] for k in range(len(order))], *refs[len(order):]),
         "combine", [info, info_peer] + [returned[k] for k in order], [(n, 2 * wide)] * 2)
-    return call(kernel(join_kernel), "join", [mine, swap(other, "tensor")], [(n, width)])[0]
+    received = swap(other, "tensor")
+    first, second = jnp.where(t == 0, mine, received), jnp.where(t == 0, received, mine)
+    return jnp.concatenate([first[:, :wide], second[:, :wide], first[:, wide:], second[:, wide:]], axis=1)
 
 
 def by_gathers(tokens, expert_ids, route_weights, gate_weight, up_weight, down_weight):

time: 68.1 us -> 67.5 us (level)
  Pallas kernels: 16.4 us -> 15.1 us
  other arithmetic: 0.08 us -> 0.94 us
    pallas_call x8 -> x7, Pallas kernels: 16.4 us -> 15.1 us  [call(): pl.pallas_call(kernel, in_specs=[smem] + [vmem] * len(ins), out_specs=[vm...]
    concatenate x0 -> x1, other arithmetic: none -> 0.83 us  [on_device(): jnp.concatenate([first[:, :wide], second[:, :wide], first[:, wide:], seco...]
where the time goes in v6:
time: 67.5 us; the launch traced here: 67.3 us
  starting transfers between devices  25.7 us (38%)
  waiting for transfers between devices  23.6 us (35%)
  Pallas kernels  15.1 us (22%)
  local copies, waits for them, and re-layouts  1.76 us (3%)
  other arithmetic  0.94 us (1%)
    ppermute x10, starting transfers between devices, move(): lax.ppermute(x, ('expert', 'context'), [(i * 2 + k, (i ^ r) * 2 + (k ^ dc...  15.3 us
    pallas_call x7, Pallas kernels, call(): pl.pallas_call(kernel, in_specs=[smem] + [vmem] * len(ins), out_specs=[vm...  15.1 us
    ppermute x10, waiting for transfers between devices, move(): lax.ppermute(x, ('expert', 'context'), [(i * 2 + k, (i ^ r) * 2 + (k ^ dc...  15 us
    ppermute x20, starting transfers between devices, swap(): return lax.ppermute(x, axis, [(0, 1), (1, 0)])  10.5 us
    ppermute x20, waiting for transfers between devices, swap(): return lax.ppermute(x, axis, [(0, 1), (1, 0)])  8.64 us
    unnamed x16, local copies, waits for them, and re-layouts  1.72 us
  transfers between devices with their start and end apart: 30, of which 11 were waited for; matrix products, arithmetic and copies ran while one was open for 0% of the time, Pallas kernels for 10%

profile of v6, /device:TPU:0, one launch (start us, length us, event | category | flops | bytes accessed | tf_op | source)
XLA Modules:
  0.0 67.3 jit_solution(4243355209644329896)
XLA Ops:
  3.0 5.1 %collective-permute-start.7 = (bf16[80,1024]{1,0:T(8,128)(2,1)S(1)}, bf16[80,1024]{1,0:T(8,128)(2,1)S(1)}, u32[]{:S(2)}, u32[]{:S(2)}) collective-permute-start(bf16[80,1024]{1,0:T(8,128)(2,1)S(1)} %get-tuple-element.25), channel_id=1, source_target_pairs={{0,12},{2,14},{4,8},{6,10},{8,4},{10,6},{12,0},{14,2},{1,13},{3,15... | collective-permute-start | bytes 491528 | tf_op jit(solution)/shard_map/ppermute | solution.py:233
  8.1 1.5 %collective-permute-start.1 = (bf16[80,1024]{1,0:T(8,128)(2,1)S(1)}, bf16[80,1024]{1,0:T(8,128)(2,1)S(1)}, u32[]{:S(2)}, u32[]{:S(2)}) collective-permute-start(bf16[80,1024]{1,0:T(8,128)(2,1)S(1)} %get-tuple-element.23.refs_0_), channel_id=1, source_target_pairs={{0,2},{2,0},{1,3},{3,1},{4,6},{6,4},{5,7},{7,5},{8,10},{10,8},{9,1... | collective-permute-start | bytes 491528 | tf_op jit(solution)/shard_map/ppermute | solution.py:189
  10.4 2.8 %collective-permute-done.7.refs_8_ = bf16[80,1024]{1,0:T(8,128)(2,1)S(1)} collective-permute-done((bf16[80,1024]{1,0:T(8,128)(2,1)S(1)}, bf16[80,1024]{1,0:T(8,128)(2,1)S(1)}, u32[]{:S(2)}, u32[]{:S(2)}) %collective-permute-start.7) | collective-permute-done | bytes 163872 | tf_op jit(solution)/shard_map/ppermute | solution.py:233
  13.2 1.7 %collective-permute-start.9 = (bf16[80,1024]{1,0:T(8,128)(2,1)S(1)}, bf16[80,1024]{1,0:T(8,128)(2,1)S(1)}, u32[]{:S(2)}, u32[]{:S(2)}) collective-permute-start(bf16[80,1024]{1,0:T(8,128)(2,1)S(1)} %collective-permute-done.7.refs_8_), channel_id=1, source_target_pairs={{0,2},{2,0},{1,3},{3,1},{4,6},{6,4},{5,7},{7,5},{8,10},{10,8},{9,1... | collective-permute-start | bytes 491528 | tf_op jit(solution)/shard_map/ppermute | solution.py:189
  14.8 2.0 %collective-permute-done.3.refs_4_ = bf16[80,1024]{1,0:T(8,128)(2,1)S(1)} collective-permute-done((bf16[80,1024]{1,0:T(8,128)(2,1)S(1)}, bf16[80,1024]{1,0:T(8,128)(2,1)S(1)}, u32[]{:S(2)}, u32[]{:S(2)}) %collective-permute-start.3) | collective-permute-done | bytes 163872 | tf_op jit(solution)/shard_map/ppermute | solution.py:233
  16.9 1.4 %collective-permute-start.5 = (bf16[80,1024]{1,0:T(8,128)(2,1)S(1)}, bf16[80,1024]{1,0:T(8,128)(2,1)S(1)}, u32[]{:S(2)}, u32[]{:S(2)}) collective-permute-start(bf16[80,1024]{1,0:T(8,128)(2,1)S(1)} %collective-permute-done.3.refs_4_), channel_id=1, source_target_pairs={{0,2},{2,0},{1,3},{3,1},{4,6},{6,4},{5,7},{7,5},{8,10},{10,8},{9,1... | collective-permute-start | bytes 491528 | tf_op jit(solution)/shard_map/ppermute | solution.py:189
  18.8 3.2 %collective-permute-done.12.refs_0_ = bf16[80,1024]{1,0:T(8,128)(2,1)S(1)} collective-permute-done((bf16[80,1024]{1,0:T(8,128)(2,1)S(1)}, bf16[80,1024]{1,0:T(8,128)(2,1)S(1)}, u32[]{:S(2)}, u32[]{:S(2)}) %collective-permute-start.12) | collective-permute-done | bytes 163872 | tf_op jit(solution)/shard_map/ppermute | solution.py:233
  22.0 1.5 %collective-permute-start.14 = (bf16[80,1024]{1,0:T(8,128)(2,1)S(1)}, bf16[80,1024]{1,0:T(8,128)(2,1)S(1)}, u32[]{:S(2)}, u32[]{:S(2)}) collective-permute-start(bf16[80,1024]{1,0:T(8,128)(2,1)S(1)} %collective-permute-done.12.refs_0_), channel_id=1, source_target_pairs={{0,2},{2,0},{1,3},{3,1},{4,6},{6,4},{5,7},{7,5},{8,10},{10,8},{9,1... | collective-permute-start | bytes 491528 | tf_op jit(solution)/shard_map/ppermute | solution.py:189
  24.5 2.8 %collective-permute-done.14.refs_2_ = bf16[80,1024]{1,0:T(8,128)(2,1)S(1)} collective-permute-done((bf16[80,1024]{1,0:T(8,128)(2,1)S(1)}, bf16[80,1024]{1,0:T(8,128)(2,1)S(1)}, u32[]{:S(2)}, u32[]{:S(2)}) %collective-permute-start.14) | collective-permute-done | bytes 163872 | tf_op jit(solution)/shard_map/ppermute | solution.py:189
  27.3 1.5 %near.1 = (bf16[4,96,4096]{2,1,0:T(8,128)(2,1)S(1)}, f32[2,64]{1,0:T(2,128)S(1)}) custom-call(s32[3]{0:T(128)S(1)} %pad_add_fusion.pos_ref, bf16[80,1024]{1,0:T(8,128)(2,1)S(1)} %get-tuple-element.23.refs_0_, bf16[80,1024]{1,0:T(8,128)(2,1)S(1)} %collective-permute-done.refs_1_, bf16[80,1024]{1,0:T(8,128)(2,1)S(1)} %collective-permute-done.1.refs_2_, ...), custom_call_target="tpu_custom_call" | custom-call | flops 1000000000 | tf_op jit(solution)/shard_map/near/pallas_call | solution.py:222
  28.9 3.5 %hidden_a.1 = (bf16[160,384]{1,0:T(8,128)(2,1)S(1)}, bf16[2,32,4096]{2,1,0:T(8,128)(2,1)S(1)}) custom-call(s32[3]{0:T(128)S(1)} %pad_add_fusion.pos_ref, bf16[80,1024]{1,0:T(8,128)(2,1)S(1)} %collective-permute-done.12.refs_0_, bf16[80,1024]{1,0:T(8,128)(2,1)S(1)} %collective-permute-done.13.refs_1_, bf16[80,1024]{1,0:T(8,128)(2,1)S(1)} %collective-permute-done.14.refs_2_, ...), custom_call_target="tpu_custom_call" | custom-call | flops 10000000000 | tf_op jit(solution)/shard_map/hidden_a/pallas_call | solution.py:222
  32.4 1.6 %collective-permute-start.19 = (bf16[160,384]{1,0:T(8,128)(2,1)S(1)}, bf16[160,384]{1,0:T(8,128)(2,1)S(1)}, u32[]{:S(2)}, u32[]{:S(2)}) collective-permute-start(bf16[160,384]{1,0:T(8,128)(2,1)S(1)} %get-tuple-element.30.own), channel_id=1, source_target_pairs={{0,2},{2,0},{1,3},{3,1},{4,6},{6,4},{5,7},{7,5},{8,10},{10,8},{9,1... | collective-permute-start | bytes 368648 | tf_op jit(solution)/shard_map/ppermute | solution.py:189
  34.0 3.2 %hidden_b.1.own = bf16[160,384]{1,0:T(8,128)(2,1)S(1)} custom-call(s32[3]{0:T(128)S(1)} %pad_add_fusion.pos_ref, bf16[4,96,4096]{2,1,0:T(8,128)(2,1)S(1)} %get-tuple-element.27.refs_4_.near, bf16[2,32,4096]{2,1,0:T(8,128)(2,1)S(1)} %get-tuple-element.29.far, bf16[4,4096,384]{2,1,0:T(8,128)(2,1)S(1)} %copy-done, bf16[4,4096,384]{2,1,0:T(8,128)(2,1)S(1)} %copy-done.1), custom_call_target="tpu_custom_call" | custom-call | flops 10000000000 | tf_op jit(solution)/shard_map/hidden_b/pallas_call | solution.py:222
  38.8 3.9 %collective-permute-done.16.x = bf16[160,384]{1,0:T(8,128)(2,1)S(1)} collective-permute-done((bf16[160,384]{1,0:T(8,128)(2,1)S(1)}, bf16[160,384]{1,0:T(8,128)(2,1)S(1)}, u32[]{:S(2)}, u32[]{:S(2)}) %collective-permute-start.16) | collective-permute-done | bytes 122912 | tf_op jit(solution)/shard_map/ppermute | solution.py:189
  42.8 1.8 %down_a.1.before = bf16[160,1024]{1,0:T(8,128)(2,1)S(1)} custom-call(s32[3]{0:T(128)S(1)} %pad_add_fusion.pos_ref, bf16[160,384]{1,0:T(8,128)(2,1)S(1)} %get-tuple-element.30.own, bf16[160,384]{1,0:T(8,128)(2,1)S(1)} %collective-permute-done.19.x, bf16[160,384]{1,0:T(8,128)(2,1)S(1)} %collective-permute-done.20.core, ...), custom_call_target="tpu_custom_call" | custom-call | flops 10000000000 | tf_op jit(solution)/shard_map/down_a/pallas_call | solution.py:222
  44.6 2.8 %down_b.1 = (bf16[80,512]{1,0:T(8,128)(2,1)S(1)}, bf16[80,512]{1,0:T(8,128)(2,1)S(1)}, bf16[80,512]{1,0:T(8,128)(2,1)S(1)}, bf16[80,512]{1,0:T(8,128)(2,1)S(1)},...) custom-call(s32[3]{0:T(128)S(1)} %pad_add_fusion.pos_ref, ...), custom_call_target="tpu_custom_call" | custom-call | flops 10000000000 | tf_op jit(solution)/shard_map/down_b/pallas_call | solution.py:222
  47.4 1.3 %collective-permute-start.22 = (bf16[80,512]{1,0:T(8,128)(2,1)S(1)}, bf16[80,512]{1,0:T(8,128)(2,1)S(1)}, u32[]{:S(2)}, u32[]{:S(2)}) collective-permute-start(bf16[80,512]{1,0:T(8,128)(2,1)S(1)} %get-tuple-element.32), channel_id=1, source_target_pairs={{0,8},{2,10},{4,12},{6,14},{8,0},{10,2},{12,4},{14,6},{1,9},{3,11}... | collective-permute-start | bytes 245768 | tf_op jit(solution)/shard_map/ppermute | solution.py:233
  48.7 1.7 %collective-permute-start.23 = (bf16[80,512]{1,0:T(8,128)(2,1)S(1)}, bf16[80,512]{1,0:T(8,128)(2,1)S(1)}, u32[]{:S(2)}, u32[]{:S(2)}) collective-permute-start(bf16[80,512]{1,0:T(8,128)(2,1)S(1)} %get-tuple-element.33), channel_id=1, source_target_pairs={{0,6},{2,4},{4,2},{6,0},{8,14},{10,12},{12,10},{14,8},{1,7},{3,5},... | collective-permute-start | bytes 245768 | tf_op jit(solution)/shard_map/ppermute | solution.py:233
  50.5 1.6 %collective-permute-start.24 = (bf16[80,512]{1,0:T(8,128)(2,1)S(1)}, bf16[80,512]{1,0:T(8,128)(2,1)S(1)}, u32[]{:S(2)}, u32[]{:S(2)}) collective-permute-start(bf16[80,512]{1,0:T(8,128)(2,1)S(1)} %get-tuple-element.34), channel_id=1, source_target_pairs={{0,10},{2,8},{4,14},{6,12},{8,2},{10,0},{12,6},{14,4},{1,11},{3,9}... | collective-permute-start | bytes 245768 | tf_op jit(solution)/shard_map/ppermute | solution.py:233
  52.5 2.0 %collective-permute-start.26 = (bf16[80,512]{1,0:T(8,128)(2,1)S(1)}, bf16[80,512]{1,0:T(8,128)(2,1)S(1)}, u32[]{:S(2)}, u32[]{:S(2)}) collective-permute-start(bf16[80,512]{1,0:T(8,128)(2,1)S(1)} %get-tuple-element.36), channel_id=1, source_target_pairs={{0,12},{2,14},{4,8},{6,10},{8,4},{10,6},{12,0},{14,2},{1,13},{3,15... | collective-permute-start | bytes 245768 | tf_op jit(solution)/shard_map/ppermute | solution.py:233
  55.2 2.2 %collective-permute-start.27 = (bf16[80,512]{1,0:T(8,128)(2,1)S(1)}, bf16[80,512]{1,0:T(8,128)(2,1)S(1)}, u32[]{:S(2)}, u32[]{:S(2)}) collective-permute-start(bf16[80,512]{1,0:T(8,128)(2,1)S(1)} %get-tuple-element.37), channel_id=1, source_target_pairs={{0,14},{2,12},{4,10},{6,8},{8,6},{10,4},{12,2},{14,0},{1,15},{3,13... | collective-permute-start | bytes 245768 | tf_op jit(solution)/shard_map/ppermute | solution.py:233
  57.4 4.0 %collective-permute-done.24.refs_3_ = bf16[80,512]{1,0:T(8,128)(2,1)S(1)} collective-permute-done((bf16[80,512]{1,0:T(8,128)(2,1)S(1)}, bf16[80,512]{1,0:T(8,128)(2,1)S(1)}, u32[]{:S(2)}, u32[]{:S(2)}) %collective-permute-start.24) | collective-permute-done | bytes 81952 | tf_op jit(solution)/shard_map/ppermute | solution.py:233
  61.4 1.5 %collective-permute-done.27.refs_6_ = bf16[80,512]{1,0:T(8,128)(2,1)S(1)} collective-permute-done((bf16[80,512]{1,0:T(8,128)(2,1)S(1)}, bf16[80,512]{1,0:T(8,128)(2,1)S(1)}, u32[]{:S(2)}, u32[]{:S(2)}) %collective-permute-start.27) | collective-permute-done | bytes 81952 | tf_op jit(solution)/shard_map/ppermute | solution.py:233
  64.9 1.5 %collective-permute-done.29 = bf16[64,2048]{1,0:T(8,128)(2,1)S(1)} collective-permute-done((bf16[64,2048]{1,0:T(8,128)(2,1)S(1)}, bf16[64,2048]{1,0:T(8,128)(2,1)S(1)}, u32[]{:S(2)}, u32[]{:S(2)}) %collective-permute-start.29) | collective-permute-done | bytes 262176 | tf_op jit(solution)/shard_map/ppermute | solution.py:189
  (64 shorter events, 10.9 us)
Async XLA Ops:
  3.0 10.2 %collective-permute-start.7 = (bf16[80,1024]{1,0:T(8,128)(2,1)S(1)}, bf16[80,1024]{1,0:T(8,128)(2,1)S(1)}, u32[]{:S(2)}, u32[]{:S(2)}) collective-permute-start(bf16[80,1024]{1,0:T(8,128)(2,1)S(1)} %get-tuple-element.25), channel_id=1, source_target_pairs={{0,12},{2,14},{4,8},{6,10},{8,4},{10,6},{12,0},{14,2},{1,13},{3,15... | collective-permute-start | bytes 491528 | tf_op jit(solution)/shard_map/ppermute | solution.py:233
  8.1 8.8 %collective-permute-start.3 = (bf16[80,1024]{1,0:T(8,128)(2,1)S(1)}, bf16[80,1024]{1,0:T(8,128)(2,1)S(1)}, u32[]{:S(2)}, u32[]{:S(2)}) collective-permute-start(bf16[80,1024]{1,0:T(8,128)(2,1)S(1)} %get-tuple-element.24), channel_id=1, source_target_pairs={{0,4},{2,6},{4,0},{6,2},{8,12},{10,14},{12,8},{14,10},{1,5},{3,7},... | collective-permute-start | bytes 491528 | tf_op jit(solution)/shard_map/ppermute | solution.py:233
  8.1 10.2 %collective-permute-start.1 = (bf16[80,1024]{1,0:T(8,128)(2,1)S(1)}, bf16[80,1024]{1,0:T(8,128)(2,1)S(1)}, u32[]{:S(2)}, u32[]{:S(2)}) collective-permute-start(bf16[80,1024]{1,0:T(8,128)(2,1)S(1)} %get-tuple-element.23.refs_0_), channel_id=1, source_target_pairs={{0,2},{2,0},{1,3},{3,1},{4,6},{6,4},{5,7},{7,5},{8,10},{10,8},{9,1... | collective-permute-start | bytes 491528 | tf_op jit(solution)/shard_map/ppermute | solution.py:189
  9.6 8.7 %collective-permute-start = (bf16[80,1024]{1,0:T(8,128)(2,1)S(1)}, bf16[80,1024]{1,0:T(8,128)(2,1)S(1)}, u32[]{:S(2)}, u32[]{:S(2)}) collective-permute-start(bf16[80,1024]{1,0:T(8,128)(2,1)S(1)} %get-tuple-element.23.refs_0_), channel_id=1, source_target_pairs={{0,1},{1,0},{2,3},{3,2},{4,5},{5,4},{6,7},{7,6},{8,9},{9,8},{10,11... | collective-permute-start | bytes 491528 | tf_op jit(solution)/shard_map/ppermute | solution.py:189
  9.6 12.4 %collective-permute-start.12 = (bf16[80,1024]{1,0:T(8,128)(2,1)S(1)}, bf16[80,1024]{1,0:T(8,128)(2,1)S(1)}, u32[]{:S(2)}, u32[]{:S(2)}) collective-permute-start(bf16[80,1024]{1,0:T(8,128)(2,1)S(1)} %get-tuple-element.28), channel_id=1, source_target_pairs={{0,8},{2,10},{4,12},{6,14},{8,0},{10,2},{12,4},{14,6},{1,9},{3,11}... | collective-permute-start | bytes 491528 | tf_op jit(solution)/shard_map/ppermute | solution.py:233
  13.2 10.3 %collective-permute-start.9 = (bf16[80,1024]{1,0:T(8,128)(2,1)S(1)}, bf16[80,1024]{1,0:T(8,128)(2,1)S(1)}, u32[]{:S(2)}, u32[]{:S(2)}) collective-permute-start(bf16[80,1024]{1,0:T(8,128)(2,1)S(1)} %collective-permute-done.7.refs_8_), channel_id=1, source_target_pairs={{0,2},{2,0},{1,3},{3,1},{4,6},{6,4},{5,7},{7,5},{8,10},{10,8},{9,1... | collective-permute-start | bytes 491528 | tf_op jit(solution)/shard_map/ppermute | solution.py:189
  16.9 6.6 %collective-permute-start.5 = (bf16[80,1024]{1,0:T(8,128)(2,1)S(1)}, bf16[80,1024]{1,0:T(8,128)(2,1)S(1)}, u32[]{:S(2)}, u32[]{:S(2)}) collective-permute-start(bf16[80,1024]{1,0:T(8,128)(2,1)S(1)} %collective-permute-done.3.refs_4_), channel_id=1, source_target_pairs={{0,2},{2,0},{1,3},{3,1},{4,6},{6,4},{5,7},{7,5},{8,10},{10,8},{9,1... | collective-permute-start | bytes 491528 | tf_op jit(solution)/shard_map/ppermute | solution.py:189
  18.3 5.7 %collective-permute-start.2 = (bf16[80,1024]{1,0:T(8,128)(2,1)S(1)}, bf16[80,1024]{1,0:T(8,128)(2,1)S(1)}, u32[]{:S(2)}, u32[]{:S(2)}) collective-permute-start(bf16[80,1024]{1,0:T(8,128)(2,1)S(1)} %collective-permute-done.1.refs_2_), channel_id=1, source_target_pairs={{0,1},{1,0},{2,3},{3,2},{4,5},{5,4},{6,7},{7,6},{8,9},{9,8},{10,11... | collective-permute-start | bytes 491528 | tf_op jit(solution)/shard_map/ppermute | solution.py:189
  18.3 5.7 %collective-permute-start.4 = (bf16[80,1024]{1,0:T(8,128)(2,1)S(1)}, bf16[80,1024]{1,0:T(8,128)(2,1)S(1)}, u32[]{:S(2)}, u32[]{:S(2)}) collective-permute-start(bf16[80,1024]{1,0:T(8,128)(2,1)S(1)} %collective-permute-done.3.refs_4_), channel_id=1, source_target_pairs={{0,1},{1,0},{2,3},{3,2},{4,5},{5,4},{6,7},{7,6},{8,9},{9,8},{10,11... | collective-permute-start | bytes 491528 | tf_op jit(solution)/shard_map/ppermute | solution.py:189
  22.0 5.3 %collective-permute-start.14 = (bf16[80,1024]{1,0:T(8,128)(2,1)S(1)}, bf16[80,1024]{1,0:T(8,128)(2,1)S(1)}, u32[]{:S(2)}, u32[]{:S(2)}) collective-permute-start(bf16[80,1024]{1,0:T(8,128)(2,1)S(1)} %collective-permute-done.12.refs_0_), channel_id=1, source_target_pairs={{0,2},{2,0},{1,3},{3,1},{4,6},{6,4},{5,7},{7,5},{8,10},{10,8},{9,1... | collective-permute-start | bytes 491528 | tf_op jit(solution)/shard_map/ppermute | solution.py:189
  24.0 4.8 %collective-permute-start.13 = (bf16[80,1024]{1,0:T(8,128)(2,1)S(1)}, bf16[80,1024]{1,0:T(8,128)(2,1)S(1)}, u32[]{:S(2)}, u32[]{:S(2)}) collective-permute-start(bf16[80,1024]{1,0:T(8,128)(2,1)S(1)} %collective-permute-done.12.refs_0_), channel_id=1, source_target_pairs={{0,1},{1,0},{2,3},{3,2},{4,5},{5,4},{6,7},{7,6},{8,9},{9,8},{10,11... | collective-permute-start | bytes 491528 | tf_op jit(solution)/shard_map/ppermute | solution.py:189
  32.4 5.8 %collective-permute-start.19 = (bf16[160,384]{1,0:T(8,128)(2,1)S(1)}, bf16[160,384]{1,0:T(8,128)(2,1)S(1)}, u32[]{:S(2)}, u32[]{:S(2)}) collective-permute-start(bf16[160,384]{1,0:T(8,128)(2,1)S(1)} %get-tuple-element.30.own), channel_id=1, source_target_pairs={{0,2},{2,0},{1,3},{3,1},{4,6},{6,4},{5,7},{7,5},{8,10},{10,8},{9,1... | collective-permute-start | bytes 368648 | tf_op jit(solution)/shard_map/ppermute | solution.py:189
  37.2 5.5 %collective-permute-start.16 = (bf16[160,384]{1,0:T(8,128)(2,1)S(1)}, bf16[160,384]{1,0:T(8,128)(2,1)S(1)}, u32[]{:S(2)}, u32[]{:S(2)}) collective-permute-start(bf16[160,384]{1,0:T(8,128)(2,1)S(1)} %hidden_b.1.own), channel_id=1, source_target_pairs={{0,2},{2,0},{1,3},{3,1},{4,6},{6,4},{5,7},{7,5},{8,10},{10,8},{9,1... | collective-permute-start | bytes 368648 | tf_op jit(solution)/shard_map/ppermute | solution.py:189
  37.8 4.9 %collective-permute-start.20 = (bf16[160,384]{1,0:T(8,128)(2,1)S(1)}, bf16[160,384]{1,0:T(8,128)(2,1)S(1)}, u32[]{:S(2)}, u32[]{:S(2)}) collective-permute-start(bf16[160,384]{1,0:T(8,128)(2,1)S(1)} %get-tuple-element.30.own), channel_id=1, source_target_pairs={{0,1},{1,0},{2,3},{3,2},{4,5},{5,4},{6,7},{7,6},{8,9},{9,8},{10,11... | collective-permute-start | bytes 368648 | tf_op jit(solution)/shard_map/ppermute | solution.py:189
  38.2 4.5 %collective-permute-start.21 = (bf16[160,384]{1,0:T(8,128)(2,1)S(1)}, bf16[160,384]{1,0:T(8,128)(2,1)S(1)}, u32[]{:S(2)}, u32[]{:S(2)}) collective-permute-start(bf16[160,384]{1,0:T(8,128)(2,1)S(1)} %collective-permute-done.19.x), channel_id=1, source_target_pairs={{0,1},{1,0},{2,3},{3,2},{4,5},{5,4},{6,7},{7,6},{8,9},{9,8},{10,11... | collective-permute-start | bytes 368648 | tf_op jit(solution)/shard_map/ppermute | solution.py:189
  38.3 4.4 %collective-permute-start.11 = (f32[2,64]{1,0:T(2,128)S(1)}, f32[2,64]{1,0:T(2,128)S(1)}, u32[]{:S(2)}, u32[]{:S(2)}) collective-permute-start(f32[2,64]{1,0:T(2,128)S(1)} %get-tuple-element.26.own), channel_id=1, source_target_pairs={{0,1},{1,0},{2,3},{3,2},{4,5},{5,4},{6,7},{7,6},{8,9},{9,8},{10,11... | collective-permute-start | bytes 1544 | tf_op jit(solution)/shard_map/ppermute | solution.py:189
  38.7 5.9 %collective-permute-start.17 = (bf16[160,384]{1,0:T(8,128)(2,1)S(1)}, bf16[160,384]{1,0:T(8,128)(2,1)S(1)}, u32[]{:S(2)}, u32[]{:S(2)}) collective-permute-start(bf16[160,384]{1,0:T(8,128)(2,1)S(1)} %hidden_b.1.own), channel_id=1, source_target_pairs={{0,1},{1,0},{2,3},{3,2},{4,5},{5,4},{6,7},{7,6},{8,9},{9,8},{10,11... | collective-permute-start | bytes 368648 | tf_op jit(solution)/shard_map/ppermute | solution.py:189
  47.4 7.8 %collective-permute-start.22 = (bf16[80,512]{1,0:T(8,128)(2,1)S(1)}, bf16[80,512]{1,0:T(8,128)(2,1)S(1)}, u32[]{:S(2)}, u32[]{:S(2)}) collective-permute-start(bf16[80,512]{1,0:T(8,128)(2,1)S(1)} %get-tuple-element.32), channel_id=1, source_target_pairs={{0,8},{2,10},{4,12},{6,14},{8,0},{10,2},{12,4},{14,6},{1,9},{3,11}... | collective-permute-start | bytes 245768 | tf_op jit(solution)/shard_map/ppermute | solution.py:233
  48.7 8.7 %collective-permute-start.23 = (bf16[80,512]{1,0:T(8,128)(2,1)S(1)}, bf16[80,512]{1,0:T(8,128)(2,1)S(1)}, u32[]{:S(2)}, u32[]{:S(2)}) collective-permute-start(bf16[80,512]{1,0:T(8,128)(2,1)S(1)} %get-tuple-element.33), channel_id=1, source_target_pairs={{0,6},{2,4},{4,2},{6,0},{8,14},{10,12},{12,10},{14,8},{1,7},{3,5},... | collective-permute-start | bytes 245768 | tf_op jit(solution)/shard_map/ppermute | solution.py:233
  50.5 10.9 %collective-permute-start.24 = (bf16[80,512]{1,0:T(8,128)(2,1)S(1)}, bf16[80,512]{1,0:T(8,128)(2,1)S(1)}, u32[]{:S(2)}, u32[]{:S(2)}) collective-permute-start(bf16[80,512]{1,0:T(8,128)(2,1)S(1)} %get-tuple-element.34), channel_id=1, source_target_pairs={{0,10},{2,8},{4,14},{6,12},{8,2},{10,0},{12,6},{14,4},{1,11},{3,9}... | collective-permute-start | bytes 245768 | tf_op jit(solution)/shard_map/ppermute | solution.py:233
  52.1 9.3 %collective-permute-start.25 = (bf16[80,512]{1,0:T(8,128)(2,1)S(1)}, bf16[80,512]{1,0:T(8,128)(2,1)S(1)}, u32[]{:S(2)}, u32[]{:S(2)}) collective-permute-start(bf16[80,512]{1,0:T(8,128)(2,1)S(1)} %get-tuple-element.35), channel_id=1, source_target_pairs={{0,2},{2,0},{4,6},{6,4},{8,10},{10,8},{12,14},{14,12},{1,3},{3,1},... | collective-permute-start | bytes 245768 | tf_op jit(solution)/shard_map/ppermute | solution.py:233
  52.5 8.9 %collective-permute-start.26 = (bf16[80,512]{1,0:T(8,128)(2,1)S(1)}, bf16[80,512]{1,0:T(8,128)(2,1)S(1)}, u32[]{:S(2)}, u32[]{:S(2)}) collective-permute-start(bf16[80,512]{1,0:T(8,128)(2,1)S(1)} %get-tuple-element.36), channel_id=1, source_target_pairs={{0,12},{2,14},{4,8},{6,10},{8,4},{10,6},{12,0},{14,2},{1,13},{3,15... | collective-permute-start | bytes 245768 | tf_op jit(solution)/shard_map/ppermute | solution.py:233
  55.2 7.7 %collective-permute-start.27 = (bf16[80,512]{1,0:T(8,128)(2,1)S(1)}, bf16[80,512]{1,0:T(8,128)(2,1)S(1)}, u32[]{:S(2)}, u32[]{:S(2)}) collective-permute-start(bf16[80,512]{1,0:T(8,128)(2,1)S(1)} %get-tuple-element.37), channel_id=1, source_target_pairs={{0,14},{2,12},{4,10},{6,8},{8,6},{10,4},{12,2},{14,0},{1,15},{3,13... | collective-permute-start | bytes 245768 | tf_op jit(solution)/shard_map/ppermute | solution.py:233
  57.4 6.3 %collective-permute-start.28 = (bf16[80,512]{1,0:T(8,128)(2,1)S(1)}, bf16[80,512]{1,0:T(8,128)(2,1)S(1)}, u32[]{:S(2)}, u32[]{:S(2)}) collective-permute-start(bf16[80,512]{1,0:T(8,128)(2,1)S(1)} %get-tuple-element.38), channel_id=1, source_target_pairs={{0,4},{2,6},{4,0},{6,2},{8,12},{10,14},{12,8},{14,10},{1,5},{3,7},... | collective-permute-start | bytes 245768 | tf_op jit(solution)/shard_map/ppermute | solution.py:233
  (14 other events, 133.9 us)

commit v7 on v6

--- a/solution.py
+++ b/solution.py
@@ -52,9 +52,11 @@
     i = iota((cfg.rp, 1), 0)
     j = div(i, cfg.rows)
     target = i - j * cfg.rows + j * BIG
+    bases = [jnp.bitwise_xor(z, r) * cfg.local * cfg.cap for r in range(cfg.groups)]
+    picks = jnp.concatenate([onehot(keys - base == target) for base in bases], axis=0)
+    picked = dot(picks, stacked).astype(BF16)
     for r in range(cfg.groups):
-        base = jnp.bitwise_xor(z, r) * cfg.local * cfg.cap
-        outs[r][...] = dot(onehot(keys - base == target), stacked).astype(BF16)
+        outs[r][...] = picked[r * cfg.rp:(r + 1) * cfg.rp]
 
 
 def place(cfg, srcs, store):
@@ -138,10 +140,13 @@
     slot = p - e * cfg.cap
     want = (qt >> 1) * (cfg.ne * per) + e * per + (qt & 1) * cfg.cap + slot
     lane = iota((1, 2 * cfg.ne * per), 1)
+    picks = []
+    for k in range(len(outs)):
+        r, dc = divmod(k, 2)
+        picks.append(onehot(lane - (r * 2 + jnp.bitwise_xor(pos_ref[1], dc)) * 2 * cfg.cap == want))
+    sorted_rows = dot(jnp.concatenate(picks, axis=0), stacked).astype(BF16)
     for k, out in enumerate(outs):
-        r, dc = divmod(k, 2)
-        place_at = (r * 2 + jnp.bitwise_xor(pos_ref[1], dc)) * 2 * cfg.cap
-        out[...] = dot(onehot(lane - place_at == want), stacked).astype(BF16)
+        out[...] = sorted_rows[k * 4 * cfg.rows:(k + 1) * 4 * cfg.rows]
 
 
 def down_first_kernel(cfg, pos_ref, own, x, core, xcore, down, info, out, full):

time: 67.5 us -> 66.9 us (level)
  no operation moved by 1% of the time
where the time goes in v7:
time: 66.9 us; the launch traced here: 66.8 us
  starting transfers between devices  25.7 us (38%)
  waiting for transfers between devices  23.6 us (35%)
  Pallas kernels  14.5 us (22%)
  local copies, waits for them, and re-layouts  1.76 us (3%)
  other arithmetic  0.94 us (1%)
    ppermute x10, starting transfers between devices, move(): lax.ppermute(x, ('expert', 'context'), [(i * 2 + k, (i ^ r) * 2 + (k ^ dc...  15.3 us
    ppermute x10, waiting for transfers between devices, move(): lax.ppermute(x, ('expert', 'context'), [(i * 2 + k, (i ^ r) * 2 + (k ^ dc...  15 us
    pallas_call x7, Pallas kernels, call(): pl.pallas_call(kernel, in_specs=[smem] + [vmem] * len(ins), out_specs=[vm...  14.5 us
    ppermute x20, starting transfers between devices, swap(): return lax.ppermute(x, axis, [(0, 1), (1, 0)])  10.5 us
    ppermute x20, waiting for transfers between devices, swap(): return lax.ppermute(x, axis, [(0, 1), (1, 0)])  8.64 us
    unnamed x16, local copies, waits for them, and re-layouts  1.72 us
  transfers between devices with their start and end apart: 30, of which 11 were waited for; matrix products, arithmetic and copies ran while one was open for 0% of the time, Pallas kernels for 10%

profile of v7, /device:TPU:0, one launch (start us, length us, event | category | flops | bytes accessed | tf_op | source)
XLA Modules:
  0.0 66.8 jit_solution(5560274846520505433)
XLA Ops:
  2.8 5.1 %collective-permute-start.7 = (bf16[80,1024]{1,0:T(8,128)(2,1)S(1)}, bf16[80,1024]{1,0:T(8,128)(2,1)S(1)}, u32[]{:S(2)}, u32[]{:S(2)}) collective-permute-start(bf16[80,1024]{1,0:T(8,128)(2,1)S(1)} %get-tuple-element.25), channel_id=1, source_target_pairs={{0,12},{2,14},{4,8},{6,10},{8,4},{10,6},{12,0},{14,2},{1,13},{3,15... | collective-permute-start | bytes 491528 | tf_op jit(solution)/shard_map/ppermute | solution.py:238
  7.9 1.5 %collective-permute-start.1 = (bf16[80,1024]{1,0:T(8,128)(2,1)S(1)}, bf16[80,1024]{1,0:T(8,128)(2,1)S(1)}, u32[]{:S(2)}, u32[]{:S(2)}) collective-permute-start(bf16[80,1024]{1,0:T(8,128)(2,1)S(1)} %get-tuple-element.23.refs_0_), channel_id=1, source_target_pairs={{0,2},{2,0},{1,3},{3,1},{4,6},{6,4},{5,7},{7,5},{8,10},{10,8},{9,1... | collective-permute-start | bytes 491528 | tf_op jit(solution)/shard_map/ppermute | solution.py:194
  10.2 2.8 %collective-permute-done.7.refs_8_ = bf16[80,1024]{1,0:T(8,128)(2,1)S(1)} collective-permute-done((bf16[80,1024]{1,0:T(8,128)(2,1)S(1)}, bf16[80,1024]{1,0:T(8,128)(2,1)S(1)}, u32[]{:S(2)}, u32[]{:S(2)}) %collective-permute-start.7) | collective-permute-done | bytes 163872 | tf_op jit(solution)/shard_map/ppermute | solution.py:238
  13.0 1.7 %collective-permute-start.9 = (bf16[80,1024]{1,0:T(8,128)(2,1)S(1)}, bf16[80,1024]{1,0:T(8,128)(2,1)S(1)}, u32[]{:S(2)}, u32[]{:S(2)}) collective-permute-start(bf16[80,1024]{1,0:T(8,128)(2,1)S(1)} %collective-permute-done.7.refs_8_), channel_id=1, source_target_pairs={{0,2},{2,0},{1,3},{3,1},{4,6},{6,4},{5,7},{7,5},{8,10},{10,8},{9,1... | collective-permute-start | bytes 491528 | tf_op jit(solution)/shard_map/ppermute | solution.py:194
  14.7 2.0 %collective-permute-done.3.refs_4_ = bf16[80,1024]{1,0:T(8,128)(2,1)S(1)} collective-permute-done((bf16[80,1024]{1,0:T(8,128)(2,1)S(1)}, bf16[80,1024]{1,0:T(8,128)(2,1)S(1)}, u32[]{:S(2)}, u32[]{:S(2)}) %collective-permute-start.3) | collective-permute-done | bytes 163872 | tf_op jit(solution)/shard_map/ppermute | solution.py:238
  16.7 1.4 %collective-permute-start.5 = (bf16[80,1024]{1,0:T(8,128)(2,1)S(1)}, bf16[80,1024]{1,0:T(8,128)(2,1)S(1)}, u32[]{:S(2)}, u32[]{:S(2)}) collective-permute-start(bf16[80,1024]{1,0:T(8,128)(2,1)S(1)} %collective-permute-done.3.refs_4_), channel_id=1, source_target_pairs={{0,2},{2,0},{1,3},{3,1},{4,6},{6,4},{5,7},{7,5},{8,10},{10,8},{9,1... | collective-permute-start | bytes 491528 | tf_op jit(solution)/shard_map/ppermute | solution.py:194
  18.7 3.2 %collective-permute-done.12.refs_0_ = bf16[80,1024]{1,0:T(8,128)(2,1)S(1)} collective-permute-done((bf16[80,1024]{1,0:T(8,128)(2,1)S(1)}, bf16[80,1024]{1,0:T(8,128)(2,1)S(1)}, u32[]{:S(2)}, u32[]{:S(2)}) %collective-permute-start.12) | collective-permute-done | bytes 163872 | tf_op jit(solution)/shard_map/ppermute | solution.py:238
  21.8 1.5 %collective-permute-start.14 = (bf16[80,1024]{1,0:T(8,128)(2,1)S(1)}, bf16[80,1024]{1,0:T(8,128)(2,1)S(1)}, u32[]{:S(2)}, u32[]{:S(2)}) collective-permute-start(bf16[80,1024]{1,0:T(8,128)(2,1)S(1)} %collective-permute-done.12.refs_0_), channel_id=1, source_target_pairs={{0,2},{2,0},{1,3},{3,1},{4,6},{6,4},{5,7},{7,5},{8,10},{10,8},{9,1... | collective-permute-start | bytes 491528 | tf_op jit(solution)/shard_map/ppermute | solution.py:194
  24.3 2.8 %collective-permute-done.14.refs_2_ = bf16[80,1024]{1,0:T(8,128)(2,1)S(1)} collective-permute-done((bf16[80,1024]{1,0:T(8,128)(2,1)S(1)}, bf16[80,1024]{1,0:T(8,128)(2,1)S(1)}, u32[]{:S(2)}, u32[]{:S(2)}) %collective-permute-start.14) | collective-permute-done | bytes 163872 | tf_op jit(solution)/shard_map/ppermute | solution.py:194
  27.2 1.5 %near.1 = (bf16[4,96,4096]{2,1,0:T(8,128)(2,1)S(1)}, f32[2,64]{1,0:T(2,128)S(1)}) custom-call(s32[3]{0:T(128)S(1)} %pad_add_fusion.pos_ref, bf16[80,1024]{1,0:T(8,128)(2,1)S(1)} %get-tuple-element.23.refs_0_, bf16[80,1024]{1,0:T(8,128)(2,1)S(1)} %collective-permute-done.refs_1_, bf16[80,1024]{1,0:T(8,128)(2,1)S(1)} %collective-permute-done.1.refs_2_, ...), custom_call_target="tpu_custom_call" | custom-call | flops 1000000000 | tf_op jit(solution)/shard_map/near/pallas_call | solution.py:227
  28.8 3.5 %hidden_a.1 = (bf16[160,384]{1,0:T(8,128)(2,1)S(1)}, bf16[2,32,4096]{2,1,0:T(8,128)(2,1)S(1)}) custom-call(s32[3]{0:T(128)S(1)} %pad_add_fusion.pos_ref, bf16[80,1024]{1,0:T(8,128)(2,1)S(1)} %collective-permute-done.12.refs_0_, bf16[80,1024]{1,0:T(8,128)(2,1)S(1)} %collective-permute-done.13.refs_1_, bf16[80,1024]{1,0:T(8,128)(2,1)S(1)} %collective-permute-done.14.refs_2_, ...), custom_call_target="tpu_custom_call" | custom-call | flops 10000000000 | tf_op jit(solution)/shard_map/hidden_a/pallas_call | solution.py:227
  32.3 1.6 %collective-permute-start.19 = (bf16[160,384]{1,0:T(8,128)(2,1)S(1)}, bf16[160,384]{1,0:T(8,128)(2,1)S(1)}, u32[]{:S(2)}, u32[]{:S(2)}) collective-permute-start(bf16[160,384]{1,0:T(8,128)(2,1)S(1)} %get-tuple-element.30.own), channel_id=1, source_target_pairs={{0,2},{2,0},{1,3},{3,1},{4,6},{6,4},{5,7},{7,5},{8,10},{10,8},{9,1... | collective-permute-start | bytes 368648 | tf_op jit(solution)/shard_map/ppermute | solution.py:194
  33.8 3.2 %hidden_b.1.own = bf16[160,384]{1,0:T(8,128)(2,1)S(1)} custom-call(s32[3]{0:T(128)S(1)} %pad_add_fusion.pos_ref, bf16[4,96,4096]{2,1,0:T(8,128)(2,1)S(1)} %get-tuple-element.27.refs_4_.near, bf16[2,32,4096]{2,1,0:T(8,128)(2,1)S(1)} %get-tuple-element.29.far, bf16[4,4096,384]{2,1,0:T(8,128)(2,1)S(1)} %copy-done, bf16[4,4096,384]{2,1,0:T(8,128)(2,1)S(1)} %copy-done.1), custom_call_target="tpu_custom_call" | custom-call | flops 10000000000 | tf_op jit(solution)/shard_map/hidden_b/pallas_call | solution.py:227
  38.7 3.9 %collective-permute-done.16.x = bf16[160,384]{1,0:T(8,128)(2,1)S(1)} collective-permute-done((bf16[160,384]{1,0:T(8,128)(2,1)S(1)}, bf16[160,384]{1,0:T(8,128)(2,1)S(1)}, u32[]{:S(2)}, u32[]{:S(2)}) %collective-permute-start.16) | collective-permute-done | bytes 122912 | tf_op jit(solution)/shard_map/ppermute | solution.py:194
  42.6 1.8 %down_a.1.before = bf16[160,1024]{1,0:T(8,128)(2,1)S(1)} custom-call(s32[3]{0:T(128)S(1)} %pad_add_fusion.pos_ref, bf16[160,384]{1,0:T(8,128)(2,1)S(1)} %get-tuple-element.30.own, bf16[160,384]{1,0:T(8,128)(2,1)S(1)} %collective-permute-done.19.x, bf16[160,384]{1,0:T(8,128)(2,1)S(1)} %collective-permute-done.20.core, ...), custom_call_target="tpu_custom_call" | custom-call | flops 10000000000 | tf_op jit(solution)/shard_map/down_a/pallas_call | solution.py:227
  44.5 2.4 %down_b.1 = (bf16[80,512]{1,0:T(8,128)(2,1)S(1)}, bf16[80,512]{1,0:T(8,128)(2,1)S(1)}, bf16[80,512]{1,0:T(8,128)(2,1)S(1)}, bf16[80,512]{1,0:T(8,128)(2,1)S(1)},...) custom-call(s32[3]{0:T(128)S(1)} %pad_add_fusion.pos_ref, ...), custom_call_target="tpu_custom_call" | custom-call | flops 10000000000 | tf_op jit(solution)/shard_map/down_b/pallas_call | solution.py:227
  46.9 1.3 %collective-permute-start.22 = (bf16[80,512]{1,0:T(8,128)(2,1)S(1)}, bf16[80,512]{1,0:T(8,128)(2,1)S(1)}, u32[]{:S(2)}, u32[]{:S(2)}) collective-permute-start(bf16[80,512]{1,0:T(8,128)(2,1)S(1)} %get-tuple-element.32), channel_id=1, source_target_pairs={{0,8},{2,10},{4,12},{6,14},{8,0},{10,2},{12,4},{14,6},{1,9},{3,11}... | collective-permute-start | bytes 245768 | tf_op jit(solution)/shard_map/ppermute | solution.py:238
  48.2 1.8 %collective-permute-start.23 = (bf16[80,512]{1,0:T(8,128)(2,1)S(1)}, bf16[80,512]{1,0:T(8,128)(2,1)S(1)}, u32[]{:S(2)}, u32[]{:S(2)}) collective-permute-start(bf16[80,512]{1,0:T(8,128)(2,1)S(1)} %get-tuple-element.33), channel_id=1, source_target_pairs={{0,6},{2,4},{4,2},{6,0},{8,14},{10,12},{12,10},{14,8},{1,7},{3,5},... | collective-permute-start | bytes 245768 | tf_op jit(solution)/shard_map/ppermute | solution.py:238
  49.9 1.6 %collective-permute-start.24 = (bf16[80,512]{1,0:T(8,128)(2,1)S(1)}, bf16[80,512]{1,0:T(8,128)(2,1)S(1)}, u32[]{:S(2)}, u32[]{:S(2)}) collective-permute-start(bf16[80,512]{1,0:T(8,128)(2,1)S(1)} %get-tuple-element.34), channel_id=1, source_target_pairs={{0,10},{2,8},{4,14},{6,12},{8,2},{10,0},{12,6},{14,4},{1,11},{3,9}... | collective-permute-start | bytes 245768 | tf_op jit(solution)/shard_map/ppermute | solution.py:238
  52.0 2.1 %collective-permute-start.26 = (bf16[80,512]{1,0:T(8,128)(2,1)S(1)}, bf16[80,512]{1,0:T(8,128)(2,1)S(1)}, u32[]{:S(2)}, u32[]{:S(2)}) collective-permute-start(bf16[80,512]{1,0:T(8,128)(2,1)S(1)} %get-tuple-element.36), channel_id=1, source_target_pairs={{0,12},{2,14},{4,8},{6,10},{8,4},{10,6},{12,0},{14,2},{1,13},{3,15... | collective-permute-start | bytes 245768 | tf_op jit(solution)/shard_map/ppermute | solution.py:238
  54.6 2.2 %collective-permute-start.27 = (bf16[80,512]{1,0:T(8,128)(2,1)S(1)}, bf16[80,512]{1,0:T(8,128)(2,1)S(1)}, u32[]{:S(2)}, u32[]{:S(2)}) collective-permute-start(bf16[80,512]{1,0:T(8,128)(2,1)S(1)} %get-tuple-element.37), channel_id=1, source_target_pairs={{0,14},{2,12},{4,10},{6,8},{8,6},{10,4},{12,2},{14,0},{1,15},{3,13... | collective-permute-start | bytes 245768 | tf_op jit(solution)/shard_map/ppermute | solution.py:238
  56.9 4.0 %collective-permute-done.24.refs_3_ = bf16[80,512]{1,0:T(8,128)(2,1)S(1)} collective-permute-done((bf16[80,512]{1,0:T(8,128)(2,1)S(1)}, bf16[80,512]{1,0:T(8,128)(2,1)S(1)}, u32[]{:S(2)}, u32[]{:S(2)}) %collective-permute-start.24) | collective-permute-done | bytes 81952 | tf_op jit(solution)/shard_map/ppermute | solution.py:238
  60.9 1.5 %collective-permute-done.27.refs_6_ = bf16[80,512]{1,0:T(8,128)(2,1)S(1)} collective-permute-done((bf16[80,512]{1,0:T(8,128)(2,1)S(1)}, bf16[80,512]{1,0:T(8,128)(2,1)S(1)}, u32[]{:S(2)}, u32[]{:S(2)}) %collective-permute-start.27) | collective-permute-done | bytes 81952 | tf_op jit(solution)/shard_map/ppermute | solution.py:238
  64.3 1.5 %collective-permute-done.29 = bf16[64,2048]{1,0:T(8,128)(2,1)S(1)} collective-permute-done((bf16[64,2048]{1,0:T(8,128)(2,1)S(1)}, bf16[64,2048]{1,0:T(8,128)(2,1)S(1)}, u32[]{:S(2)}, u32[]{:S(2)}) %collective-permute-start.29) | collective-permute-done | bytes 262176 | tf_op jit(solution)/shard_map/ppermute | solution.py:194
  (64 shorter events, 10.7 us)
Async XLA Ops:
  2.8 10.2 %collective-permute-start.7 = (bf16[80,1024]{1,0:T(8,128)(2,1)S(1)}, bf16[80,1024]{1,0:T(8,128)(2,1)S(1)}, u32[]{:S(2)}, u32[]{:S(2)}) collective-permute-start(bf16[80,1024]{1,0:T(8,128)(2,1)S(1)} %get-tuple-element.25), channel_id=1, source_target_pairs={{0,12},{2,14},{4,8},{6,10},{8,4},{10,6},{12,0},{14,2},{1,13},{3,15... | collective-permute-start | bytes 491528 | tf_op jit(solution)/shard_map/ppermute | solution.py:238
  7.9 8.8 %collective-permute-start.3 = (bf16[80,1024]{1,0:T(8,128)(2,1)S(1)}, bf16[80,1024]{1,0:T(8,128)(2,1)S(1)}, u32[]{:S(2)}, u32[]{:S(2)}) collective-permute-start(bf16[80,1024]{1,0:T(8,128)(2,1)S(1)} %get-tuple-element.24), channel_id=1, source_target_pairs={{0,4},{2,6},{4,0},{6,2},{8,12},{10,14},{12,8},{14,10},{1,5},{3,7},... | collective-permute-start | bytes 491528 | tf_op jit(solution)/shard_map/ppermute | solution.py:238
  7.9 10.2 %collective-permute-start.1 = (bf16[80,1024]{1,0:T(8,128)(2,1)S(1)}, bf16[80,1024]{1,0:T(8,128)(2,1)S(1)}, u32[]{:S(2)}, u32[]{:S(2)}) collective-permute-start(bf16[80,1024]{1,0:T(8,128)(2,1)S(1)} %get-tuple-element.23.refs_0_), channel_id=1, source_target_pairs={{0,2},{2,0},{1,3},{3,1},{4,6},{6,4},{5,7},{7,5},{8,10},{10,8},{9,1... | collective-permute-start | bytes 491528 | tf_op jit(solution)/shard_map/ppermute | solution.py:194
  9.4 8.7 %collective-permute-start = (bf16[80,1024]{1,0:T(8,128)(2,1)S(1)}, bf16[80,1024]{1,0:T(8,128)(2,1)S(1)}, u32[]{:S(2)}, u32[]{:S(2)}) collective-permute-start(bf16[80,1024]{1,0:T(8,128)(2,1)S(1)} %get-tuple-element.23.refs_0_), channel_id=1, source_target_pairs={{0,1},{1,0},{2,3},{3,2},{4,5},{5,4},{6,7},{7,6},{8,9},{9,8},{10,11... | collective-permute-start | bytes 491528 | tf_op jit(solution)/shard_map/ppermute | solution.py:194
  9.4 12.4 %collective-permute-start.12 = (bf16[80,1024]{1,0:T(8,128)(2,1)S(1)}, bf16[80,1024]{1,0:T(8,128)(2,1)S(1)}, u32[]{:S(2)}, u32[]{:S(2)}) collective-permute-start(bf16[80,1024]{1,0:T(8,128)(2,1)S(1)} %get-tuple-element.28), channel_id=1, source_target_pairs={{0,8},{2,10},{4,12},{6,14},{8,0},{10,2},{12,4},{14,6},{1,9},{3,11}... | collective-permute-start | bytes 491528 | tf_op jit(solution)/shard_map/ppermute | solution.py:238
  13.0 10.3 %collective-permute-start.9 = (bf16[80,1024]{1,0:T(8,128)(2,1)S(1)}, bf16[80,1024]{1,0:T(8,128)(2,1)S(1)}, u32[]{:S(2)}, u32[]{:S(2)}) collective-permute-start(bf16[80,1024]{1,0:T(8,128)(2,1)S(1)} %collective-permute-done.7.refs_8_), channel_id=1, source_target_pairs={{0,2},{2,0},{1,3},{3,1},{4,6},{6,4},{5,7},{7,5},{8,10},{10,8},{9,1... | collective-permute-start | bytes 491528 | tf_op jit(solution)/shard_map/ppermute | solution.py:194
  16.7 6.6 %collective-permute-start.5 = (bf16[80,1024]{1,0:T(8,128)(2,1)S(1)}, bf16[80,1024]{1,0:T(8,128)(2,1)S(1)}, u32[]{:S(2)}, u32[]{:S(2)}) collective-permute-start(bf16[80,1024]{1,0:T(8,128)(2,1)S(1)} %collective-permute-done.3.refs_4_), channel_id=1, source_target_pairs={{0,2},{2,0},{1,3},{3,1},{4,6},{6,4},{5,7},{7,5},{8,10},{10,8},{9,1... | collective-permute-start | bytes 491528 | tf_op jit(solution)/shard_map/ppermute | solution.py:194
  18.1 5.7 %collective-permute-start.2 = (bf16[80,1024]{1,0:T(8,128)(2,1)S(1)}, bf16[80,1024]{1,0:T(8,128)(2,1)S(1)}, u32[]{:S(2)}, u32[]{:S(2)}) collective-permute-start(bf16[80,1024]{1,0:T(8,128)(2,1)S(1)} %collective-permute-done.1.refs_2_), channel_id=1, source_target_pairs={{0,1},{1,0},{2,3},{3,2},{4,5},{5,4},{6,7},{7,6},{8,9},{9,8},{10,11... | collective-permute-start | bytes 491528 | tf_op jit(solution)/shard_map/ppermute | solution.py:194
  18.1 5.7 %collective-permute-start.4 = (bf16[80,1024]{1,0:T(8,128)(2,1)S(1)}, bf16[80,1024]{1,0:T(8,128)(2,1)S(1)}, u32[]{:S(2)}, u32[]{:S(2)}) collective-permute-start(bf16[80,1024]{1,0:T(8,128)(2,1)S(1)} %collective-permute-done.3.refs_4_), channel_id=1, source_target_pairs={{0,1},{1,0},{2,3},{3,2},{4,5},{5,4},{6,7},{7,6},{8,9},{9,8},{10,11... | collective-permute-start | bytes 491528 | tf_op jit(solution)/shard_map/ppermute | solution.py:194
  21.8 5.3 %collective-permute-start.14 = (bf16[80,1024]{1,0:T(8,128)(2,1)S(1)}, bf16[80,1024]{1,0:T(8,128)(2,1)S(1)}, u32[]{:S(2)}, u32[]{:S(2)}) collective-permute-start(bf16[80,1024]{1,0:T(8,128)(2,1)S(1)} %collective-permute-done.12.refs_0_), channel_id=1, source_target_pairs={{0,2},{2,0},{1,3},{3,1},{4,6},{6,4},{5,7},{7,5},{8,10},{10,8},{9,1... | collective-permute-start | bytes 491528 | tf_op jit(solution)/shard_map/ppermute | solution.py:194
  23.9 4.8 %collective-permute-start.13 = (bf16[80,1024]{1,0:T(8,128)(2,1)S(1)}, bf16[80,1024]{1,0:T(8,128)(2,1)S(1)}, u32[]{:S(2)}, u32[]{:S(2)}) collective-permute-start(bf16[80,1024]{1,0:T(8,128)(2,1)S(1)} %collective-permute-done.12.refs_0_), channel_id=1, source_target_pairs={{0,1},{1,0},{2,3},{3,2},{4,5},{5,4},{6,7},{7,6},{8,9},{9,8},{10,11... | collective-permute-start | bytes 491528 | tf_op jit(solution)/shard_map/ppermute | solution.py:194
  32.3 5.8 %collective-permute-start.19 = (bf16[160,384]{1,0:T(8,128)(2,1)S(1)}, bf16[160,384]{1,0:T(8,128)(2,1)S(1)}, u32[]{:S(2)}, u32[]{:S(2)}) collective-permute-start(bf16[160,384]{1,0:T(8,128)(2,1)S(1)} %get-tuple-element.30.own), channel_id=1, source_target_pairs={{0,2},{2,0},{1,3},{3,1},{4,6},{6,4},{5,7},{7,5},{8,10},{10,8},{9,1... | collective-permute-start | bytes 368648 | tf_op jit(solution)/shard_map/ppermute | solution.py:194
  37.0 5.5 %collective-permute-start.16 = (bf16[160,384]{1,0:T(8,128)(2,1)S(1)}, bf16[160,384]{1,0:T(8,128)(2,1)S(1)}, u32[]{:S(2)}, u32[]{:S(2)}) collective-permute-start(bf16[160,384]{1,0:T(8,128)(2,1)S(1)} %hidden_b.1.own), channel_id=1, source_target_pairs={{0,2},{2,0},{1,3},{3,1},{4,6},{6,4},{5,7},{7,5},{8,10},{10,8},{9,1... | collective-permute-start | bytes 368648 | tf_op jit(solution)/shard_map/ppermute | solution.py:194
  37.6 4.9 %collective-permute-start.20 = (bf16[160,384]{1,0:T(8,128)(2,1)S(1)}, bf16[160,384]{1,0:T(8,128)(2,1)S(1)}, u32[]{:S(2)}, u32[]{:S(2)}) collective-permute-start(bf16[160,384]{1,0:T(8,128)(2,1)S(1)} %get-tuple-element.30.own), channel_id=1, source_target_pairs={{0,1},{1,0},{2,3},{3,2},{4,5},{5,4},{6,7},{7,6},{8,9},{9,8},{10,11... | collective-permute-start | bytes 368648 | tf_op jit(solution)/shard_map/ppermute | solution.py:194
  38.0 4.5 %collective-permute-start.21 = (bf16[160,384]{1,0:T(8,128)(2,1)S(1)}, bf16[160,384]{1,0:T(8,128)(2,1)S(1)}, u32[]{:S(2)}, u32[]{:S(2)}) collective-permute-start(bf16[160,384]{1,0:T(8,128)(2,1)S(1)} %collective-permute-done.19.x), channel_id=1, source_target_pairs={{0,1},{1,0},{2,3},{3,2},{4,5},{5,4},{6,7},{7,6},{8,9},{9,8},{10,11... | collective-permute-start | bytes 368648 | tf_op jit(solution)/shard_map/ppermute | solution.py:194
  38.1 4.4 %collective-permute-start.11 = (f32[2,64]{1,0:T(2,128)S(1)}, f32[2,64]{1,0:T(2,128)S(1)}, u32[]{:S(2)}, u32[]{:S(2)}) collective-permute-start(f32[2,64]{1,0:T(2,128)S(1)} %get-tuple-element.26.own), channel_id=1, source_target_pairs={{0,1},{1,0},{2,3},{3,2},{4,5},{5,4},{6,7},{7,6},{8,9},{9,8},{10,11... | collective-permute-start | bytes 1544 | tf_op jit(solution)/shard_map/ppermute | solution.py:194
  38.6 5.9 %collective-permute-start.17 = (bf16[160,384]{1,0:T(8,128)(2,1)S(1)}, bf16[160,384]{1,0:T(8,128)(2,1)S(1)}, u32[]{:S(2)}, u32[]{:S(2)}) collective-permute-start(bf16[160,384]{1,0:T(8,128)(2,1)S(1)} %hidden_b.1.own), channel_id=1, source_target_pairs={{0,1},{1,0},{2,3},{3,2},{4,5},{5,4},{6,7},{7,6},{8,9},{9,8},{10,11... | collective-permute-start | bytes 368648 | tf_op jit(solution)/shard_map/ppermute | solution.py:194
  46.9 7.8 %collective-permute-start.22 = (bf16[80,512]{1,0:T(8,128)(2,1)S(1)}, bf16[80,512]{1,0:T(8,128)(2,1)S(1)}, u32[]{:S(2)}, u32[]{:S(2)}) collective-permute-start(bf16[80,512]{1,0:T(8,128)(2,1)S(1)} %get-tuple-element.32), channel_id=1, source_target_pairs={{0,8},{2,10},{4,12},{6,14},{8,0},{10,2},{12,4},{14,6},{1,9},{3,11}... | collective-permute-start | bytes 245768 | tf_op jit(solution)/shard_map/ppermute | solution.py:238
  48.2 8.7 %collective-permute-start.23 = (bf16[80,512]{1,0:T(8,128)(2,1)S(1)}, bf16[80,512]{1,0:T(8,128)(2,1)S(1)}, u32[]{:S(2)}, u32[]{:S(2)}) collective-permute-start(bf16[80,512]{1,0:T(8,128)(2,1)S(1)} %get-tuple-element.33), channel_id=1, source_target_pairs={{0,6},{2,4},{4,2},{6,0},{8,14},{10,12},{12,10},{14,8},{1,7},{3,5},... | collective-permute-start | bytes 245768 | tf_op jit(solution)/shard_map/ppermute | solution.py:238
  49.9 10.9 %collective-permute-start.24 = (bf16[80,512]{1,0:T(8,128)(2,1)S(1)}, bf16[80,512]{1,0:T(8,128)(2,1)S(1)}, u32[]{:S(2)}, u32[]{:S(2)}) collective-permute-start(bf16[80,512]{1,0:T(8,128)(2,1)S(1)} %get-tuple-element.34), channel_id=1, source_target_pairs={{0,10},{2,8},{4,14},{6,12},{8,2},{10,0},{12,6},{14,4},{1,11},{3,9}... | collective-permute-start | bytes 245768 | tf_op jit(solution)/shard_map/ppermute | solution.py:238
  51.6 9.3 %collective-permute-start.25 = (bf16[80,512]{1,0:T(8,128)(2,1)S(1)}, bf16[80,512]{1,0:T(8,128)(2,1)S(1)}, u32[]{:S(2)}, u32[]{:S(2)}) collective-permute-start(bf16[80,512]{1,0:T(8,128)(2,1)S(1)} %get-tuple-element.35), channel_id=1, source_target_pairs={{0,2},{2,0},{4,6},{6,4},{8,10},{10,8},{12,14},{14,12},{1,3},{3,1},... | collective-permute-start | bytes 245768 | tf_op jit(solution)/shard_map/ppermute | solution.py:238
  52.0 8.9 %collective-permute-start.26 = (bf16[80,512]{1,0:T(8,128)(2,1)S(1)}, bf16[80,512]{1,0:T(8,128)(2,1)S(1)}, u32[]{:S(2)}, u32[]{:S(2)}) collective-permute-start(bf16[80,512]{1,0:T(8,128)(2,1)S(1)} %get-tuple-element.36), channel_id=1, source_target_pairs={{0,12},{2,14},{4,8},{6,10},{8,4},{10,6},{12,0},{14,2},{1,13},{3,15... | collective-permute-start | bytes 245768 | tf_op jit(solution)/shard_map/ppermute | solution.py:238
  54.6 7.7 %collective-permute-start.27 = (bf16[80,512]{1,0:T(8,128)(2,1)S(1)}, bf16[80,512]{1,0:T(8,128)(2,1)S(1)}, u32[]{:S(2)}, u32[]{:S(2)}) collective-permute-start(bf16[80,512]{1,0:T(8,128)(2,1)S(1)} %get-tuple-element.37), channel_id=1, source_target_pairs={{0,14},{2,12},{4,10},{6,8},{8,6},{10,4},{12,2},{14,0},{1,15},{3,13... | collective-permute-start | bytes 245768 | tf_op jit(solution)/shard_map/ppermute | solution.py:238
  56.9 6.4 %collective-permute-start.28 = (bf16[80,512]{1,0:T(8,128)(2,1)S(1)}, bf16[80,512]{1,0:T(8,128)(2,1)S(1)}, u32[]{:S(2)}, u32[]{:S(2)}) collective-permute-start(bf16[80,512]{1,0:T(8,128)(2,1)S(1)} %get-tuple-element.38), channel_id=1, source_target_pairs={{0,4},{2,6},{4,0},{6,2},{8,12},{10,14},{12,8},{14,10},{1,5},{3,7},... | collective-permute-start | bytes 245768 | tf_op jit(solution)/shard_map/ppermute | solution.py:238
  (14 other events, 133.5 us)

commit v8 on v7

--- a/solution.py
+++ b/solution.py
@@ -93,13 +93,17 @@
     for k, r in enumerate(cfg.visits):
         rel = rel + jnp.where((s >> 2) == r, 4 * k, 0)
     compact = onehot(iota((1, cfg.sources * 8), 1) == rel * 8 + slot)
+    found = []
     for k in range(cfg.ne // 2):
         e = first + k
         x = jnp.concatenate([near[e], far[k]], axis=0)
         both = dot(x, jnp.concatenate([gate[e], up[e]], axis=1))
         g, u = jnp.split(both, 2, axis=1)
-        hid = (g / (1.0 + jnp.exp(-g)) * u).astype(BF16)
-        out_ref[k * per:(k + 1) * per] = dot(compact, hid).astype(BF16)
+        found.append((g / (1.0 + jnp.exp(-g)) * u).astype(BF16))
+    packed = dot(compact, jnp.concatenate(found, axis=1)).astype(BF16)
+    f = out_ref.shape[1]
+    for k in range(cfg.ne // 2):
+        out_ref[k * per:(k + 1) * per] = packed[:, k * f:(k + 1) * f]
 
 
 def hidden_first_kernel(cfg, pos_ref, *refs):

time: 66.9 us -> 65.5 us (0.979)
  Pallas kernels: 14.5 us -> 13.1 us
    pallas_call x7, Pallas kernels: 14.5 us -> 13.1 us  [call(): pl.pallas_call(kernel, in_specs=[smem] + [vmem] * len(ins), out_specs=[vm...]
  transfers between devices with their start and end apart: 30 -> 30, of which waited for: 11 -> 11; matrix products, arithmetic and copies ran while one was open for 0% -> 0% of each run, Pallas kernels for 10% -> 9%
where the time goes in v8:
time: 65.5 us; the launch traced here: 65.3 us
  starting transfers between devices  25.6 us (39%)
  waiting for transfers between devices  23.7 us (36%)
  Pallas kernels  13.1 us (20%)
  local copies, waits for them, and re-layouts  1.76 us (3%)
  other arithmetic  0.94 us (1%)
    ppermute x10, starting transfers between devices, move(): lax.ppermute(x, ('expert', 'context'), [(i * 2 + k, (i ^ r) * 2 + (k ^ dc...  15.3 us
    ppermute x10, waiting for transfers between devices, move(): lax.ppermute(x, ('expert', 'context'), [(i * 2 + k, (i ^ r) * 2 + (k ^ dc...  15 us
    pallas_call x7, Pallas kernels, call(): pl.pallas_call(kernel, in_specs=[smem] + [vmem] * len(ins), out_specs=[vm...  13.1 us
    ppermute x20, starting transfers between devices, swap(): return lax.ppermute(x, axis, [(0, 1), (1, 0)])  10.4 us
    ppermute x20, waiting for transfers between devices, swap(): return lax.ppermute(x, axis, [(0, 1), (1, 0)])  8.74 us
    unnamed x16, local copies, waits for them, and re-layouts  1.72 us
  transfers between devices with their start and end apart: 30, of which 11 were waited for; matrix products, arithmetic and copies ran while one was open for 0% of the time, Pallas kernels for 9%

profile of v8, /device:TPU:0, one launch (start us, length us, event | category | flops | bytes accessed | tf_op | source)
XLA Modules:
  0.0 65.3 jit_solution(4916531730088844730)
XLA Ops:
  2.8 5.1 %collective-permute-start.7 = (bf16[80,1024]{1,0:T(8,128)(2,1)S(1)}, bf16[80,1024]{1,0:T(8,128)(2,1)S(1)}, u32[]{:S(2)}, u32[]{:S(2)}) collective-permute-start(bf16[80,1024]{1,0:T(8,128)(2,1)S(1)} %get-tuple-element.25), channel_id=1, source_target_pairs={{0,12},{2,14},{4,8},{6,10},{8,4},{10,6},{12,0},{14,2},{1,13},{3,15... | collective-permute-start | bytes 491528 | tf_op jit(solution)/shard_map/ppermute | solution.py:242
  7.9 1.5 %collective-permute-start.1 = (bf16[80,1024]{1,0:T(8,128)(2,1)S(1)}, bf16[80,1024]{1,0:T(8,128)(2,1)S(1)}, u32[]{:S(2)}, u32[]{:S(2)}) collective-permute-start(bf16[80,1024]{1,0:T(8,128)(2,1)S(1)} %get-tuple-element.23.refs_0_), channel_id=1, source_target_pairs={{0,2},{2,0},{1,3},{3,1},{4,6},{6,4},{5,7},{7,5},{8,10},{10,8},{9,1... | collective-permute-start | bytes 491528 | tf_op jit(solution)/shard_map/ppermute | solution.py:198
  10.2 2.8 %collective-permute-done.7.refs_8_ = bf16[80,1024]{1,0:T(8,128)(2,1)S(1)} collective-permute-done((bf16[80,1024]{1,0:T(8,128)(2,1)S(1)}, bf16[80,1024]{1,0:T(8,128)(2,1)S(1)}, u32[]{:S(2)}, u32[]{:S(2)}) %collective-permute-start.7) | collective-permute-done | bytes 163872 | tf_op jit(solution)/shard_map/ppermute | solution.py:242
  13.0 1.7 %collective-permute-start.9 = (bf16[80,1024]{1,0:T(8,128)(2,1)S(1)}, bf16[80,1024]{1,0:T(8,128)(2,1)S(1)}, u32[]{:S(2)}, u32[]{:S(2)}) collective-permute-start(bf16[80,1024]{1,0:T(8,128)(2,1)S(1)} %collective-permute-done.7.refs_8_), channel_id=1, source_target_pairs={{0,2},{2,0},{1,3},{3,1},{4,6},{6,4},{5,7},{7,5},{8,10},{10,8},{9,1... | collective-permute-start | bytes 491528 | tf_op jit(solution)/shard_map/ppermute | solution.py:198
  14.7 2.0 %collective-permute-done.3.refs_4_ = bf16[80,1024]{1,0:T(8,128)(2,1)S(1)} collective-permute-done((bf16[80,1024]{1,0:T(8,128)(2,1)S(1)}, bf16[80,1024]{1,0:T(8,128)(2,1)S(1)}, u32[]{:S(2)}, u32[]{:S(2)}) %collective-permute-start.3) | collective-permute-done | bytes 163872 | tf_op jit(solution)/shard_map/ppermute | solution.py:242
  16.7 1.4 %collective-permute-start.5 = (bf16[80,1024]{1,0:T(8,128)(2,1)S(1)}, bf16[80,1024]{1,0:T(8,128)(2,1)S(1)}, u32[]{:S(2)}, u32[]{:S(2)}) collective-permute-start(bf16[80,1024]{1,0:T(8,128)(2,1)S(1)} %collective-permute-done.3.refs_4_), channel_id=1, source_target_pairs={{0,2},{2,0},{1,3},{3,1},{4,6},{6,4},{5,7},{7,5},{8,10},{10,8},{9,1... | collective-permute-start | bytes 491528 | tf_op jit(solution)/shard_map/ppermute | solution.py:198
  18.7 3.2 %collective-permute-done.12.refs_0_ = bf16[80,1024]{1,0:T(8,128)(2,1)S(1)} collective-permute-done((bf16[80,1024]{1,0:T(8,128)(2,1)S(1)}, bf16[80,1024]{1,0:T(8,128)(2,1)S(1)}, u32[]{:S(2)}, u32[]{:S(2)}) %collective-permute-start.12) | collective-permute-done | bytes 163872 | tf_op jit(solution)/shard_map/ppermute | solution.py:242
  21.8 1.5 %collective-permute-start.14 = (bf16[80,1024]{1,0:T(8,128)(2,1)S(1)}, bf16[80,1024]{1,0:T(8,128)(2,1)S(1)}, u32[]{:S(2)}, u32[]{:S(2)}) collective-permute-start(bf16[80,1024]{1,0:T(8,128)(2,1)S(1)} %collective-permute-done.12.refs_0_), channel_id=1, source_target_pairs={{0,2},{2,0},{1,3},{3,1},{4,6},{6,4},{5,7},{7,5},{8,10},{10,8},{9,1... | collective-permute-start | bytes 491528 | tf_op jit(solution)/shard_map/ppermute | solution.py:198
  24.3 2.8 %collective-permute-done.14.refs_2_ = bf16[80,1024]{1,0:T(8,128)(2,1)S(1)} collective-permute-done((bf16[80,1024]{1,0:T(8,128)(2,1)S(1)}, bf16[80,1024]{1,0:T(8,128)(2,1)S(1)}, u32[]{:S(2)}, u32[]{:S(2)}) %collective-permute-start.14) | collective-permute-done | bytes 163872 | tf_op jit(solution)/shard_map/ppermute | solution.py:198
  27.2 1.5 %near.1 = (bf16[4,96,4096]{2,1,0:T(8,128)(2,1)S(1)}, f32[2,64]{1,0:T(2,128)S(1)}) custom-call(s32[3]{0:T(128)S(1)} %pad_add_fusion.pos_ref, bf16[80,1024]{1,0:T(8,128)(2,1)S(1)} %get-tuple-element.23.refs_0_, bf16[80,1024]{1,0:T(8,128)(2,1)S(1)} %collective-permute-done.refs_1_, bf16[80,1024]{1,0:T(8,128)(2,1)S(1)} %collective-permute-done.1.refs_2_, ...), custom_call_target="tpu_custom_call" | custom-call | flops 1000000000 | tf_op jit(solution)/shard_map/near/pallas_call | solution.py:231
  28.8 2.8 %hidden_a.1 = (bf16[160,384]{1,0:T(8,128)(2,1)S(1)}, bf16[2,32,4096]{2,1,0:T(8,128)(2,1)S(1)}) custom-call(s32[3]{0:T(128)S(1)} %pad_add_fusion.pos_ref, bf16[80,1024]{1,0:T(8,128)(2,1)S(1)} %collective-permute-done.12.refs_0_, bf16[80,1024]{1,0:T(8,128)(2,1)S(1)} %collective-permute-done.13.refs_1_, bf16[80,1024]{1,0:T(8,128)(2,1)S(1)} %collective-permute-done.14.refs_2_, ...), custom_call_target="tpu_custom_call" | custom-call | flops 10000000000 | tf_op jit(solution)/shard_map/hidden_a/pallas_call | solution.py:231
  31.5 1.6 %collective-permute-start.19 = (bf16[160,384]{1,0:T(8,128)(2,1)S(1)}, bf16[160,384]{1,0:T(8,128)(2,1)S(1)}, u32[]{:S(2)}, u32[]{:S(2)}) collective-permute-start(bf16[160,384]{1,0:T(8,128)(2,1)S(1)} %get-tuple-element.30.own), channel_id=1, source_target_pairs={{0,2},{2,0},{1,3},{3,1},{4,6},{6,4},{5,7},{7,5},{8,10},{10,8},{9,1... | collective-permute-start | bytes 368648 | tf_op jit(solution)/shard_map/ppermute | solution.py:198
  33.1 2.5 %hidden_b.1.own = bf16[160,384]{1,0:T(8,128)(2,1)S(1)} custom-call(s32[3]{0:T(128)S(1)} %pad_add_fusion.pos_ref, bf16[4,96,4096]{2,1,0:T(8,128)(2,1)S(1)} %get-tuple-element.27.refs_4_.near, bf16[2,32,4096]{2,1,0:T(8,128)(2,1)S(1)} %get-tuple-element.29.far, bf16[4,4096,384]{2,1,0:T(8,128)(2,1)S(1)} %copy-done, bf16[4,4096,384]{2,1,0:T(8,128)(2,1)S(1)} %copy-done.1), custom_call_target="tpu_custom_call" | custom-call | flops 10000000000 | tf_op jit(solution)/shard_map/hidden_b/pallas_call | solution.py:231
  37.8 3.3 %collective-permute-done.16.x = bf16[160,384]{1,0:T(8,128)(2,1)S(1)} collective-permute-done((bf16[160,384]{1,0:T(8,128)(2,1)S(1)}, bf16[160,384]{1,0:T(8,128)(2,1)S(1)}, u32[]{:S(2)}, u32[]{:S(2)}) %collective-permute-start.16) | collective-permute-done | bytes 122912 | tf_op jit(solution)/shard_map/ppermute | solution.py:198
  41.2 1.8 %down_a.1.before = bf16[160,1024]{1,0:T(8,128)(2,1)S(1)} custom-call(s32[3]{0:T(128)S(1)} %pad_add_fusion.pos_ref, bf16[160,384]{1,0:T(8,128)(2,1)S(1)} %get-tuple-element.30.own, bf16[160,384]{1,0:T(8,128)(2,1)S(1)} %collective-permute-done.19.x, bf16[160,384]{1,0:T(8,128)(2,1)S(1)} %collective-permute-done.20.core, ...), custom_call_target="tpu_custom_call" | custom-call | flops 10000000000 | tf_op jit(solution)/shard_map/down_a/pallas_call | solution.py:231
  43.0 2.4 %down_b.1 = (bf16[80,512]{1,0:T(8,128)(2,1)S(1)}, bf16[80,512]{1,0:T(8,128)(2,1)S(1)}, bf16[80,512]{1,0:T(8,128)(2,1)S(1)}, bf16[80,512]{1,0:T(8,128)(2,1)S(1)},...) custom-call(s32[3]{0:T(128)S(1)} %pad_add_fusion.pos_ref, ...), custom_call_target="tpu_custom_call" | custom-call | flops 10000000000 | tf_op jit(solution)/shard_map/down_b/pallas_call | solution.py:231
  45.4 1.3 %collective-permute-start.22 = (bf16[80,512]{1,0:T(8,128)(2,1)S(1)}, bf16[80,512]{1,0:T(8,128)(2,1)S(1)}, u32[]{:S(2)}, u32[]{:S(2)}) collective-permute-start(bf16[80,512]{1,0:T(8,128)(2,1)S(1)} %get-tuple-element.32), channel_id=1, source_target_pairs={{0,8},{2,10},{4,12},{6,14},{8,0},{10,2},{12,4},{14,6},{1,9},{3,11}... | collective-permute-start | bytes 245768 | tf_op jit(solution)/shard_map/ppermute | solution.py:242
  46.8 1.8 %collective-permute-start.23 = (bf16[80,512]{1,0:T(8,128)(2,1)S(1)}, bf16[80,512]{1,0:T(8,128)(2,1)S(1)}, u32[]{:S(2)}, u32[]{:S(2)}) collective-permute-start(bf16[80,512]{1,0:T(8,128)(2,1)S(1)} %get-tuple-element.33), channel_id=1, source_target_pairs={{0,6},{2,4},{4,2},{6,0},{8,14},{10,12},{12,10},{14,8},{1,7},{3,5},... | collective-permute-start | bytes 245768 | tf_op jit(solution)/shard_map/ppermute | solution.py:242
  48.5 1.6 %collective-permute-start.24 = (bf16[80,512]{1,0:T(8,128)(2,1)S(1)}, bf16[80,512]{1,0:T(8,128)(2,1)S(1)}, u32[]{:S(2)}, u32[]{:S(2)}) collective-permute-start(bf16[80,512]{1,0:T(8,128)(2,1)S(1)} %get-tuple-element.34), channel_id=1, source_target_pairs={{0,10},{2,8},{4,14},{6,12},{8,2},{10,0},{12,6},{14,4},{1,11},{3,9}... | collective-permute-start | bytes 245768 | tf_op jit(solution)/shard_map/ppermute | solution.py:242
  50.5 2.1 %collective-permute-start.26 = (bf16[80,512]{1,0:T(8,128)(2,1)S(1)}, bf16[80,512]{1,0:T(8,128)(2,1)S(1)}, u32[]{:S(2)}, u32[]{:S(2)}) collective-permute-start(bf16[80,512]{1,0:T(8,128)(2,1)S(1)} %get-tuple-element.36), channel_id=1, source_target_pairs={{0,12},{2,14},{4,8},{6,10},{8,4},{10,6},{12,0},{14,2},{1,13},{3,15... | collective-permute-start | bytes 245768 | tf_op jit(solution)/shard_map/ppermute | solution.py:242
  53.2 2.2 %collective-permute-start.27 = (bf16[80,512]{1,0:T(8,128)(2,1)S(1)}, bf16[80,512]{1,0:T(8,128)(2,1)S(1)}, u32[]{:S(2)}, u32[]{:S(2)}) collective-permute-start(bf16[80,512]{1,0:T(8,128)(2,1)S(1)} %get-tuple-element.37), channel_id=1, source_target_pairs={{0,14},{2,12},{4,10},{6,8},{8,6},{10,4},{12,2},{14,0},{1,15},{3,13... | collective-permute-start | bytes 245768 | tf_op jit(solution)/shard_map/ppermute | solution.py:242
  55.4 4.0 %collective-permute-done.24.refs_3_ = bf16[80,512]{1,0:T(8,128)(2,1)S(1)} collective-permute-done((bf16[80,512]{1,0:T(8,128)(2,1)S(1)}, bf16[80,512]{1,0:T(8,128)(2,1)S(1)}, u32[]{:S(2)}, u32[]{:S(2)}) %collective-permute-start.24) | collective-permute-done | bytes 81952 | tf_op jit(solution)/shard_map/ppermute | solution.py:242
  59.5 1.5 %collective-permute-done.27.refs_6_ = bf16[80,512]{1,0:T(8,128)(2,1)S(1)} collective-permute-done((bf16[80,512]{1,0:T(8,128)(2,1)S(1)}, bf16[80,512]{1,0:T(8,128)(2,1)S(1)}, u32[]{:S(2)}, u32[]{:S(2)}) %collective-permute-start.27) | collective-permute-done | bytes 81952 | tf_op jit(solution)/shard_map/ppermute | solution.py:242
  62.9 1.5 %collective-permute-done.29 = bf16[64,2048]{1,0:T(8,128)(2,1)S(1)} collective-permute-done((bf16[64,2048]{1,0:T(8,128)(2,1)S(1)}, bf16[64,2048]{1,0:T(8,128)(2,1)S(1)}, u32[]{:S(2)}, u32[]{:S(2)}) %collective-permute-start.29) | collective-permute-done | bytes 262176 | tf_op jit(solution)/shard_map/ppermute | solution.py:198
  (64 shorter events, 11.3 us)
Async XLA Ops:
  2.8 10.2 %collective-permute-start.7 = (bf16[80,1024]{1,0:T(8,128)(2,1)S(1)}, bf16[80,1024]{1,0:T(8,128)(2,1)S(1)}, u32[]{:S(2)}, u32[]{:S(2)}) collective-permute-start(bf16[80,1024]{1,0:T(8,128)(2,1)S(1)} %get-tuple-element.25), channel_id=1, source_target_pairs={{0,12},{2,14},{4,8},{6,10},{8,4},{10,6},{12,0},{14,2},{1,13},{3,15... | collective-permute-start | bytes 491528 | tf_op jit(solution)/shard_map/ppermute | solution.py:242
  7.9 8.8 %collective-permute-start.3 = (bf16[80,1024]{1,0:T(8,128)(2,1)S(1)}, bf16[80,1024]{1,0:T(8,128)(2,1)S(1)}, u32[]{:S(2)}, u32[]{:S(2)}) collective-permute-start(bf16[80,1024]{1,0:T(8,128)(2,1)S(1)} %get-tuple-element.24), channel_id=1, source_target_pairs={{0,4},{2,6},{4,0},{6,2},{8,12},{10,14},{12,8},{14,10},{1,5},{3,7},... | collective-permute-start | bytes 491528 | tf_op jit(solution)/shard_map/ppermute | solution.py:242
  7.9 10.2 %collective-permute-start.1 = (bf16[80,1024]{1,0:T(8,128)(2,1)S(1)}, bf16[80,1024]{1,0:T(8,128)(2,1)S(1)}, u32[]{:S(2)}, u32[]{:S(2)}) collective-permute-start(bf16[80,1024]{1,0:T(8,128)(2,1)S(1)} %get-tuple-element.23.refs_0_), channel_id=1, source_target_pairs={{0,2},{2,0},{1,3},{3,1},{4,6},{6,4},{5,7},{7,5},{8,10},{10,8},{9,1... | collective-permute-start | bytes 491528 | tf_op jit(solution)/shard_map/ppermute | solution.py:198
  9.4 8.7 %collective-permute-start = (bf16[80,1024]{1,0:T(8,128)(2,1)S(1)}, bf16[80,1024]{1,0:T(8,128)(2,1)S(1)}, u32[]{:S(2)}, u32[]{:S(2)}) collective-permute-start(bf16[80,1024]{1,0:T(8,128)(2,1)S(1)} %get-tuple-element.23.refs_0_), channel_id=1, source_target_pairs={{0,1},{1,0},{2,3},{3,2},{4,5},{5,4},{6,7},{7,6},{8,9},{9,8},{10,11... | collective-permute-start | bytes 491528 | tf_op jit(solution)/shard_map/ppermute | solution.py:198
  9.4 12.4 %collective-permute-start.12 = (bf16[80,1024]{1,0:T(8,128)(2,1)S(1)}, bf16[80,1024]{1,0:T(8,128)(2,1)S(1)}, u32[]{:S(2)}, u32[]{:S(2)}) collective-permute-start(bf16[80,1024]{1,0:T(8,128)(2,1)S(1)} %get-tuple-element.28), channel_id=1, source_target_pairs={{0,8},{2,10},{4,12},{6,14},{8,0},{10,2},{12,4},{14,6},{1,9},{3,11}... | collective-permute-start | bytes 491528 | tf_op jit(solution)/shard_map/ppermute | solution.py:242
  13.0 10.3 %collective-permute-start.9 = (bf16[80,1024]{1,0:T(8,128)(2,1)S(1)}, bf16[80,1024]{1,0:T(8,128)(2,1)S(1)}, u32[]{:S(2)}, u32[]{:S(2)}) collective-permute-start(bf16[80,1024]{1,0:T(8,128)(2,1)S(1)} %collective-permute-done.7.refs_8_), channel_id=1, source_target_pairs={{0,2},{2,0},{1,3},{3,1},{4,6},{6,4},{5,7},{7,5},{8,10},{10,8},{9,1... | collective-permute-start | bytes 491528 | tf_op jit(solution)/shard_map/ppermute | solution.py:198
  16.7 6.6 %collective-permute-start.5 = (bf16[80,1024]{1,0:T(8,128)(2,1)S(1)}, bf16[80,1024]{1,0:T(8,128)(2,1)S(1)}, u32[]{:S(2)}, u32[]{:S(2)}) collective-permute-start(bf16[80,1024]{1,0:T(8,128)(2,1)S(1)} %collective-permute-done.3.refs_4_), channel_id=1, source_target_pairs={{0,2},{2,0},{1,3},{3,1},{4,6},{6,4},{5,7},{7,5},{8,10},{10,8},{9,1... | collective-permute-start | bytes 491528 | tf_op jit(solution)/shard_map/ppermute | solution.py:198
  18.1 5.7 %collective-permute-start.2 = (bf16[80,1024]{1,0:T(8,128)(2,1)S(1)}, bf16[80,1024]{1,0:T(8,128)(2,1)S(1)}, u32[]{:S(2)}, u32[]{:S(2)}) collective-permute-start(bf16[80,1024]{1,0:T(8,128)(2,1)S(1)} %collective-permute-done.1.refs_2_), channel_id=1, source_target_pairs={{0,1},{1,0},{2,3},{3,2},{4,5},{5,4},{6,7},{7,6},{8,9},{9,8},{10,11... | collective-permute-start | bytes 491528 | tf_op jit(solution)/shard_map/ppermute | solution.py:198
  18.1 5.7 %collective-permute-start.4 = (bf16[80,1024]{1,0:T(8,128)(2,1)S(1)}, bf16[80,1024]{1,0:T(8,128)(2,1)S(1)}, u32[]{:S(2)}, u32[]{:S(2)}) collective-permute-start(bf16[80,1024]{1,0:T(8,128)(2,1)S(1)} %collective-permute-done.3.refs_4_), channel_id=1, source_target_pairs={{0,1},{1,0},{2,3},{3,2},{4,5},{5,4},{6,7},{7,6},{8,9},{9,8},{10,11... | collective-permute-start | bytes 491528 | tf_op jit(solution)/shard_map/ppermute | solution.py:198
  21.8 5.3 %collective-permute-start.14 = (bf16[80,1024]{1,0:T(8,128)(2,1)S(1)}, bf16[80,1024]{1,0:T(8,128)(2,1)S(1)}, u32[]{:S(2)}, u32[]{:S(2)}) collective-permute-start(bf16[80,1024]{1,0:T(8,128)(2,1)S(1)} %collective-permute-done.12.refs_0_), channel_id=1, source_target_pairs={{0,2},{2,0},{1,3},{3,1},{4,6},{6,4},{5,7},{7,5},{8,10},{10,8},{9,1... | collective-permute-start | bytes 491528 | tf_op jit(solution)/shard_map/ppermute | solution.py:198
  23.3 3.8 %collective-permute-start.8 = (bf16[80,1024]{1,0:T(8,128)(2,1)S(1)}, bf16[80,1024]{1,0:T(8,128)(2,1)S(1)}, u32[]{:S(2)}, u32[]{:S(2)}) collective-permute-start(bf16[80,1024]{1,0:T(8,128)(2,1)S(1)} %collective-permute-done.7.refs_8_), channel_id=1, source_target_pairs={{0,1},{1,0},{2,3},{3,2},{4,5},{5,4},{6,7},{7,6},{8,9},{9,8},{10,11... | collective-permute-start | bytes 491528 | tf_op jit(solution)/shard_map/ppermute | solution.py:198
  23.3 3.8 %collective-permute-start.10 = (bf16[80,1024]{1,0:T(8,128)(2,1)S(1)}, bf16[80,1024]{1,0:T(8,128)(2,1)S(1)}, u32[]{:S(2)}, u32[]{:S(2)}) collective-permute-start(bf16[80,1024]{1,0:T(8,128)(2,1)S(1)} %collective-permute-done.9.refs_10_), channel_id=1, source_target_pairs={{0,1},{1,0},{2,3},{3,2},{4,5},{5,4},{6,7},{7,6},{8,9},{9,8},{10,11... | collective-permute-start | bytes 491528 | tf_op jit(solution)/shard_map/ppermute | solution.py:198
  23.9 4.8 %collective-permute-start.13 = (bf16[80,1024]{1,0:T(8,128)(2,1)S(1)}, bf16[80,1024]{1,0:T(8,128)(2,1)S(1)}, u32[]{:S(2)}, u32[]{:S(2)}) collective-permute-start(bf16[80,1024]{1,0:T(8,128)(2,1)S(1)} %collective-permute-done.12.refs_0_), channel_id=1, source_target_pairs={{0,1},{1,0},{2,3},{3,2},{4,5},{5,4},{6,7},{7,6},{8,9},{9,8},{10,11... | collective-permute-start | bytes 491528 | tf_op jit(solution)/shard_map/ppermute | solution.py:198
  31.5 5.8 %collective-permute-start.19 = (bf16[160,384]{1,0:T(8,128)(2,1)S(1)}, bf16[160,384]{1,0:T(8,128)(2,1)S(1)}, u32[]{:S(2)}, u32[]{:S(2)}) collective-permute-start(bf16[160,384]{1,0:T(8,128)(2,1)S(1)} %get-tuple-element.30.own), channel_id=1, source_target_pairs={{0,2},{2,0},{1,3},{3,1},{4,6},{6,4},{5,7},{7,5},{8,10},{10,8},{9,1... | collective-permute-start | bytes 368648 | tf_op jit(solution)/shard_map/ppermute | solution.py:198
  35.6 5.5 %collective-permute-start.16 = (bf16[160,384]{1,0:T(8,128)(2,1)S(1)}, bf16[160,384]{1,0:T(8,128)(2,1)S(1)}, u32[]{:S(2)}, u32[]{:S(2)}) collective-permute-start(bf16[160,384]{1,0:T(8,128)(2,1)S(1)} %hidden_b.1.own), channel_id=1, source_target_pairs={{0,2},{2,0},{1,3},{3,1},{4,6},{6,4},{5,7},{7,5},{8,10},{10,8},{9,1... | collective-permute-start | bytes 368648 | tf_op jit(solution)/shard_map/ppermute | solution.py:198
  36.2 4.9 %collective-permute-start.20 = (bf16[160,384]{1,0:T(8,128)(2,1)S(1)}, bf16[160,384]{1,0:T(8,128)(2,1)S(1)}, u32[]{:S(2)}, u32[]{:S(2)}) collective-permute-start(bf16[160,384]{1,0:T(8,128)(2,1)S(1)} %get-tuple-element.30.own), channel_id=1, source_target_pairs={{0,1},{1,0},{2,3},{3,2},{4,5},{5,4},{6,7},{7,6},{8,9},{9,8},{10,11... | collective-permute-start | bytes 368648 | tf_op jit(solution)/shard_map/ppermute | solution.py:198
  37.8 5.2 %collective-permute-start.17 = (bf16[160,384]{1,0:T(8,128)(2,1)S(1)}, bf16[160,384]{1,0:T(8,128)(2,1)S(1)}, u32[]{:S(2)}, u32[]{:S(2)}) collective-permute-start(bf16[160,384]{1,0:T(8,128)(2,1)S(1)} %hidden_b.1.own), channel_id=1, source_target_pairs={{0,1},{1,0},{2,3},{3,2},{4,5},{5,4},{6,7},{7,6},{8,9},{9,8},{10,11... | collective-permute-start | bytes 368648 | tf_op jit(solution)/shard_map/ppermute | solution.py:198
  45.4 7.8 %collective-permute-start.22 = (bf16[80,512]{1,0:T(8,128)(2,1)S(1)}, bf16[80,512]{1,0:T(8,128)(2,1)S(1)}, u32[]{:S(2)}, u32[]{:S(2)}) collective-permute-start(bf16[80,512]{1,0:T(8,128)(2,1)S(1)} %get-tuple-element.32), channel_id=1, source_target_pairs={{0,8},{2,10},{4,12},{6,14},{8,0},{10,2},{12,4},{14,6},{1,9},{3,11}... | collective-permute-start | bytes 245768 | tf_op jit(solution)/shard_map/ppermute | solution.py:242
  46.8 8.7 %collective-permute-start.23 = (bf16[80,512]{1,0:T(8,128)(2,1)S(1)}, bf16[80,512]{1,0:T(8,128)(2,1)S(1)}, u32[]{:S(2)}, u32[]{:S(2)}) collective-permute-start(bf16[80,512]{1,0:T(8,128)(2,1)S(1)} %get-tuple-element.33), channel_id=1, source_target_pairs={{0,6},{2,4},{4,2},{6,0},{8,14},{10,12},{12,10},{14,8},{1,7},{3,5},... | collective-permute-start | bytes 245768 | tf_op jit(solution)/shard_map/ppermute | solution.py:242
  48.5 10.9 %collective-permute-start.24 = (bf16[80,512]{1,0:T(8,128)(2,1)S(1)}, bf16[80,512]{1,0:T(8,128)(2,1)S(1)}, u32[]{:S(2)}, u32[]{:S(2)}) collective-permute-start(bf16[80,512]{1,0:T(8,128)(2,1)S(1)} %get-tuple-element.34), channel_id=1, source_target_pairs={{0,10},{2,8},{4,14},{6,12},{8,2},{10,0},{12,6},{14,4},{1,11},{3,9}... | collective-permute-start | bytes 245768 | tf_op jit(solution)/shard_map/ppermute | solution.py:242
  50.1 9.3 %collective-permute-start.25 = (bf16[80,512]{1,0:T(8,128)(2,1)S(1)}, bf16[80,512]{1,0:T(8,128)(2,1)S(1)}, u32[]{:S(2)}, u32[]{:S(2)}) collective-permute-start(bf16[80,512]{1,0:T(8,128)(2,1)S(1)} %get-tuple-element.35), channel_id=1, source_target_pairs={{0,2},{2,0},{4,6},{6,4},{8,10},{10,8},{12,14},{14,12},{1,3},{3,1},... | collective-permute-start | bytes 245768 | tf_op jit(solution)/shard_map/ppermute | solution.py:242
  50.5 8.9 %collective-permute-start.26 = (bf16[80,512]{1,0:T(8,128)(2,1)S(1)}, bf16[80,512]{1,0:T(8,128)(2,1)S(1)}, u32[]{:S(2)}, u32[]{:S(2)}) collective-permute-start(bf16[80,512]{1,0:T(8,128)(2,1)S(1)} %get-tuple-element.36), channel_id=1, source_target_pairs={{0,12},{2,14},{4,8},{6,10},{8,4},{10,6},{12,0},{14,2},{1,13},{3,15... | collective-permute-start | bytes 245768 | tf_op jit(solution)/shard_map/ppermute | solution.py:242
  53.2 7.7 %collective-permute-start.27 = (bf16[80,512]{1,0:T(8,128)(2,1)S(1)}, bf16[80,512]{1,0:T(8,128)(2,1)S(1)}, u32[]{:S(2)}, u32[]{:S(2)}) collective-permute-start(bf16[80,512]{1,0:T(8,128)(2,1)S(1)} %get-tuple-element.37), channel_id=1, source_target_pairs={{0,14},{2,12},{4,10},{6,8},{8,6},{10,4},{12,2},{14,0},{1,15},{3,13... | collective-permute-start | bytes 245768 | tf_op jit(solution)/shard_map/ppermute | solution.py:242
  55.4 6.4 %collective-permute-start.28 = (bf16[80,512]{1,0:T(8,128)(2,1)S(1)}, bf16[80,512]{1,0:T(8,128)(2,1)S(1)}, u32[]{:S(2)}, u32[]{:S(2)}) collective-permute-start(bf16[80,512]{1,0:T(8,128)(2,1)S(1)} %get-tuple-element.38), channel_id=1, source_target_pairs={{0,4},{2,6},{4,0},{6,2},{8,12},{10,14},{12,8},{14,10},{1,5},{3,7},... | collective-permute-start | bytes 245768 | tf_op jit(solution)/shard_map/ppermute | solution.py:242
  (14 other events, 129.8 us)
